TPU v7x, 256 devices: a whole 4x4x8 slice. The times are simulated.
256 devices in a mesh: occ: 8 (over y, x_lo), cabs: 16 (over z, core), aux: 2 (over x_hi).
Axes of the slice: x: 4 (x_hi: 2, x_lo: 2; x = x_hi * 2 + x_lo), y: 4, z: 8, core: 2. Of those that a mesh axis runs over, the one named last changes fastest.
Arguments:
- occ_fit: bfloat16 [8, 160, 5120], P('occ', None, 'aux'), may hold values from -6 to 6
- cabs_fit: bfloat16 [8, 4096, 5120], P('occ', 'cabs', 'aux'), may hold values from -0.0034179688 to 0.0034179688
- fock: bfloat16 [4096, 4096], P(None, 'cabs'), may hold values from -1.5 to 1.5, as said below
- cabs_block: int32 [4096], replicated, may hold values from 0 to 1
- pair_block: int32 [8], replicated, may hold values from 0 to 1
Outputs:
- pair_exchange: float32 [8, 8], P('occ')
Inputs may be any that keep to these rules, and one draw needn't show every extreme that they name: fock is symmetric.
All inputs are finite; a program needn't handle non-finite values.
Results may differ from a plain program's by a relative error of at most 0.0028.
Values may be sent and summed in bfloat16 or wider, within the bound.
No kernel may reach another device: no remote copies, remote signals or barrier semaphores. Data moves between devices by JAX's collectives and lax.ppermute only.
A program may use at most 64 MiB of HBM per device.

v0:
```python
import jax
import jax.numpy as jnp
from jax import lax
from jax.sharding import PartitionSpec as P


def from_behind(shard, axis, by):
    devices = lax.axis_size(axis)
    return lax.ppermute(shard, axis, [(i, (i + by) % devices) for i in range(devices)])


def apply_fock(swapped, coupled):
    zeroed = jnp.zeros(swapped.shape[:-1] + (coupled.shape[1],), jnp.float32)
    portion = lax.all_gather(swapped, "cabs", axis=4, tiled=True)
    flattened = portion.reshape(-1, portion.shape[-1])
    product = jnp.dot(flattened, coupled, preferred_element_type=jnp.float32)
    return product.reshape(zeroed.shape)


def fit_reduce(partial_sums):
    totals = lax.psum(partial_sums, "aux")
    return totals.astype(jnp.bfloat16)


def pair_values(direct, applied, my_blocks, partners, labels):
    product = jnp.einsum("sijmb,sjimb->sijb", direct.astype(jnp.float32), applied)
    pair_label = (my_blocks[None, :, None] + partners[:, None, :]) % 2
    keep_column = labels[None, None, None, :] == pair_label[..., None]
    return jnp.sum(jnp.where(keep_column, product, jnp.float32(0.0)), axis=3)


def shards(occ_fit, cabs_fit, fock, cabs_block, pair_block):
    cycle_size = lax.axis_size("occ")
    my_index = lax.axis_index("occ")
    my_rows = occ_fit.shape[0]
    cabs_width = cabs_fit.shape[1]
    labels = lax.dynamic_slice_in_dim(cabs_block, lax.axis_index("cabs") * cabs_width, cabs_width)
    same_block = cabs_block[:, None] == labels[None, :]
    coupled = jnp.where(same_block, fock, jnp.zeros_like(fock))
    my_blocks = lax.dynamic_slice_in_dim(pair_block, my_index * my_rows, my_rows)
    pair_rows = jnp.zeros((my_rows, cycle_size * my_rows), jnp.float32)
    near_occ = occ_fit
    near_cabs = cabs_fit
    for cycle_step in range(cycle_size):
        if cycle_step > 0:
            near_occ, near_cabs = from_behind((near_occ, near_cabs), "occ", 1)
        partner_block = (my_index - cycle_step) % cycle_size
        direct_part = jnp.einsum(
            "imp,jap->ijma", occ_fit, near_cabs, preferred_element_type=jnp.float32
        )
        swapped_part = jnp.einsum(
            "jmp,iap->jima", near_occ, cabs_fit, preferred_element_type=jnp.float32
        )
        summed = fit_reduce(jnp.stack([direct_part, swapped_part]))
        applied = apply_fock(summed[1:2], coupled)
        partners = lax.dynamic_slice_in_dim(pair_block, partner_block * my_rows, my_rows)[None, :]
        values = pair_values(summed[0:1], applied, my_blocks, partners, labels)
        pair_rows = lax.dynamic_update_slice_in_dim(
            pair_rows, values[0], partner_block * my_rows, 1
        )
    result = lax.psum(pair_rows, "cabs")
    return result


def solution(mesh):
    in_specs = (P("occ", None, "aux"), P("occ", "cabs", "aux"), P(None, "cabs"), P(), P())
    out_specs = P("occ", None)
    return jax.shard_map(shards, mesh=mesh, in_specs=in_specs, out_specs=out_specs, check_vma=False)
```

profile of v0, /device:TPU:1, one launch (start us, length us, event | category | flops | bytes accessed | tf_op | source)
XLA Modules:
  0.0 755.9 jit_solution(15792489235986945551)
XLA Ops:
  8.6 29.3 %collective-permute-done = bf16[1,256,2560]{2,1,0:T(8,128)(2,1)S(1)} collective-permute-done((bf16[1,256,2560]{2,1,0:T(8,128)(2,1)}, bf16[1,256,2560]{2,1,0:T(8,128)(2,1)S(1)}, u32[]{:S(2)}, u32[]{:S(2)}) %collective-permute-start) | collective-permute-done | bytes 1310752 | tf_op jit(solution)/shard_map/ppermute | solution.py:9
  38.1 2.5 collective-permute-start.1
  40.6 26.5 %collective-permute-done.2 = bf16[1,256,2560]{2,1,0:T(8,128)(2,1)S(1)} collective-permute-done((bf16[1,256,2560]{2,1,0:T(8,128)(2,1)S(1)}, bf16[1,256,2560]{2,1,0:T(8,128)(2,1)S(1)}, u32[]{:S(2)}, u32[]{:S(2)}) %collective-permute-start.2) | collective-permute-done | bytes 1310752 | tf_op jit(solution)/shard_map/ppermute | solution.py:9
  67.1 17.5 %collective-permute-done.1 = bf16[1,160,2560]{2,1,0:T(8,128)(2,1)S(1)} collective-permute-done((bf16[1,160,2560]{2,1,0:T(8,128)(2,1)}, bf16[1,160,2560]{2,1,0:T(8,128)(2,1)S(1)}, u32[]{:S(2)}, u32[]{:S(2)}) %collective-permute-start.1) | collective-permute-done | bytes 819232 | tf_op jit(solution)/shard_map/ppermute | solution.py:9
  84.8 27.9 %collective-permute-done.4 = bf16[1,256,2560]{2,1,0:T(8,128)(2,1)S(1)} collective-permute-done((bf16[1,256,2560]{2,1,0:T(8,128)(2,1)S(1)}, bf16[1,256,2560]{2,1,0:T(8,128)(2,1)S(1)}, u32[]{:S(2)}, u32[]{:S(2)}) %collective-permute-start.4) | collective-permute-done | bytes 1310752 | tf_op jit(solution)/shard_map/ppermute | solution.py:9
  112.8 17.5 %collective-permute-done.3 = bf16[1,160,2560]{2,1,0:T(8,128)(2,1)S(1)} collective-permute-done((bf16[1,160,2560]{2,1,0:T(8,128)(2,1)S(1)}, bf16[1,160,2560]{2,1,0:T(8,128)(2,1)S(1)}, u32[]{:S(2)}, u32[]{:S(2)}) %collective-permute-start.3) | collective-permute-done | bytes 819232 | tf_op jit(solution)/shard_map/ppermute | solution.py:9
  130.3 45.6 %collective-permute-done.5 = bf16[1,160,2560]{2,1,0:T(8,128)(2,1)S(1)} collective-permute-done((bf16[1,160,2560]{2,1,0:T(8,128)(2,1)S(1)}, bf16[1,160,2560]{2,1,0:T(8,128)(2,1)S(1)}, u32[]{:S(2)}, u32[]{:S(2)}) %collective-permute-start.5) | collective-permute-done | bytes 819232 | tf_op jit(solution)/shard_map/ppermute | solution.py:9
  176.0 3.1 collective-permute-start.8
  181.2 12.5 %collective-permute-done.7 = bf16[1,160,2560]{2,1,0:T(8,128)(2,1)S(1)} collective-permute-done((bf16[1,160,2560]{2,1,0:T(8,128)(2,1)S(1)}, bf16[1,160,2560]{2,1,0:T(8,128)(2,1)S(1)}, u32[]{:S(2)}, u32[]{:S(2)}) %collective-permute-start.7) | collective-permute-done | bytes 819232 | tf_op jit(solution)/shard_map/ppermute | solution.py:9
  195.9 43.4 %collective-permute-done.9 = bf16[1,160,2560]{2,1,0:T(8,128)(2,1)S(1)} collective-permute-done((bf16[1,160,2560]{2,1,0:T(8,128)(2,1)S(1)}, bf16[1,160,2560]{2,1,0:T(8,128)(2,1)S(1)}, u32[]{:S(2)}, u32[]{:S(2)}) %collective-permute-start.9) | collective-permute-done | bytes 819232 | tf_op jit(solution)/shard_map/ppermute | solution.py:9
  239.8 3.1 collective-permute-start.10
  245.2 10.9 %collective-permute-done.11 = bf16[1,160,2560]{2,1,0:T(8,128)(2,1)S(1)} collective-permute-done((bf16[1,160,2560]{2,1,0:T(8,128)(2,1)S(1)}, bf16[1,160,2560]{2,1,0:T(8,128)(2,1)S(1)}, u32[]{:S(2)}, u32[]{:S(2)}) %collective-permute-start.11) | collective-permute-done | bytes 819232 | tf_op jit(solution)/shard_map/ppermute | solution.py:9
  257.6 26.6 %collective-permute-done.10 = bf16[1,256,2560]{2,1,0:T(8,128)(2,1)S(1)} collective-permute-done((bf16[1,256,2560]{2,1,0:T(8,128)(2,1)S(1)}, bf16[1,256,2560]{2,1,0:T(8,128)(2,1)S(1)}, u32[]{:S(2)}, u32[]{:S(2)}) %collective-permute-start.10) | collective-permute-done | bytes 1310752 | tf_op jit(solution)/shard_map/ppermute | solution.py:9
  286.3 15.5 %collective-permute-done.13 = bf16[1,160,2560]{2,1,0:T(8,128)(2,1)S(1)} collective-permute-done((bf16[1,160,2560]{2,1,0:T(8,128)(2,1)S(1)}, bf16[1,160,2560]{2,1,0:T(8,128)(2,1)S(1)}, u32[]{:S(2)}, u32[]{:S(2)}) %collective-permute-start.13) | collective-permute-done | bytes 819232 | tf_op jit(solution)/shard_map/ppermute | solution.py:9
  303.6 26.3 %collective-permute-done.12 = bf16[1,256,2560]{2,1,0:T(8,128)(2,1)S(1)} collective-permute-done((bf16[1,256,2560]{2,1,0:T(8,128)(2,1)S(1)}, bf16[1,256,2560]{2,1,0:T(8,128)(2,1)S(1)}, u32[]{:S(2)}, u32[]{:S(2)}) %collective-permute-start.12) | collective-permute-done | bytes 1310752 | tf_op jit(solution)/shard_map/ppermute | solution.py:9
  330.5 66.0 %all-reduce.2 = (bf16[2,1,1,160,256]{4,3,2,1,0:T(8,128)(2,1)}, bf16[2,1,1,160,256]{4,3,2,1,0:T(8,128)(2,1)}, bf16[2,1,1,160,256]{4,3,2,1,0:T(8,128)(2,1)}, bf16[...) all-reduce(f32[2,1,1,160,256]{4,3,2,1,0:T(8,128)S(1)} %pad_maximum_, ...), channel_id=1, replica_groups=mesh['occ'=8,'cabs'=16,'aux'=2] {'aux'}, use_global_device_ids=true, to_apply=%region_14.15 | all-reduce | flops 655360 | bytes 3932160 | tf_op jit(solution)/shard_map/psum | solution.py:21
  415.6 27.0 %all-gather.23.cloned.1.call-done = bf16[1,1,1,160,4096]{4,3,2,1,0:T(8,128)(2,1)} async-done(((bf16[1,1,1,160,256]{4,3,2,1,0:T(8,128)(2,1)}), bf16[1,1,1,160,4096]{4,3,2,1,0:T(8,128)(2,1)}) %all-gather.23.cloned.1.call-update) | async-done | bytes 1310736 | tf_op jit(solution)/shard_map/all_gather | solution.py:14
  442.6 2.9 fusion.139
  445.5 36.2 %all-gather.21.cloned.1.call-done = bf16[1,1,1,160,4096]{4,3,2,1,0:T(8,128)(2,1)} async-done(((bf16[1,1,1,160,256]{4,3,2,1,0:T(8,128)(2,1)}), bf16[1,1,1,160,4096]{4,3,2,1,0:T(8,128)(2,1)}) %all-gather.21.cloned.1.call-update) | async-done | bytes 1310736 | tf_op jit(solution)/shard_map/all_gather | solution.py:14
  481.8 2.9 fusion.142
  484.7 36.2 %all-gather.19.cloned.1.call-done = bf16[1,1,1,160,4096]{4,3,2,1,0:T(8,128)(2,1)} async-done(((bf16[1,1,1,160,256]{4,3,2,1,0:T(8,128)(2,1)}), bf16[1,1,1,160,4096]{4,3,2,1,0:T(8,128)(2,1)}) %all-gather.19.cloned.1.call-update) | async-done | bytes 1310736 | tf_op jit(solution)/shard_map/all_gather | solution.py:14
  521.0 3.0 fusion.145
  523.9 36.1 %all-gather.17.cloned.1.call-done = bf16[1,1,1,160,4096]{4,3,2,1,0:T(8,128)(2,1)} async-done(((bf16[1,1,1,160,256]{4,3,2,1,0:T(8,128)(2,1)}), bf16[1,1,1,160,4096]{4,3,2,1,0:T(8,128)(2,1)}) %all-gather.17.cloned.1.call-update) | async-done | bytes 1310736 | tf_op jit(solution)/shard_map/all_gather | solution.py:14
  560.0 3.0 fusion.148
  563.0 36.1 %all-gather.15.cloned.1.call-done = bf16[1,1,1,160,4096]{4,3,2,1,0:T(8,128)(2,1)} async-done(((bf16[1,1,1,160,256]{4,3,2,1,0:T(8,128)(2,1)}), bf16[1,1,1,160,4096]{4,3,2,1,0:T(8,128)(2,1)}) %all-gather.15.cloned.1.call-update) | async-done | bytes 1310736 | tf_op jit(solution)/shard_map/all_gather | solution.py:14
  599.0 3.0 fusion.151
  602.0 36.1 %all-gather.13.cloned.1.call-done = bf16[1,1,1,160,4096]{4,3,2,1,0:T(8,128)(2,1)} async-done(((bf16[1,1,1,160,256]{4,3,2,1,0:T(8,128)(2,1)}), bf16[1,1,1,160,4096]{4,3,2,1,0:T(8,128)(2,1)}) %all-gather.13.cloned.1.call-update) | async-done | bytes 1310736 | tf_op jit(solution)/shard_map/all_gather | solution.py:14
  638.1 3.0 fusion.154
  641.1 36.2 %all-gather.11.cloned.1.call-done = bf16[1,1,1,160,4096]{4,3,2,1,0:T(8,128)(2,1)} async-done(((bf16[1,1,1,160,256]{4,3,2,1,0:T(8,128)(2,1)}), bf16[1,1,1,160,4096]{4,3,2,1,0:T(8,128)(2,1)}) %all-gather.11.cloned.1.call-update) | async-done | bytes 1310736 | tf_op jit(solution)/shard_map/all_gather | solution.py:14
  677.3 3.0 fusion.157
  680.3 36.2 %all-gather.9.cloned.1.call-done = bf16[1,1,1,160,4096]{4,3,2,1,0:T(8,128)(2,1)} async-done(((bf16[1,1,1,160,256]{4,3,2,1,0:T(8,128)(2,1)}), bf16[1,1,1,160,4096]{4,3,2,1,0:T(8,128)(2,1)}) %all-gather.9.cloned.1.call-update) | async-done | bytes 1310736 | tf_op jit(solution)/shard_map/all_gather | solution.py:14
  725.4 23.7 %psum.71 = f32[1,8]{1,0:T(1,128)} all-reduce(f32[1,8]{1,0:T(1,128)S(1)} %dynamic_update_slice.31), channel_id=1, replica_groups=mesh['occ'=8,'cabs'=16,'aux'=2] {'cabs'}, use_global_device_ids=true, to_apply=%region_16.17 | all-reduce | flops 8 | bytes 64 | tf_op jit(solution)/shard_map/psum | solution.py:61
  (89 shorter events, 33.7 us)
Async XLA Ops:
  6.5 187.6 %copy-start = (bf16[1,256,2560]{2,1,0:T(8,128)(2,1)S(1)}, bf16[1,256,2560]{2,1,0:T(8,128)(2,1)}, u32[]{:S(2)}) copy-start(bf16[1,256,2560]{2,1,0:T(8,128)(2,1)} %param.6) | copy-start | bytes 3932164
  6.5 436.0 %all-gather.23.cloned.1.call-start = ((), (), s32[]{:S(2)}) async-start(), calls=%async_computation.7 | async-start | bytes 1392640 | tf_op jit(solution)/shard_map/all_gather | solution.py:14
  6.5 31.3 %collective-permute-start = (bf16[1,256,2560]{2,1,0:T(8,128)(2,1)}, bf16[1,256,2560]{2,1,0:T(8,128)(2,1)S(1)}, u32[]{:S(2)}, u32[]{:S(2)}) collective-permute-start(bf16[1,256,2560]{2,1,0:T(8,128)(2,1)} %param.6), channel_id=1, source_target_pairs={{0,32},{32,64},{64,96},{96,128},{128,160},{160,192},{192,224},{224... | collective-permute-start | bytes 3932168 | tf_op jit(solution)/shard_map/ppermute | solution.py:9
  37.9 29.2 %collective-permute-start.2 = (bf16[1,256,2560]{2,1,0:T(8,128)(2,1)S(1)}, bf16[1,256,2560]{2,1,0:T(8,128)(2,1)S(1)}, u32[]{:S(2)}, u32[]{:S(2)}) collective-permute-start(bf16[1,256,2560]{2,1,0:T(8,128)(2,1)S(1)} %collective-permute-done), channel_id=1, source_target_pairs={{0,32},{32,64},{64,96},{96,128},{128,160},{160,192},{192,224},{224... | collective-permute-start | bytes 3932168 | tf_op jit(solution)/shard_map/ppermute | solution.py:9
  38.1 46.5 %collective-permute-start.1 = (bf16[1,160,2560]{2,1,0:T(8,128)(2,1)}, bf16[1,160,2560]{2,1,0:T(8,128)(2,1)S(1)}, u32[]{:S(2)}, u32[]{:S(2)}) collective-permute-start(bf16[1,160,2560]{2,1,0:T(8,128)(2,1)} %param.5), channel_id=1, source_target_pairs={{0,32},{32,64},{64,96},{96,128},{128,160},{160,192},{192,224},{224... | collective-permute-start | bytes 2457608 | tf_op jit(solution)/shard_map/ppermute | solution.py:9
  67.1 45.6 %collective-permute-start.4 = (bf16[1,256,2560]{2,1,0:T(8,128)(2,1)S(1)}, bf16[1,256,2560]{2,1,0:T(8,128)(2,1)S(1)}, u32[]{:S(2)}, u32[]{:S(2)}) collective-permute-start(bf16[1,256,2560]{2,1,0:T(8,128)(2,1)S(1)} %collective-permute-done.2), channel_id=1, source_target_pairs={{0,32},{32,64},{64,96},{96,128},{128,160},{160,192},{192,224},{224... | collective-permute-start | bytes 3932168 | tf_op jit(solution)/shard_map/ppermute | solution.py:9
  84.6 45.6 %collective-permute-start.3 = (bf16[1,160,2560]{2,1,0:T(8,128)(2,1)S(1)}, bf16[1,160,2560]{2,1,0:T(8,128)(2,1)S(1)}, u32[]{:S(2)}, u32[]{:S(2)}) collective-permute-start(bf16[1,160,2560]{2,1,0:T(8,128)(2,1)S(1)} %collective-permute-done.1), channel_id=1, source_target_pairs={{0,32},{32,64},{64,96},{96,128},{128,160},{160,192},{192,224},{224... | collective-permute-start | bytes 2457608 | tf_op jit(solution)/shard_map/ppermute | solution.py:9
  112.7 63.3 %collective-permute-start.6 = (bf16[1,256,2560]{2,1,0:T(8,128)(2,1)S(1)}, bf16[1,256,2560]{2,1,0:T(8,128)(2,1)S(1)}, u32[]{:S(2)}, u32[]{:S(2)}) collective-permute-start(bf16[1,256,2560]{2,1,0:T(8,128)(2,1)S(1)} %collective-permute-done.4), channel_id=1, source_target_pairs={{0,32},{32,64},{64,96},{96,128},{128,160},{160,192},{192,224},{224... | collective-permute-start | bytes 3932168 | tf_op jit(solution)/shard_map/ppermute | solution.py:9
  130.3 45.6 %collective-permute-start.5 = (bf16[1,160,2560]{2,1,0:T(8,128)(2,1)S(1)}, bf16[1,160,2560]{2,1,0:T(8,128)(2,1)S(1)}, u32[]{:S(2)}, u32[]{:S(2)}) collective-permute-start(bf16[1,160,2560]{2,1,0:T(8,128)(2,1)S(1)} %collective-permute-done.3), channel_id=1, source_target_pairs={{0,32},{32,64},{64,96},{96,128},{128,160},{160,192},{192,224},{224... | collective-permute-start | bytes 2457608 | tf_op jit(solution)/shard_map/ppermute | solution.py:9
  175.9 17.7 %collective-permute-start.7 = (bf16[1,160,2560]{2,1,0:T(8,128)(2,1)S(1)}, bf16[1,160,2560]{2,1,0:T(8,128)(2,1)S(1)}, u32[]{:S(2)}, u32[]{:S(2)}) collective-permute-start(bf16[1,160,2560]{2,1,0:T(8,128)(2,1)S(1)} %collective-permute-done.5), channel_id=1, source_target_pairs={{0,32},{32,64},{64,96},{96,128},{128,160},{160,192},{192,224},{224... | collective-permute-start | bytes 2457608 | tf_op jit(solution)/shard_map/ppermute | solution.py:9
  176.0 63.8 %collective-permute-start.8 = (bf16[1,256,2560]{2,1,0:T(8,128)(2,1)S(1)}, bf16[1,256,2560]{2,1,0:T(8,128)(2,1)S(1)}, u32[]{:S(2)}, u32[]{:S(2)}) collective-permute-start(bf16[1,256,2560]{2,1,0:T(8,128)(2,1)S(1)} %collective-permute-done.6), channel_id=1, source_target_pairs={{0,32},{32,64},{64,96},{96,128},{128,160},{160,192},{192,224},{224... | collective-permute-start | bytes 3932168 | tf_op jit(solution)/shard_map/ppermute | solution.py:9
  181.2 13.6 %copy-start.1 = (bf16[1,160,2560]{2,1,0:T(8,128)(2,1)S(1)}, bf16[1,160,2560]{2,1,0:T(8,128)(2,1)}, u32[]{:S(2)}) copy-start(bf16[1,160,2560]{2,1,0:T(8,128)(2,1)} %param.5) | copy-start | bytes 2457604
  193.7 45.6 %collective-permute-start.9 = (bf16[1,160,2560]{2,1,0:T(8,128)(2,1)S(1)}, bf16[1,160,2560]{2,1,0:T(8,128)(2,1)S(1)}, u32[]{:S(2)}, u32[]{:S(2)}) collective-permute-start(bf16[1,160,2560]{2,1,0:T(8,128)(2,1)S(1)} %collective-permute-done.7), channel_id=1, source_target_pairs={{0,32},{32,64},{64,96},{96,128},{128,160},{160,192},{192,224},{224... | collective-permute-start | bytes 2457608 | tf_op jit(solution)/shard_map/ppermute | solution.py:9
  239.3 16.8 %collective-permute-start.11 = (bf16[1,160,2560]{2,1,0:T(8,128)(2,1)S(1)}, bf16[1,160,2560]{2,1,0:T(8,128)(2,1)S(1)}, u32[]{:S(2)}, u32[]{:S(2)}) collective-permute-start(bf16[1,160,2560]{2,1,0:T(8,128)(2,1)S(1)} %collective-permute-done.9), channel_id=1, source_target_pairs={{0,32},{32,64},{64,96},{96,128},{128,160},{160,192},{192,224},{224... | collective-permute-start | bytes 2457608 | tf_op jit(solution)/shard_map/ppermute | solution.py:9
  239.8 44.4 %collective-permute-start.10 = (bf16[1,256,2560]{2,1,0:T(8,128)(2,1)S(1)}, bf16[1,256,2560]{2,1,0:T(8,128)(2,1)S(1)}, u32[]{:S(2)}, u32[]{:S(2)}) collective-permute-start(bf16[1,256,2560]{2,1,0:T(8,128)(2,1)S(1)} %collective-permute-done.8), channel_id=1, source_target_pairs={{0,32},{32,64},{64,96},{96,128},{128,160},{160,192},{192,224},{224... | collective-permute-start | bytes 3932168 | tf_op jit(solution)/shard_map/ppermute | solution.py:9
  256.1 45.6 %collective-permute-start.13 = (bf16[1,160,2560]{2,1,0:T(8,128)(2,1)S(1)}, bf16[1,160,2560]{2,1,0:T(8,128)(2,1)S(1)}, u32[]{:S(2)}, u32[]{:S(2)}) collective-permute-start(bf16[1,160,2560]{2,1,0:T(8,128)(2,1)S(1)} %collective-permute-done.11), channel_id=1, source_target_pairs={{0,32},{32,64},{64,96},{96,128},{128,160},{160,192},{192,224},{224... | collective-permute-start | bytes 2457608 | tf_op jit(solution)/shard_map/ppermute | solution.py:9
  284.2 45.6 %collective-permute-start.12 = (bf16[1,256,2560]{2,1,0:T(8,128)(2,1)S(1)}, bf16[1,256,2560]{2,1,0:T(8,128)(2,1)S(1)}, u32[]{:S(2)}, u32[]{:S(2)}) collective-permute-start(bf16[1,256,2560]{2,1,0:T(8,128)(2,1)S(1)} %collective-permute-done.10), channel_id=1, source_target_pairs={{0,32},{32,64},{64,96},{96,128},{128,160},{160,192},{192,224},{224... | collective-permute-start | bytes 3932168 | tf_op jit(solution)/shard_map/ppermute | solution.py:9
  396.4 8.0 %copy-start.2 = (s32[8]{0:T(128)S(1)}, s32[8]{0:T(128)}, u32[]{:S(2)}) copy-start(s32[8]{0:T(128)} %param.9) | copy-start | bytes 100
  396.5 18.3 %copy-start.6 = (s32[4096]{0:T(1024)S(1)}, s32[4096]{0:T(1024)}, u32[]{:S(2)}) copy-start(s32[4096]{0:T(1024)} %param.8) | copy-start | bytes 49156
  396.5 46.1 %copy-start.5 = (bf16[2,1,1,160,256]{4,3,2,1,0:T(8,128)(2,1)S(1)}, bf16[2,1,1,160,256]{4,3,2,1,0:T(8,128)(2,1)}, u32[]{:S(2)}) copy-start(bf16[2,1,1,160,256]{4,3,2,1,0:T(8,128)(2,1)} %get-tuple-element.13) | copy-start | bytes 491524
  398.1 83.7 %all-gather.21.cloned.1.call-start = ((), (), s32[]{:S(2)}) async-start(), calls=%async_computation.6 | async-start | bytes 1392640 | tf_op jit(solution)/shard_map/all_gather | solution.py:14
  399.7 121.3 %all-gather.19.cloned.1.call-start = ((), (), s32[]{:S(2)}) async-start(), calls=%async_computation.5 | async-start | bytes 1392640 | tf_op jit(solution)/shard_map/all_gather | solution.py:14
  401.3 158.7 %all-gather.17.cloned.1.call-start = ((), (), s32[]{:S(2)}) async-start(), calls=%async_computation.4 | async-start | bytes 1392640 | tf_op jit(solution)/shard_map/all_gather | solution.py:14
  402.0 197.1 %all-gather.15.cloned.1.call-start = ((), (), s32[]{:S(2)}) async-start(), calls=%async_computation.3 | async-start | bytes 1392640 | tf_op jit(solution)/shard_map/all_gather | solution.py:14
  402.7 235.4 %all-gather.13.cloned.1.call-start = ((), (), s32[]{:S(2)}) async-start(), calls=%async_computation.2 | async-start | bytes 1392640 | tf_op jit(solution)/shard_map/all_gather | solution.py:14
  403.4 273.9 %all-gather.11.cloned.1.call-start = ((), (), s32[]{:S(2)}) async-start(), calls=%async_computation.1 | async-start | bytes 1392640 | tf_op jit(solution)/shard_map/all_gather | solution.py:14
  404.2 312.3 %all-gather.9.cloned.1.call-start = ((), (), s32[]{:S(2)}) async-start(), calls=%async_computation | async-start | bytes 1392640 | tf_op jit(solution)/shard_map/all_gather | solution.py:14
  415.6 66.2 %copy-start.4 = (bf16[2,1,1,160,256]{4,3,2,1,0:T(8,128)(2,1)S(1)}, bf16[2,1,1,160,256]{4,3,2,1,0:T(8,128)(2,1)}, u32[]{:S(2)}) copy-start(bf16[2,1,1,160,256]{4,3,2,1,0:T(8,128)(2,1)} %get-tuple-element.14) | copy-start | bytes 491524
  445.5 75.4 %copy-start.3 = (bf16[2,1,1,160,256]{4,3,2,1,0:T(8,128)(2,1)S(1)}, bf16[2,1,1,160,256]{4,3,2,1,0:T(8,128)(2,1)}, u32[]{:S(2)}) copy-start(bf16[2,1,1,160,256]{4,3,2,1,0:T(8,128)(2,1)} %get-tuple-element.15) | copy-start | bytes 491524
  641.1 75.4 %copy-start.7 = (bf16[4096,256]{1,0:T(8,128)(2,1)S(1)}, bf16[4096,256]{1,0:T(8,128)(2,1)}, u32[]{:S(2)}) copy-start(bf16[4096,256]{1,0:T(8,128)(2,1)} %param.7) | copy-start | bytes 6291460
Sparse Core Ops, SparseCore 0:
  398.2 44.2 all-gather.22
  444.3 37.4 all-gather.20
  483.5 37.3 all-gather.18
  522.6 37.3 all-gather.16
  561.6 37.3 all-gather.14
  600.7 37.3 all-gather.12
  639.8 37.4 all-gather.10
  679.0 37.4 all-gather.8
where the time goes:
time: 758 us; the launch traced here: 756 us
  waiting for transfers between devices  580 us (77%)
  blocking collectives  89.6 us (12%)
  matrix products  33 us (4%)
  between operations  23.6 us (3%)
  local copies, waits for them, and re-layouts  14.5 us (2%)
  starting transfers between devices  14.4 us (2%)
    ppermute x14, waiting for transfers between devices, from_behind(): lax.ppermute(shard, axis, [(i, (i + by) % devices) for i in range(devices)])  299 us
    all_gather x8, waiting for transfers between devices, apply_fock(): portion = lax.all_gather(swapped, 'cabs', axis=4, tiled=True)  280 us
    psum x1, blocking collectives, fit_reduce(): totals = lax.psum(partial_sums, 'aux')  66 us
    psum x1, blocking collectives, shards(): result = lax.psum(pair_rows, 'cabs')  23.7 us
    dot_general x8, matrix products, apply_fock(): product = jnp.dot(flattened, coupled, preferred_element_type=jnp.float32)  22.9 us
  transfers between devices with their start and end apart: 22, of which 20 were waited for; matrix products, arithmetic and copies ran while one was open for 5% of the time, Pallas kernels for 0%

commit v1 on v0

v1 whole, which is shorter than its diff:
```python
import jax
import jax.numpy as jnp
from jax import lax
from jax.sharding import PartitionSpec as P

BF = jnp.bfloat16
F32 = jnp.float32
Y = 4
Z = 8


def occ_hop(value, dy, flip):
    pairs = []
    for o in range(2 * Y):
        y, xl = o // 2, o % 2
        pairs.append((o, ((y + dy) % Y) * 2 + (xl ^ flip)))
    return lax.ppermute(value, "occ", pairs)


def z_hop(value, dz):
    return lax.ppermute(value, "cabs", [(c, ((c // 2 + dz) % Z) * 2 + c % 2) for c in range(2 * Z)])


def core_swap(value):
    return lax.ppermute(value, "cabs", [(c, c ^ 1) for c in range(2 * Z)])


def aux_swap(value):
    return lax.ppermute(value, "aux", [(0, 1), (1, 0)])


def rows_dot(left, right):
    return lax.dot_general(left, right, (((1,), (1,)), ((), ())), preferred_element_type=F32)


def plain_dot(left, right):
    return lax.dot_general(left, right, (((1,), (0,)), ((), ())), preferred_element_type=F32)


def shards(occ_fit, cabs_fit, fock, cabs_block, pair_block):
    me = lax.axis_index("occ")
    cabs = lax.axis_index("cabs")
    side = lax.axis_index("aux")
    core = cabs % 2
    z = cabs // 2
    my_y, my_x = me // 2, me % 2
    m_rows, fit = occ_fit.shape[1:]
    width = cabs_fit.shape[1]
    half_fit = fit // 2
    half = m_rows // 2
    quarter = half // 2

    mine = lax.dynamic_slice_in_dim(occ_fit[0], core * half_fit, half_fit, 1)
    own = jnp.where(side == 0, mine, jnp.concatenate([mine[half:], mine[:half]], 0))
    slab = cabs_fit[0]
    slab_own = lax.dynamic_slice_in_dim(slab, core * half_fit, half_fit, 1)
    slab_other = lax.dynamic_slice_in_dim(slab, (1 - core) * half_fit, half_fit, 1)

    by_core = fock.reshape(Z, 2, width, width)
    tile_own = lax.dynamic_index_in_dim(by_core, core, 1, False)
    tile_send = lax.dynamic_index_in_dim(by_core, 1 - core, 1, False)
    tile_other = core_swap(tile_send)

    p0 = occ_hop(own, 0, 1)
    a = occ_hop(own, 1, 0)
    b = occ_hop(own, -1, 0)
    pb = occ_hop(b, 0, 1)
    pa = occ_hop(p0, 1, 0)
    c = occ_hop(b, -1, 0)
    cut1, cut2 = 48, 96
    pc = jnp.concatenate(
        [occ_hop(pa[:cut1], 1, 0), occ_hop(pb[cut1:cut2], -1, 0), occ_hop(c[cut2:], 0, 1)], 0
    )

    labels = lax.dynamic_slice_in_dim(cabs_block, cabs * width, width)

    def partner(dy, flip):
        return ((my_y + dy) % Y) * 2 + (my_x + flip) % 2

    def label_of(dy, flip):
        return (pair_block[me] + pair_block[partner(dy, flip)]) % 2

    def integrals(slices, places):
        keep, send = [], []
        for part in slices:
            other = core_swap(part)
            total = rows_dot(part, slab_own) + rows_dot(other, slab_other)
            keep.append(total[:half])
            send.append(total[half:])
        got = aux_swap(jnp.stack(send))
        whole = (jnp.stack(keep) + got).astype(BF)
        want = jnp.stack([label_of(dy, flip) for dy, flip in places])
        return jnp.where(labels[None, None, :] == want[:, None, None], whole, jnp.zeros_like(whole))

    d_self, d_p0, d_a, d_b = integrals([own, p0, a, b], [(0, 0), (0, 1), (-1, 0), (1, 0)])
    d_pb, d_pa, d_c = integrals([pb, pa, c], [(1, 1), (-1, 1), (2, 0)])
    (d_pc,) = integrals([pc], [(2, 1)])

    def halves(value, second):
        take = lax.dynamic_slice_in_dim(value, jnp.where(second, quarter, 0), quarter, 0)
        give = lax.dynamic_slice_in_dim(value, jnp.where(second, 0, quarter), quarter, 0)
        return take, give

    high_x = my_x == 1
    high_y = my_y >= 2
    take_p0, give_p0 = halves(d_p0, high_x)
    take_c, give_c = halves(d_c, high_y)
    take_pc, give_pc = halves(d_pc, high_y)

    left = jnp.concatenate([d_self, d_a, take_p0, d_pa, take_c, take_pc], 0)
    right = jnp.concatenate(
        [
            d_self,
            occ_hop(d_b, 1, 0),
            occ_hop(give_p0, 0, 1),
            occ_hop(d_pb, 1, 1),
            occ_hop(give_c, 2, 0),
            occ_hop(give_pc, 2, 1),
        ],
        0,
    )
    right_other = core_swap(right)

    rows = left.shape[0]
    cut = (rows // 2 + 15) // 16 * 16
    blocks = [(0, left)]
    up = down = left
    for step in range(1, Z // 2):
        up, down = z_hop(up, 1), z_hop(down, -1)
        blocks += [(-step, up), (step, down)]
    blocks.append((Z // 2, jnp.concatenate([z_hop(up[:cut], 1), z_hop(down[cut:], -1)], 0)))
    applied_own = applied_other = 0.0
    for offset, block in blocks:
        place = (z + offset) % Z
        applied_own += plain_dot(block, lax.dynamic_index_in_dim(tile_own, place, 0, False))
        applied_other += plain_dot(block, lax.dynamic_index_in_dim(tile_other, place, 0, False))
    product = applied_own * right.astype(F32) + applied_other * right_other.astype(F32)
    per_row = jnp.sum(product, axis=1)
    spans = [half, half, quarter, half, quarter, quarter]
    sums, start = [], 0
    for span in spans:
        sums.append(jnp.sum(per_row[start : start + span]))
        start += span
    s_self, s_a, s_p0, s_pa, s_c, s_pc = sums
    g_b = occ_hop(s_a, -1, 0)
    g_pb = occ_hop(s_pa, -1, 1)
    g_p0 = occ_hop(s_p0, 0, 1)
    g_c = occ_hop(s_c, 2, 0)
    g_pc = occ_hop(s_pc, 2, 1)
    places = [(0, 0), (0, 1), (1, 0), (1, 1), (2, 0), (2, 1), (-1, 0), (-1, 1)]
    values = [s_self, s_p0 + g_p0, g_b, g_pb, s_c + g_c, s_pc + g_pc, s_a, s_pa]
    row = jnp.zeros((2 * Y,), F32)
    lane = lax.iota(jnp.int32, 2 * Y)
    for (dy, flip), value in zip(places, values):
        row += jnp.where(lane == partner(dy, flip), value, jnp.float32(0.0))
    peers = 4 * Z
    spread = lax.all_to_all(
        jnp.broadcast_to(row, (peers, 2 * Y)), ("cabs", "aux"), 0, 0, tiled=True
    )
    return jnp.sum(spread, axis=0)[None, :]


def solution(mesh):
    in_specs = (P("occ", None, "aux"), P("occ", "cabs", "aux"), P(None, "cabs"), P(), P())
    out_specs = P("occ", None)
    return jax.shard_map(shards, mesh=mesh, in_specs=in_specs, out_specs=out_specs, check_vma=False)
```

time: 758 us -> 156 us (0.21)
  waiting for transfers between devices: 580 us -> 44.9 us
  blocking collectives: 89.6 us -> 19.2 us
  starting transfers between devices: 14.4 us -> 49.5 us
  matrix products: 33 us -> 15.6 us
  local copies, waits for them, and re-layouts: 14.5 us -> 2.99 us
  between operations: 23.6 us -> 14.5 us
    all_gather x8 -> x0, waiting for transfers between devices: 280 us -> none  [apply_fock(): portion = lax.all_gather(swapped, 'cabs', axis=4, tiled=True)]
    ppermute x14 -> x40, waiting for transfers between devices: 299 us -> 44.9 us  [the longest x19 21.8 us: occ_hop(): return lax.ppermute(value, 'occ', pairs)]
    psum x2 -> x0, blocking collectives: 89.6 us -> none  [the longest x1 66 us: fit_reduce(): totals = lax.psum(partial_sums, 'aux')]
    ppermute x14 -> x40, starting transfers between devices: 14.1 us -> 49.5 us  [the longest x19 17.1 us: occ_hop(): return lax.ppermute(value, 'occ', pairs)]
    all_to_all x0 -> x1, blocking collectives: none -> 19.2 us  [shards(): lax.all_to_all(jnp.broadcast_to(row, (peers, 2 * Y)), ('cabs', 'aux'), 0,...]
    dot_general x23 -> x32, matrix products: 33 us -> 15.6 us  [the longest x16 12.1 us: rows_dot(): lax.dot_general(left, right, (((1,), (1,)), ((), ())), preferred_element_...]
  transfers between devices with their start and end apart: 22 -> 40, of which waited for: 20 -> 11; matrix products, arithmetic and copies ran while one was open for 5% -> 11% of each run, Pallas kernels for 0% -> 0%
where the time goes in v1:
time: 156 us; the launch traced here: 155 us
  starting transfers between devices  49.5 us (32%)
  waiting for transfers between devices  44.9 us (29%)
  blocking collectives  19.2 us (12%)
  matrix products  15.6 us (10%)
  between operations  14.5 us (9%)
  other arithmetic  8.33 us (5%)
  local copies, waits for them, and re-layouts  2.99 us (2%)
    ppermute x19, waiting for transfers between devices, occ_hop(): return lax.ppermute(value, 'occ', pairs)  21.8 us
    all_to_all x1, blocking collectives, shards(): lax.all_to_all(jnp.broadcast_to(row, (peers, 2 * Y)), ('cabs', 'aux'), 0,...  19.2 us
    ppermute x19, starting transfers between devices, occ_hop(): return lax.ppermute(value, 'occ', pairs)  17.1 us
    ppermute x10, starting transfers between devices, core_swap(): return lax.ppermute(value, 'cabs', [(c, c ^ 1) for c in range(2 * Z)])  13.3 us
    ppermute x8, starting transfers between devices, z_hop(): lax.ppermute(value, 'cabs', [(c, (c // 2 + dz) % Z * 2 + c % 2) for c in...  13.2 us
    ppermute x3, waiting for transfers between devices, aux_swap(): return lax.ppermute(value, 'aux', [(0, 1), (1, 0)])  12.4 us
    dot_general x16, matrix products, rows_dot(): lax.dot_general(left, right, (((1,), (1,)), ((), ())), preferred_element_...  12.1 us
    ppermute x8, waiting for transfers between devices, z_hop(): lax.ppermute(value, 'cabs', [(c, (c // 2 + dz) % Z * 2 + c % 2) for c in...  10.6 us
  transfers between devices with their start and end apart: 40, of which 11 were waited for; matrix products, arithmetic and copies ran while one was open for 11% of the time, Pallas kernels for 0%

profile of v1, /device:TPU:1, one launch (start us, length us, event | category | flops | bytes accessed | tf_op | source)
XLA Modules:
  0.0 155.0 jit_solution(13343015804508277956)
XLA Ops:
  1.9 1.9 %maximum_select_fusion.1 = bf16[160,1280]{1,0:T(8,128)(2,1)} fusion(bf16[80,1280]{1,0:T(8,128)(2,1)S(1)} %bitcast.217, bf16[80,1280]{1,0:T(8,128)(2,1)S(1)} %bitcast.216, pred[]{:T(512)S(6)} %eq.155, bf16[1,160,2560]{2,1,0:T(8,128)(2,1)} %param.5, s32[]{:T(128)S(6)} %select_n.352), kind=kLoop, calls=%fused_computation.55 | loop fusion | flops 1024000 | bytes 1228805 | tf_op jit(solution)/shard_map/jit(_where)/select_n | solution.py:54
  3.8 2.0 %collective-permute-start.1 = (bf16[160,1280]{1,0:T(8,128)(2,1)}, bf16[160,1280]{1,0:T(8,128)(2,1)}, u32[]{:S(2)}, u32[]{:S(2)}) collective-permute-start(bf16[160,1280]{1,0:T(8,128)(2,1)} %maximum_select_fusion.1), channel_id=1, source_target_pairs={{0,32},{32,0},{64,96},{96,64},{128,160},{160,128},{192,224},{224,1... | collective-permute-start | bytes 1228808 | tf_op jit(solution)/shard_map/ppermute | solution.py:17
  5.8 2.7 %collective-permute-start.5 = (bf16[160,1280]{1,0:T(8,128)(2,1)}, bf16[160,1280]{1,0:T(8,128)(2,1)}, u32[]{:S(2)}, u32[]{:S(2)}) collective-permute-start(bf16[160,1280]{1,0:T(8,128)(2,1)} %maximum_select_fusion.1), channel_id=1, source_target_pairs={{0,192},{32,224},{64,0},{96,32},{128,64},{160,96},{192,128},{224,1... | collective-permute-start | bytes 1228808 | tf_op jit(solution)/shard_map/ppermute | solution.py:17
  21.7 2.3 %fusion.33 = f32[160,256]{1,0:T(8,128)} fusion(bf16[1,80,1280]{2,1,0:T(8,128)(2,1)} %copy-done.3, bf16[1,80,1280]{2,1,0:T(8,128)(2,1)} %copy-done.2, pred[]{:T(512)S(6)} %eq.155, bf16[1,160,2560]{2,1,0:T(8,128)(2,1)} %param.5, s32[]{:T(128)S(6)} %select_n.352, bf16[1,256,2560]{2,1,0:T(8,128)(2,1)S(1)} %copy-done.1), kind=kOutput, calls=%fused_computation.49 | convolution fusion | flops 105881600 | bytes 1639936 | tf_op jit(solution)/shard_map/dot_general | solution.py:33
  25.2 2.2 %collective-permute-start.12 = (bf16[160,1280]{1,0:T(8,128)(2,1)}, bf16[160,1280]{1,0:T(8,128)(2,1)S(1)}, u32[]{:S(2)}, u32[]{:S(2)}) collective-permute-start(bf16[160,1280]{1,0:T(8,128)(2,1)} %collective-permute-done.5), channel_id=1, source_target_pairs={{0,192},{32,224},{64,0},{96,32},{128,64},{160,96},{192,128},{224,1... | collective-permute-start | bytes 1228808 | tf_op jit(solution)/shard_map/ppermute | solution.py:17
  27.4 1.4 fusion.31
  33.8 5.5 %collective-permute-done.10 = bf16[160,1280]{1,0:T(8,128)(2,1)S(1)} collective-permute-done((bf16[160,1280]{1,0:T(8,128)(2,1)}, bf16[160,1280]{1,0:T(8,128)(2,1)S(1)}, u32[]{:S(2)}, u32[]{:S(2)}) %collective-permute-start.10) | collective-permute-done | bytes 409632 | tf_op jit(solution)/shard_map/ppermute | solution.py:17
  39.3 1.4 collective-permute-start.33
  41.0 2.7 %collective-permute-start.16 = (bf16[48,1280]{1,0:T(8,128)(2,1)S(1)}, bf16[48,1280]{1,0:T(8,128)(2,1)S(1)}, u32[]{:S(2)}, u32[]{:S(2)}) collective-permute-start(bf16[48,1280]{1,0:T(8,128)(2,1)S(1)} %slice.139), channel_id=1, source_target_pairs={{0,192},{32,224},{64,0},{96,32},{128,64},{160,96},{192,128},{224,1... | collective-permute-start | bytes 368648 | tf_op jit(solution)/shard_map/ppermute | solution.py:17
  46.3 2.7 %collective-permute-start.7 = (f32[4,80,256]{2,1,0:T(8,128)S(1)}, f32[4,80,256]{2,1,0:T(8,128)S(1)}, u32[]{:S(2)}, u32[]{:S(2)}) collective-permute-start(f32[4,80,256]{2,1,0:T(8,128)S(1)} %pad_maximum_fusion), channel_id=1, source_target_pairs={{0,1},{1,0},{2,3},{3,2},{4,5},{5,4},{6,7},{7,6},{8,9},{9,8},{10,11... | collective-permute-start | bytes 983048 | tf_op jit(solution)/shard_map/ppermute | solution.py:29
  50.2 1.7 %collective-permute-start.9 = (bf16[160,1280]{1,0:T(8,128)(2,1)S(1)}, bf16[160,1280]{1,0:T(8,128)(2,1)S(1)}, u32[]{:S(2)}, u32[]{:S(2)}) collective-permute-start(bf16[160,1280]{1,0:T(8,128)(2,1)S(1)} %collective-permute-done.8), channel_id=1, source_target_pairs={{0,2},{2,0},{4,6},{6,4},{8,10},{10,8},{12,14},{14,12},{16,18},{18,... | collective-permute-start | bytes 1228808 | tf_op jit(solution)/shard_map/ppermute | solution.py:25
  52.6 5.5 %collective-permute-done.7 = f32[4,80,256]{2,1,0:T(8,128)S(1)} collective-permute-done((f32[4,80,256]{2,1,0:T(8,128)S(1)}, f32[4,80,256]{2,1,0:T(8,128)S(1)}, u32[]{:S(2)}, u32[]{:S(2)}) %collective-permute-start.7) | collective-permute-done | bytes 327712 | tf_op jit(solution)/shard_map/ppermute | solution.py:29
  58.3 4.0 %collective-permute-done.28 = bf16[80,256]{1,0:T(8,128)(2,1)S(1)} collective-permute-done((bf16[80,256]{1,0:T(8,128)(2,1)S(1)}, bf16[80,256]{1,0:T(8,128)(2,1)S(1)}, u32[]{:S(2)}, u32[]{:S(2)}) %collective-permute-start.28) | collective-permute-done | bytes 40992 | tf_op jit(solution)/shard_map/ppermute | solution.py:17
  62.3 2.7 %collective-permute-done.29 = bf16[40,256]{1,0:T(8,128)(2,1)S(1)} collective-permute-done((bf16[40,256]{1,0:T(8,128)(2,1)S(1)}, bf16[40,256]{1,0:T(8,128)(2,1)S(1)}, u32[]{:S(2)}, u32[]{:S(2)}) %collective-permute-start.29) | collective-permute-done | bytes 20512 | tf_op jit(solution)/shard_map/ppermute | solution.py:17
  65.0 4.2 %collective-permute-start.18 = (bf16[160,1280]{1,0:T(8,128)(2,1)S(1)}, bf16[160,1280]{1,0:T(8,128)(2,1)S(1)}, u32[]{:S(2)}, u32[]{:S(2)}) collective-permute-start(bf16[160,1280]{1,0:T(8,128)(2,1)S(1)} %constant_dynamic-update-slice_fusion), channel_id=1, source_target_pairs={{0,2},{2,0},{4,6},{6,4},{8,10},{10,8},{12,14},{14,12},{16,18},{18,... | collective-permute-start | bytes 1228808 | tf_op jit(solution)/shard_map/ppermute | solution.py:25
  72.0 2.5 %collective-permute-start.19 = (f32[1,80,256]{2,1,0:T(8,128)S(1)}, f32[1,80,256]{2,1,0:T(8,128)S(1)}, u32[]{:S(2)}, u32[]{:S(2)}) collective-permute-start(f32[1,80,256]{2,1,0:T(8,128)S(1)} %slice_bitcast_fusion), channel_id=1, source_target_pairs={{0,1},{1,0},{2,3},{3,2},{4,5},{5,4},{6,7},{7,6},{8,9},{9,8},{10,11... | collective-permute-start | bytes 245768 | tf_op jit(solution)/shard_map/ppermute | solution.py:29
  74.4 5.2 %collective-permute-done.14 = f32[3,80,256]{2,1,0:T(8,128)S(1)} collective-permute-done((f32[3,80,256]{2,1,0:T(8,128)S(1)}, f32[3,80,256]{2,1,0:T(8,128)S(1)}, u32[]{:S(2)}, u32[]{:S(2)}) %collective-permute-start.14) | collective-permute-done | bytes 245792 | tf_op jit(solution)/shard_map/ppermute | solution.py:29
  79.7 1.7 %collective-permute-done.19 = f32[1,80,256]{2,1,0:T(8,128)S(1)} collective-permute-done((f32[1,80,256]{2,1,0:T(8,128)S(1)}, f32[1,80,256]{2,1,0:T(8,128)S(1)}, u32[]{:S(2)}, u32[]{:S(2)}) %collective-permute-start.19) | collective-permute-done | bytes 81952 | tf_op jit(solution)/shard_map/ppermute | solution.py:29
  81.5 1.7 %collective-permute-start.20 = (bf16[360,256]{1,0:T(8,128)(2,1)S(1)}, bf16[360,256]{1,0:T(8,128)(2,1)S(1)}, u32[]{:S(2)}, u32[]{:S(2)}) collective-permute-start(bf16[360,256]{1,0:T(8,128)(2,1)S(1)} %constant_dynamic-update-slice_fusion.3), channel_id=1, source_target_pairs={{0,4},{2,6},{4,8},{6,10},{8,12},{10,14},{12,16},{14,18},{16,20},{1... | collective-permute-start | bytes 552968 | tf_op jit(solution)/shard_map/ppermute | solution.py:21
  83.2 4.0 %collective-permute-start.21 = (bf16[360,256]{1,0:T(8,128)(2,1)S(1)}, bf16[360,256]{1,0:T(8,128)(2,1)S(1)}, u32[]{:S(2)}, u32[]{:S(2)}) collective-permute-start(bf16[360,256]{1,0:T(8,128)(2,1)S(1)} %constant_dynamic-update-slice_fusion.3), channel_id=1, source_target_pairs={{0,28},{2,30},{4,0},{6,2},{8,4},{10,6},{12,8},{14,10},{16,12},{18,... | collective-permute-start | bytes 552968 | tf_op jit(solution)/shard_map/ppermute | solution.py:21
  87.8 4.5 %collective-permute-done.30 = bf16[80,256]{1,0:T(8,128)(2,1)S(1)} collective-permute-done((bf16[80,256]{1,0:T(8,128)(2,1)S(1)}, bf16[80,256]{1,0:T(8,128)(2,1)S(1)}, u32[]{:S(2)}, u32[]{:S(2)}) %collective-permute-start.30) | collective-permute-done | bytes 40992 | tf_op jit(solution)/shard_map/ppermute | solution.py:17
  92.3 5.0 %collective-permute-done.32 = bf16[40,256]{1,0:T(8,128)(2,1)S(1)} collective-permute-done((bf16[40,256]{1,0:T(8,128)(2,1)S(1)}, bf16[40,256]{1,0:T(8,128)(2,1)S(1)}, u32[]{:S(2)}, u32[]{:S(2)}) %collective-permute-start.32) | collective-permute-done | bytes 20512 | tf_op jit(solution)/shard_map/ppermute | solution.py:17
  97.3 3.3 %collective-permute-start.34 = (bf16[360,256]{1,0:T(8,128)(2,1)S(1)}, bf16[360,256]{1,0:T(8,128)(2,1)S(1)}, u32[]{:S(2)}, u32[]{:S(2)}) collective-permute-start(bf16[360,256]{1,0:T(8,128)(2,1)S(1)} %constant_dynamic-update-slice_fusion.9), channel_id=1, source_target_pairs={{0,2},{2,0},{4,6},{6,4},{8,10},{10,8},{12,14},{14,12},{16,18},{18,... | collective-permute-start | bytes 552968 | tf_op jit(solution)/shard_map/ppermute | solution.py:25
  100.6 1.7 %collective-permute-start.23 = (bf16[360,256]{1,0:T(8,128)(2,1)S(1)}, bf16[360,256]{1,0:T(8,128)(2,1)S(1)}, u32[]{:S(2)}, u32[]{:S(2)}) collective-permute-start(bf16[360,256]{1,0:T(8,128)(2,1)S(1)} %collective-permute-done.21), channel_id=1, source_target_pairs={{0,28},{2,30},{4,0},{6,2},{8,4},{10,6},{12,8},{14,10},{16,12},{18,... | collective-permute-start | bytes 552968 | tf_op jit(solution)/shard_map/ppermute | solution.py:21
  103.4 3.4 %collective-permute-done.23 = bf16[360,256]{1,0:T(8,128)(2,1)S(1)} collective-permute-done((bf16[360,256]{1,0:T(8,128)(2,1)S(1)}, bf16[360,256]{1,0:T(8,128)(2,1)S(1)}, u32[]{:S(2)}, u32[]{:S(2)}) %collective-permute-start.23) | collective-permute-done | bytes 184352 | tf_op jit(solution)/shard_map/ppermute | solution.py:21
  107.0 2.9 %collective-permute-start.25 = (bf16[360,256]{1,0:T(8,128)(2,1)S(1)}, bf16[360,256]{1,0:T(8,128)(2,1)S(1)}, u32[]{:S(2)}, u32[]{:S(2)}) collective-permute-start(bf16[360,256]{1,0:T(8,128)(2,1)S(1)} %collective-permute-done.23), channel_id=1, source_target_pairs={{0,28},{2,30},{4,0},{6,2},{8,4},{10,6},{12,8},{14,10},{16,12},{18,... | collective-permute-start | bytes 552968 | tf_op jit(solution)/shard_map/ppermute | solution.py:21
  110.7 5.7 %collective-permute-done.24 = bf16[360,256]{1,0:T(8,128)(2,1)S(1)} collective-permute-done((bf16[360,256]{1,0:T(8,128)(2,1)S(1)}, bf16[360,256]{1,0:T(8,128)(2,1)S(1)}, u32[]{:S(2)}, u32[]{:S(2)}) %collective-permute-start.24) | collective-permute-done | bytes 184352 | tf_op jit(solution)/shard_map/ppermute | solution.py:21
  116.6 2.7 %collective-permute-start.27 = (bf16[168,256]{1,0:T(8,128)(2,1)S(1)}, bf16[168,256]{1,0:T(8,128)(2,1)S(1)}, u32[]{:S(2)}, u32[]{:S(2)}) collective-permute-start(bf16[168,256]{1,0:T(8,128)(2,1)S(1)} %slice.144), channel_id=1, source_target_pairs={{0,28},{2,30},{4,0},{6,2},{8,4},{10,6},{12,8},{14,10},{16,12},{18,... | collective-permute-start | bytes 258056 | tf_op jit(solution)/shard_map/ppermute | solution.py:21
  119.8 1.5 collective-permute-done.26
  123.8 4.1 %collective-permute-start.39 = (f32[]{:T(128)}, f32[]{:T(128)}, u32[]{:S(2)}, u32[]{:S(2)}) collective-permute-start(f32[]{:T(128)} %get-tuple-element.9), channel_id=1, source_target_pairs={{0,160},{32,128},{64,224},{96,192},{128,32},{160,0},{192,96},{224,... | collective-permute-start | bytes 20 | tf_op jit(solution)/shard_map/ppermute | solution.py:17
  132.0 3.2 %fusion.145 = f32[8]{0:T(128)S(1)} fusion(f32[]{:T(128)} %get-tuple-element.6, s32[]{:T(128)S(6)} %add.505, f32[]{:T(128)} %get-tuple-element.7, s32[]{:T(128)S(6)} %add.480, f32[]{:T(128)S(6)} %add.574, s32[]{:T(128)S(6)} %add.521, f32[]{:T(128)S(6)} %add.572, s32[]{:T(128)S(6)} %add.512, f32[]{:T(128)} %collective-permute-done.37, s32[]{:T(128)S(6)} %add.500, ...), kind=kLoop, calls=%fused_computation.217 | loop fusion | flops 184 | bytes 96 | tf_op jit(solution)/shard_map/add | solution.py:155
  135.2 19.2 %all_to_all.6 = f32[32,1,8]{2,1,0:T(1,128)S(1)} all-to-all(f32[32,1,8]{2,1,0:T(1,128)S(1)} %broadcast_in_dim.95), channel_id=1, replica_groups=mesh['occ'=8,'cabs'=16,'aux'=2] {'cabs','aux'}, dimensions={0} | all-to-all | bytes 2048 | tf_op jit(solution)/shard_map/all_to_all | solution.py:157
  (147 shorter events, 25.0 us)
Async XLA Ops:
  3.8 23.6 %collective-permute-start.1 = (bf16[160,1280]{1,0:T(8,128)(2,1)}, bf16[160,1280]{1,0:T(8,128)(2,1)}, u32[]{:S(2)}, u32[]{:S(2)}) collective-permute-start(bf16[160,1280]{1,0:T(8,128)(2,1)} %maximum_select_fusion.1), channel_id=1, source_target_pairs={{0,32},{32,0},{64,96},{96,64},{128,160},{160,128},{192,224},{224,1... | collective-permute-start | bytes 1228808 | tf_op jit(solution)/shard_map/ppermute | solution.py:17
  5.8 18.3 %collective-permute-start.5 = (bf16[160,1280]{1,0:T(8,128)(2,1)}, bf16[160,1280]{1,0:T(8,128)(2,1)}, u32[]{:S(2)}, u32[]{:S(2)}) collective-permute-start(bf16[160,1280]{1,0:T(8,128)(2,1)} %maximum_select_fusion.1), channel_id=1, source_target_pairs={{0,192},{32,224},{64,0},{96,32},{128,64},{160,96},{192,128},{224,1... | collective-permute-start | bytes 1228808 | tf_op jit(solution)/shard_map/ppermute | solution.py:17
  8.6 20.3 %collective-permute-start.3 = (bf16[160,1280]{1,0:T(8,128)(2,1)}, bf16[160,1280]{1,0:T(8,128)(2,1)}, u32[]{:S(2)}, u32[]{:S(2)}) collective-permute-start(bf16[160,1280]{1,0:T(8,128)(2,1)} %maximum_select_fusion.1), channel_id=1, source_target_pairs={{0,64},{32,96},{64,128},{96,160},{128,192},{160,224},{192,0},{224,... | collective-permute-start | bytes 1228808 | tf_op jit(solution)/shard_map/ppermute | solution.py:17
  8.6 22.3 %collective-permute-start = (bf16[160,1280]{1,0:T(8,128)(2,1)}, bf16[160,1280]{1,0:T(8,128)(2,1)}, u32[]{:S(2)}, u32[]{:S(2)}) collective-permute-start(bf16[160,1280]{1,0:T(8,128)(2,1)} %maximum_select_fusion.1), channel_id=1, source_target_pairs={{0,2},{2,0},{4,6},{6,4},{8,10},{10,8},{12,14},{14,12},{16,18},{18,... | collective-permute-start | bytes 1228808 | tf_op jit(solution)/shard_map/ppermute | solution.py:25
  24.1 16.6 %collective-permute-start.8 = (bf16[160,1280]{1,0:T(8,128)(2,1)}, bf16[160,1280]{1,0:T(8,128)(2,1)S(1)}, u32[]{:S(2)}, u32[]{:S(2)}) collective-permute-start(bf16[160,1280]{1,0:T(8,128)(2,1)} %collective-permute-done.5), channel_id=1, source_target_pairs={{0,32},{32,0},{64,96},{96,64},{128,160},{160,128},{192,224},{224,1... | collective-permute-start | bytes 1228808 | tf_op jit(solution)/shard_map/ppermute | solution.py:17
  25.2 15.7 %collective-permute-start.12 = (bf16[160,1280]{1,0:T(8,128)(2,1)}, bf16[160,1280]{1,0:T(8,128)(2,1)S(1)}, u32[]{:S(2)}, u32[]{:S(2)}) collective-permute-start(bf16[160,1280]{1,0:T(8,128)(2,1)} %collective-permute-done.5), channel_id=1, source_target_pairs={{0,192},{32,224},{64,0},{96,32},{128,64},{160,96},{192,128},{224,1... | collective-permute-start | bytes 1228808 | tf_op jit(solution)/shard_map/ppermute | solution.py:17
  27.4 11.9 %collective-permute-start.10 = (bf16[160,1280]{1,0:T(8,128)(2,1)}, bf16[160,1280]{1,0:T(8,128)(2,1)S(1)}, u32[]{:S(2)}, u32[]{:S(2)}) collective-permute-start(bf16[160,1280]{1,0:T(8,128)(2,1)} %collective-permute-done.1), channel_id=1, source_target_pairs={{0,64},{32,96},{64,128},{96,160},{128,192},{160,224},{192,0},{224,... | collective-permute-start | bytes 1228808 | tf_op jit(solution)/shard_map/ppermute | solution.py:17
  28.8 12.1 %collective-permute-start.2 = (bf16[160,1280]{1,0:T(8,128)(2,1)}, bf16[160,1280]{1,0:T(8,128)(2,1)S(1)}, u32[]{:S(2)}, u32[]{:S(2)}) collective-permute-start(bf16[160,1280]{1,0:T(8,128)(2,1)} %collective-permute-done.1), channel_id=1, source_target_pairs={{0,2},{2,0},{4,6},{6,4},{8,10},{10,8},{12,14},{14,12},{16,18},{18,... | collective-permute-start | bytes 1228808 | tf_op jit(solution)/shard_map/ppermute | solution.py:25
  30.9 13.2 %collective-permute-start.4 = (bf16[160,1280]{1,0:T(8,128)(2,1)}, bf16[160,1280]{1,0:T(8,128)(2,1)S(1)}, u32[]{:S(2)}, u32[]{:S(2)}) collective-permute-start(bf16[160,1280]{1,0:T(8,128)(2,1)} %collective-permute-done.3), channel_id=1, source_target_pairs={{0,2},{2,0},{4,6},{6,4},{8,10},{10,8},{12,14},{14,12},{16,18},{18,... | collective-permute-start | bytes 1228808 | tf_op jit(solution)/shard_map/ppermute | solution.py:25
  39.3 63.0 %collective-permute-start.33 = (bf16[8,256,256]{2,1,0:T(8,128)(2,1)S(1)}, bf16[8,256,256]{2,1,0:T(8,128)(2,1)S(1)}, u32[]{:S(2)}, u32[]{:S(2)}) collective-permute-start(bf16[8,256,256]{2,1,0:T(8,128)(2,1)S(1)} %dynamic-slice_bitcast_fusion), channel_id=1, source_target_pairs={{0,2},{2,0},{4,6},{6,4},{8,10},{10,8},{12,14},{14,12},{16,18},{18,... | collective-permute-start | bytes 3145736 | tf_op jit(solution)/shard_map/ppermute | solution.py:25
  40.7 5.1 %collective-permute-start.6 = (bf16[160,1280]{1,0:T(8,128)(2,1)}, bf16[160,1280]{1,0:T(8,128)(2,1)S(1)}, u32[]{:S(2)}, u32[]{:S(2)}) collective-permute-start(bf16[160,1280]{1,0:T(8,128)(2,1)} %collective-permute-done.5), channel_id=1, source_target_pairs={{0,2},{2,0},{4,6},{6,4},{8,10},{10,8},{12,14},{14,12},{16,18},{18,... | collective-permute-start | bytes 1228808 | tf_op jit(solution)/shard_map/ppermute | solution.py:25
  40.9 9.3 %collective-permute-start.15 = (bf16[48,1280]{1,0:T(8,128)(2,1)S(1)}, bf16[48,1280]{1,0:T(8,128)(2,1)S(1)}, u32[]{:S(2)}, u32[]{:S(2)}) collective-permute-start(bf16[48,1280]{1,0:T(8,128)(2,1)S(1)} %slice.138), channel_id=1, source_target_pairs={{0,64},{32,96},{64,128},{96,160},{128,192},{160,224},{192,0},{224,... | collective-permute-start | bytes 368648 | tf_op jit(solution)/shard_map/ppermute | solution.py:17
  41.0 10.9 %collective-permute-start.16 = (bf16[48,1280]{1,0:T(8,128)(2,1)S(1)}, bf16[48,1280]{1,0:T(8,128)(2,1)S(1)}, u32[]{:S(2)}, u32[]{:S(2)}) collective-permute-start(bf16[48,1280]{1,0:T(8,128)(2,1)S(1)} %slice.139), channel_id=1, source_target_pairs={{0,192},{32,224},{64,0},{96,32},{128,64},{160,96},{192,128},{224,1... | collective-permute-start | bytes 368648 | tf_op jit(solution)/shard_map/ppermute | solution.py:17
  44.1 7.9 %collective-permute-start.17 = (bf16[64,1280]{1,0:T(8,128)(2,1)S(1)}, bf16[64,1280]{1,0:T(8,128)(2,1)S(1)}, u32[]{:S(2)}, u32[]{:S(2)}) collective-permute-start(bf16[64,1280]{1,0:T(8,128)(2,1)S(1)} %slice.140), channel_id=1, source_target_pairs={{0,32},{32,0},{64,96},{96,64},{128,160},{160,128},{192,224},{224,1... | collective-permute-start | bytes 491528 | tf_op jit(solution)/shard_map/ppermute | solution.py:17
  46.3 11.8 %collective-permute-start.7 = (f32[4,80,256]{2,1,0:T(8,128)S(1)}, f32[4,80,256]{2,1,0:T(8,128)S(1)}, u32[]{:S(2)}, u32[]{:S(2)}) collective-permute-start(f32[4,80,256]{2,1,0:T(8,128)S(1)} %pad_maximum_fusion), channel_id=1, source_target_pairs={{0,1},{1,0},{2,3},{3,2},{4,5},{5,4},{6,7},{7,6},{8,9},{9,8},{10,11... | collective-permute-start | bytes 983048 | tf_op jit(solution)/shard_map/ppermute | solution.py:29
  50.2 19.1 %collective-permute-start.9 = (bf16[160,1280]{1,0:T(8,128)(2,1)S(1)}, bf16[160,1280]{1,0:T(8,128)(2,1)S(1)}, u32[]{:S(2)}, u32[]{:S(2)}) collective-permute-start(bf16[160,1280]{1,0:T(8,128)(2,1)S(1)} %collective-permute-done.8), channel_id=1, source_target_pairs={{0,2},{2,0},{4,6},{6,4},{8,10},{10,8},{12,14},{14,12},{16,18},{18,... | collective-permute-start | bytes 1228808 | tf_op jit(solution)/shard_map/ppermute | solution.py:25
  51.9 17.8 %collective-permute-start.11 = (bf16[160,1280]{1,0:T(8,128)(2,1)S(1)}, bf16[160,1280]{1,0:T(8,128)(2,1)S(1)}, u32[]{:S(2)}, u32[]{:S(2)}) collective-permute-start(bf16[160,1280]{1,0:T(8,128)(2,1)S(1)} %collective-permute-done.10), channel_id=1, source_target_pairs={{0,2},{2,0},{4,6},{6,4},{8,10},{10,8},{12,14},{14,12},{16,18},{18,... | collective-permute-start | bytes 1228808 | tf_op jit(solution)/shard_map/ppermute | solution.py:25
  52.0 18.0 %collective-permute-start.13 = (bf16[160,1280]{1,0:T(8,128)(2,1)S(1)}, bf16[160,1280]{1,0:T(8,128)(2,1)S(1)}, u32[]{:S(2)}, u32[]{:S(2)}) collective-permute-start(bf16[160,1280]{1,0:T(8,128)(2,1)S(1)} %collective-permute-done.12), channel_id=1, source_target_pairs={{0,2},{2,0},{4,6},{6,4},{8,10},{10,8},{12,14},{14,12},{16,18},{18,... | collective-permute-start | bytes 1228808 | tf_op jit(solution)/shard_map/ppermute | solution.py:25
  65.0 6.1 %collective-permute-start.18 = (bf16[160,1280]{1,0:T(8,128)(2,1)S(1)}, bf16[160,1280]{1,0:T(8,128)(2,1)S(1)}, u32[]{:S(2)}, u32[]{:S(2)}) collective-permute-start(bf16[160,1280]{1,0:T(8,128)(2,1)S(1)} %constant_dynamic-update-slice_fusion), channel_id=1, source_target_pairs={{0,2},{2,0},{4,6},{6,4},{8,10},{10,8},{12,14},{14,12},{16,18},{18,... | collective-permute-start | bytes 1228808 | tf_op jit(solution)/shard_map/ppermute | solution.py:25
  70.5 9.2 %collective-permute-start.14 = (f32[3,80,256]{2,1,0:T(8,128)S(1)}, f32[3,80,256]{2,1,0:T(8,128)S(1)}, u32[]{:S(2)}, u32[]{:S(2)}) collective-permute-start(f32[3,80,256]{2,1,0:T(8,128)S(1)} %pad_maximum_fusion.1), channel_id=1, source_target_pairs={{0,1},{1,0},{2,3},{3,2},{4,5},{5,4},{6,7},{7,6},{8,9},{9,8},{10,11... | collective-permute-start | bytes 737288 | tf_op jit(solution)/shard_map/ppermute | solution.py:29
  72.0 9.5 %collective-permute-start.19 = (f32[1,80,256]{2,1,0:T(8,128)S(1)}, f32[1,80,256]{2,1,0:T(8,128)S(1)}, u32[]{:S(2)}, u32[]{:S(2)}) collective-permute-start(f32[1,80,256]{2,1,0:T(8,128)S(1)} %slice_bitcast_fusion), channel_id=1, source_target_pairs={{0,1},{1,0},{2,3},{3,2},{4,5},{5,4},{6,7},{7,6},{8,9},{9,8},{10,11... | collective-permute-start | bytes 245768 | tf_op jit(solution)/shard_map/ppermute | solution.py:29
  81.5 20.8 %collective-permute-start.20 = (bf16[360,256]{1,0:T(8,128)(2,1)S(1)}, bf16[360,256]{1,0:T(8,128)(2,1)S(1)}, u32[]{:S(2)}, u32[]{:S(2)}) collective-permute-start(bf16[360,256]{1,0:T(8,128)(2,1)S(1)} %constant_dynamic-update-slice_fusion.3), channel_id=1, source_target_pairs={{0,4},{2,6},{4,8},{6,10},{8,12},{10,14},{12,16},{14,18},{16,20},{1... | collective-permute-start | bytes 552968 | tf_op jit(solution)/shard_map/ppermute | solution.py:21
  83.2 17.4 %collective-permute-start.21 = (bf16[360,256]{1,0:T(8,128)(2,1)S(1)}, bf16[360,256]{1,0:T(8,128)(2,1)S(1)}, u32[]{:S(2)}, u32[]{:S(2)}) collective-permute-start(bf16[360,256]{1,0:T(8,128)(2,1)S(1)} %constant_dynamic-update-slice_fusion.3), channel_id=1, source_target_pairs={{0,28},{2,30},{4,0},{6,2},{8,4},{10,6},{12,8},{14,10},{16,12},{18,... | collective-permute-start | bytes 552968 | tf_op jit(solution)/shard_map/ppermute | solution.py:21
  87.2 5.1 %collective-permute-start.30 = (bf16[80,256]{1,0:T(8,128)(2,1)S(1)}, bf16[80,256]{1,0:T(8,128)(2,1)S(1)}, u32[]{:S(2)}, u32[]{:S(2)}) collective-permute-start(bf16[80,256]{1,0:T(8,128)(2,1)S(1)} %get-tuple-element.31), channel_id=1, source_target_pairs={{0,96},{32,64},{64,160},{96,128},{128,224},{160,192},{192,32},{224... | collective-permute-start | bytes 122888 | tf_op jit(solution)/shard_map/ppermute | solution.py:17
  92.3 5.0 %collective-permute-start.32 = (bf16[40,256]{1,0:T(8,128)(2,1)S(1)}, bf16[40,256]{1,0:T(8,128)(2,1)S(1)}, u32[]{:S(2)}, u32[]{:S(2)}) collective-permute-start(bf16[40,256]{1,0:T(8,128)(2,1)S(1)} %dynamic-slice_bitcast_fusion.1), channel_id=1, source_target_pairs={{0,160},{32,128},{64,224},{96,192},{128,32},{160,0},{192,96},{224,... | collective-permute-start | bytes 61448 | tf_op jit(solution)/shard_map/ppermute | solution.py:17
  97.3 24.4 %collective-permute-start.34 = (bf16[360,256]{1,0:T(8,128)(2,1)S(1)}, bf16[360,256]{1,0:T(8,128)(2,1)S(1)}, u32[]{:S(2)}, u32[]{:S(2)}) collective-permute-start(bf16[360,256]{1,0:T(8,128)(2,1)S(1)} %constant_dynamic-update-slice_fusion.9), channel_id=1, source_target_pairs={{0,2},{2,0},{4,6},{6,4},{8,10},{10,8},{12,14},{14,12},{16,18},{18,... | collective-permute-start | bytes 552968 | tf_op jit(solution)/shard_map/ppermute | solution.py:25
  100.6 6.2 %collective-permute-start.23 = (bf16[360,256]{1,0:T(8,128)(2,1)S(1)}, bf16[360,256]{1,0:T(8,128)(2,1)S(1)}, u32[]{:S(2)}, u32[]{:S(2)}) collective-permute-start(bf16[360,256]{1,0:T(8,128)(2,1)S(1)} %collective-permute-done.21), channel_id=1, source_target_pairs={{0,28},{2,30},{4,0},{6,2},{8,4},{10,6},{12,8},{14,10},{16,12},{18,... | collective-permute-start | bytes 552968 | tf_op jit(solution)/shard_map/ppermute | solution.py:21
  102.3 7.9 %collective-permute-start.22 = (bf16[360,256]{1,0:T(8,128)(2,1)S(1)}, bf16[360,256]{1,0:T(8,128)(2,1)S(1)}, u32[]{:S(2)}, u32[]{:S(2)}) collective-permute-start(bf16[360,256]{1,0:T(8,128)(2,1)S(1)} %collective-permute-done.20), channel_id=1, source_target_pairs={{0,4},{2,6},{4,8},{6,10},{8,12},{10,14},{12,16},{14,18},{16,20},{1... | collective-permute-start | bytes 552968 | tf_op jit(solution)/shard_map/ppermute | solution.py:21
  107.0 9.6 %collective-permute-start.25 = (bf16[360,256]{1,0:T(8,128)(2,1)S(1)}, bf16[360,256]{1,0:T(8,128)(2,1)S(1)}, u32[]{:S(2)}, u32[]{:S(2)}) collective-permute-start(bf16[360,256]{1,0:T(8,128)(2,1)S(1)} %collective-permute-done.23), channel_id=1, source_target_pairs={{0,28},{2,30},{4,0},{6,2},{8,4},{10,6},{12,8},{14,10},{16,12},{18,... | collective-permute-start | bytes 552968 | tf_op jit(solution)/shard_map/ppermute | solution.py:21
  110.2 6.3 %collective-permute-start.24 = (bf16[360,256]{1,0:T(8,128)(2,1)S(1)}, bf16[360,256]{1,0:T(8,128)(2,1)S(1)}, u32[]{:S(2)}, u32[]{:S(2)}) collective-permute-start(bf16[360,256]{1,0:T(8,128)(2,1)S(1)} %collective-permute-done.22), channel_id=1, source_target_pairs={{0,4},{2,6},{4,8},{6,10},{8,12},{10,14},{12,16},{14,18},{16,20},{1... | collective-permute-start | bytes 552968 | tf_op jit(solution)/shard_map/ppermute | solution.py:21
  123.8 5.7 %collective-permute-start.38 = (f32[]{:T(128)}, f32[]{:T(128)}, u32[]{:S(2)}, u32[]{:S(2)}) collective-permute-start(f32[]{:T(128)} %get-tuple-element.10), channel_id=1, source_target_pairs={{0,128},{32,160},{64,192},{96,224},{128,0},{160,32},{192,64},{224,... | collective-permute-start | bytes 20 | tf_op jit(solution)/shard_map/ppermute | solution.py:17
  123.8 7.0 %collective-permute-start.39 = (f32[]{:T(128)}, f32[]{:T(128)}, u32[]{:S(2)}, u32[]{:S(2)}) collective-permute-start(f32[]{:T(128)} %get-tuple-element.9), channel_id=1, source_target_pairs={{0,160},{32,128},{64,224},{96,192},{128,32},{160,0},{192,96},{224,... | collective-permute-start | bytes 20 | tf_op jit(solution)/shard_map/ppermute | solution.py:17
  (14 other events, 99.3 us)

commit v2 on v0

v2 whole, which is shorter than its diff:
```python
import jax
import jax.numpy as jnp
from jax import lax
from jax.experimental import pallas as pl
from jax.experimental.pallas import tpu as pltpu
from jax.sharding import PartitionSpec as P

BF = jnp.bfloat16
F32 = jnp.float32
Y = 4
Z = 8
OCC = 2 * Y
KEPT = 40
HEAD = 48
VMEM = pl.BlockSpec(memory_space=pltpu.VMEM)
SMEM = pl.BlockSpec(memory_space=pltpu.SMEM)
ANY = pl.BlockSpec(memory_space=pl.ANY)
PARAMS = pltpu.CompilerParams(vmem_limit_bytes=12 * 2**20)

PLACES = ((0, 0), (0, 1), (-1, 0), (1, 0), (1, 1), (-1, 1), (2, 0), (2, 1))


def partner(me, dy, flip):
    return (((me >> 1) + dy) & (Y - 1)) * 2 + ((me & 1) ^ flip)


def occ_hop(value, dy, flip):
    return lax.ppermute(value, "occ", [(o, partner(o, dy, flip)) for o in range(OCC)])


def px_hop(value, flips):
    pairs = []
    for o in range(OCC):
        takes_c = (o & 1) ^ (o >> 2)
        pairs.append((o, partner(o, 0, 1) if takes_c == flips else partner(o, 2, 0)))
    return lax.ppermute(value, "occ", pairs)


def z_hop(value, dz):
    return lax.ppermute(value, "cabs", [(c, ((c // 2 + dz) % Z) * 2 + c % 2) for c in range(2 * Z)])


def core_swap(value):
    return lax.ppermute(value, "cabs", [(c, c ^ 1) for c in range(2 * Z)])


def aux_swap(value):
    return lax.ppermute(value, "aux", [(0, 1), (1, 0)])


def rows_dot(left, right):
    return lax.dot_general(left, right, (((1,), (1,)), ((), ())), preferred_element_type=F32)


def plain_dot(left, right):
    return lax.dot_general(left, right, (((1,), (0,)), ((), ())), preferred_element_type=F32)


def transposed(slab, slab_other):
    width, fit = slab.shape

    def body(own_ref, other_ref, out_ref):
        out_ref[:, :width] = own_ref[...].T
        out_ref[:, width:] = other_ref[...].T

    return pl.pallas_call(
        body,
        out_shape=jax.ShapeDtypeStruct((fit, 2 * width), BF),
        in_specs=[VMEM, VMEM],
        out_specs=VMEM,
        compiler_params=PARAMS,
        cost_estimate=pl.CostEstimate(
            flops=0, bytes_accessed=8 * fit * width, transcendentals=0
        ),
    )(slab, slab_other)


def fit_sums(place, slices, columns, kept_before=None):
    count = len(slices)
    rows, fit = slices[0].shape
    width = columns.shape[1]
    extra = [] if kept_before is None else [kept_before]
    shapes = [jax.ShapeDtypeStruct((count, KEPT, width), F32)]
    if not extra:
        shapes.append(jax.ShapeDtypeStruct((count, KEPT, width), F32))

    def body(place_ref, *refs):
        parts, columns_ref = refs[:count], refs[count]
        stack_ref, total_ref, sems = refs[-3:]
        outs = refs[count + 1 + len(extra) : -3]
        copies = [
            pltpu.make_async_copy(
                parts[index], stack_ref.at[pl.ds(index * rows, rows), :], sems.at[index]
            )
            for index in range(count)
        ]
        for copy in copies:
            copy.start()
        for copy in copies:
            copy.wait()
        total_ref[...] = plain_dot(stack_ref[...], columns_ref[...])
        side = place_ref[3]
        for index in range(count):
            start = index * rows

            def taken(first, length):
                return total_ref[pl.ds(pl.multiple_of(start + first, 8), length), :]

            if rows == 2 * KEPT:
                outs[0][index] = taken(side * KEPT, KEPT)
                outs[1][index] = taken((1 - side) * KEPT, KEPT)
            elif not extra:
                over = rows - KEPT
                outs[0][index, :over, :] = taken(side * KEPT, over)
                outs[1][index] = taken((1 - side) * over, KEPT)
            else:
                over = KEPT - rows
                few = refs[count + 1][index, :over, :]
                outs[0][index, pl.ds(pl.multiple_of(side * over, 8), rows), :] = taken(0, rows)
                outs[0][index, pl.ds(pl.multiple_of((1 - side) * rows, 8), over), :] = few

    return pl.pallas_call(
        body,
        out_shape=tuple(shapes),
        in_specs=[SMEM] + [ANY] * count + [VMEM] * (1 + len(extra)),
        out_specs=(VMEM,) * len(shapes),
        scratch_shapes=[
            pltpu.VMEM((count * rows, fit), BF),
            pltpu.VMEM((count * rows, width), F32),
            pltpu.SemaphoreType.DMA((count,)),
        ],
        compiler_params=PARAMS,
        cost_estimate=pl.CostEstimate(
            flops=2 * count * rows * fit * width,
            bytes_accessed=2 * width * fit + 2 * count * rows * fit + 8 * count * rows * width,
            transcendentals=0,
        ),
    )(place, *slices, columns, *extra)


def apply_tile(place_ref, offset, block, own_ref, other_ref):
    width = own_ref.shape[1]
    own = other = None
    for index in range(2):
        row = (((place_ref[1] + offset) & (Z - 1)) * 2 + (place_ref[2] ^ index)) * width
        rows = pl.ds(pl.multiple_of(row, width), width)
        part = block[:, index * width : (index + 1) * width]
        to_own = plain_dot(part, own_ref[rows, :])
        to_other = plain_dot(part, other_ref[rows, :])
        own = to_own if own is None else own + to_own
        other = to_other if other is None else other + to_other
    return own, other


def apply_near(place, offsets, blocks, fock, fock_other):
    count = len(blocks)
    rows, columns = blocks[0].shape
    width = columns // 2

    def body(place_ref, *refs):
        own_ref, other_ref, out_ref = refs[count:]
        for index in range(count):
            own, other = apply_tile(
                place_ref, offsets[index], refs[index][...], own_ref, other_ref
            )
            if index == 0:
                out_ref[:, :width] = own
                out_ref[:, width:] = other
            else:
                out_ref[:, :width] += own
                out_ref[:, width:] += other

    return pl.pallas_call(
        body,
        out_shape=jax.ShapeDtypeStruct((rows, columns), F32),
        in_specs=[SMEM] + [VMEM] * (count + 2),
        out_specs=VMEM,
        compiler_params=PARAMS,
        cost_estimate=pl.CostEstimate(
            flops=2 * count * rows * columns * columns,
            bytes_accessed=2 * count * columns * (rows + columns),
            transcendentals=0,
        ),
    )(place, *blocks, fock, fock_other)


def apply_last(place, applied, upper, lower, fock, fock_other, rights):
    cut = upper.shape[0]
    rows, columns = applied.shape
    width = columns // 2
    count = len(rights)
    span = rows // count

    def body(place_ref, applied_ref, upper_ref, lower_ref, own_ref, other_ref, *refs):
        right_refs, (row_ref, a_ref, pa_ref, px_ref, sum_ref) = refs[:count], refs[count:]
        for part, first, last in ((upper_ref, 0, cut), (lower_ref, cut, rows)):
            own, other = apply_tile(place_ref, Z // 2, part[...], own_ref, other_ref)
            sum_ref[first:last, :width] = applied_ref[first:last, :width] + own
            sum_ref[first:last, width:] = applied_ref[first:last, width:] + other
        sums = []
        for index in range(count):
            product = sum_ref[index * span : (index + 1) * span, :] * right_refs[index][...].astype(F32)
            sums.append(jnp.sum(jnp.sum(product, axis=0, keepdims=True), axis=1, keepdims=True))
        me = place_ref[0]
        takes_c = (me & 1) ^ (me >> 2)
        lanes = lax.broadcasted_iota(jnp.int32, (1, OCC), 1)
        px = jnp.where(takes_c == 1, partner(me, 2, 0), partner(me, 0, 1))
        others = (me, partner(me, -1, 0), partner(me, -1, 1), px, partner(me, 2, 1))
        row = jnp.zeros((1, OCC), F32)
        for value, place_of in zip(sums, others):
            row += jnp.where(lanes == place_of, value, 0.0)
        row_ref[...] = row
        here = lanes == me
        a_ref[...] = jnp.where(here, sums[1], 0.0)
        pa_ref[...] = jnp.where(here, sums[2], 0.0)
        px_ref[...] = jnp.where(here, sums[3], 0.0)

    shape = jax.ShapeDtypeStruct((1, OCC), F32)
    return pl.pallas_call(
        body,
        out_shape=(shape,) * 4,
        in_specs=[SMEM] + [VMEM] * (count + 5),
        out_specs=(VMEM,) * 4,
        scratch_shapes=[pltpu.VMEM((rows, columns), F32)],
        compiler_params=PARAMS,
        cost_estimate=pl.CostEstimate(
            flops=2 * rows * columns * columns,
            bytes_accessed=2 * columns * (rows + columns) + 6 * rows * columns,
            transcendentals=0,
        ),
    )(place, applied, upper, lower, fock, fock_other, *rights)


def shards(occ_fit, cabs_fit, fock, cabs_block, pair_block):
    me = lax.axis_index("occ")
    cabs = lax.axis_index("cabs")
    side = lax.axis_index("aux")
    core = cabs & 1
    z = cabs >> 1
    place = jnp.stack([me, z, core, side]).astype(jnp.int32)
    m_rows = occ_fit.shape[1]
    width = cabs_fit.shape[1]
    half = m_rows // 2

    own = lax.dynamic_slice_in_dim(occ_fit[0], core * half, half, 0)
    slab_other = core_swap(cabs_fit[0])
    fock_other = core_swap(fock)

    dy = jnp.array([p[0] for p in PLACES], jnp.int32)
    flip = jnp.array([p[1] for p in PLACES], jnp.int32)
    onehot = partner(me, dy, flip)[:, None] == lax.iota(jnp.int32, OCC)[None, :]
    theirs = jnp.sum(jnp.where(onehot, pair_block[None, :], 0), axis=1)
    mine = jnp.sum(jnp.where(lax.iota(jnp.int32, OCC) == me, pair_block, 0))
    wanted = (theirs + mine) & 1
    by_core = cabs_block.reshape(Z, 2, width)
    chip_labels = jnp.sum(
        jnp.where(lax.iota(jnp.int32, Z)[:, None, None] == z, by_core, 0), axis=0
    )
    labels = jnp.where(core == 0, chip_labels, chip_labels[::-1]).reshape(2 * width)
    keep_column = labels[None] == wanted[:, None]

    p0 = occ_hop(own, 0, 1)
    b = occ_hop(own, -1, 0)
    a = occ_hop(own, 1, 0)
    columns = transposed(cabs_fit[0], slab_other)
    p0, a, b, columns, fock_other, keep_column, place = lax.optimization_barrier(
        (p0, a, b, columns, fock_other, keep_column, place)
    )

    def head(value):
        return lax.dynamic_slice_in_dim(value, (1 - side) * (half - HEAD), HEAD, 0)

    def tail(value):
        return lax.dynamic_slice_in_dim(value, side * HEAD, half - HEAD, 0)

    def onward(from_b, from_p0):
        return [
            occ_hop(from_b, 0, 1),
            occ_hop(from_p0, 1, 0),
            occ_hop(from_b, -1, 0),
            occ_hop(from_p0, 2, 0),
        ]

    heads = onward(head(b), head(p0))
    tails = onward(tail(b), tail(p0))

    def masked(keep, got, first):
        whole = (keep + got).astype(BF)
        mask = keep_column[first : first + keep.shape[0]]
        return jnp.where(mask[:, None], whole, jnp.zeros_like(whole))

    keep, send = fit_sums(place, [own, p0, a, b], columns)
    keep, *heads = lax.optimization_barrier((keep, *heads))
    got = aux_swap(send)
    got, *tails = lax.optimization_barrier((got, *tails))
    d_self, d_p0, d_a, d_b = masked(keep, got, 0)
    right_a = occ_hop(d_b, 1, 0)
    keep, send = fit_sums(place, heads, columns)
    got = aux_swap(send)
    (keep,) = fit_sums(place, tails, columns, keep)
    got, right_a = lax.optimization_barrier((got, right_a))
    d_pb, d_pa, d_c, d_pc = masked(keep, got, 4)
    takes_c = ((me & 1) ^ (me >> 2)) == 1
    d_px = jnp.where(takes_c, d_c, d_p0)
    d_given = jnp.where(takes_c, d_p0, d_c)

    left = jnp.concatenate([d_self, d_a, d_pa, d_px, d_pc], 0)
    cut = (left.shape[0] // 2 + 15) // 16 * 16
    rights = [(d_pb, lambda v: occ_hop(v, 1, 1)), (d_given, lambda v: px_hop(v, 1)), (d_pc, lambda v: occ_hop(v, 2, 1))]
    blocks = [(0, left)]
    up = down = left
    arrived = []
    for step in range(1, Z // 2):
        value, move = rights[step - 1]
        up, down, value = lax.optimization_barrier((up, down, value))
        up, down, value = lax.optimization_barrier((z_hop(up, 1), z_hop(down, -1), move(value)))
        arrived.append(value)
        blocks += [(-step, up), (step, down)]
    upper, lower = z_hop(up[:cut], 1), z_hop(down[cut:], -1)
    applied = apply_near(place, [o for o, _ in blocks], [v for _, v in blocks], fock, fock_other)
    row, to_a, to_pa, to_px = apply_last(
        place, applied, upper, lower, fock, fock_other, [d_self, right_a, *arrived]
    )
    row += occ_hop(to_a, -1, 0) + occ_hop(to_pa, -1, 1) + px_hop(to_px, 0)
    peers = 4 * Z
    spread = lax.all_to_all(
        jnp.broadcast_to(row, (peers, OCC)), ("cabs", "aux"), 0, 0, tiled=True
    )
    return jnp.sum(spread, axis=0)[None, :]


def solution(mesh):
    in_specs = (P("occ", None, "aux"), P("occ", "cabs", "aux"), P(None, "cabs"), P(), P())
    out_specs = P("occ", None)
    return jax.shard_map(shards, mesh=mesh, in_specs=in_specs, out_specs=out_specs, check_vma=False)
```

time: 758 us -> 113 us (0.15)
  waiting for transfers between devices: 580 us -> 24.8 us
  blocking collectives: 89.6 us -> 27.6 us
  matrix products: 33 us -> 0 us
  starting transfers between devices: 14.4 us -> 39.1 us
  between operations: 23.6 us -> 0.25 us
  Pallas kernels: 0 us -> 11.8 us
  local copies, waits for them, and re-layouts: 14.5 us -> 4.9 us
    all_gather x8 -> x0, waiting for transfers between devices: 280 us -> none  [apply_fock(): portion = lax.all_gather(swapped, 'cabs', axis=4, tiled=True)]
    ppermute x14 -> x30, waiting for transfers between devices: 299 us -> 24.8 us  [the longest x16 19.9 us: occ_hop(): lax.ppermute(value, 'occ', [(o, partner(o, dy, flip)) for o in range(OCC)])]
    psum x2 -> x0, blocking collectives: 89.6 us -> none  [the longest x1 66 us: fit_reduce(): totals = lax.psum(partial_sums, 'aux')]
    dot_general x23 -> x0, matrix products: 33 us -> none  [the longest x8 22.9 us: apply_fock(): product = jnp.dot(flattened, coupled, preferred_element_type=jnp.float32)]
    all_to_all x0 -> x1, blocking collectives: none -> 27.6 us  [shards(): lax.all_to_all(jnp.broadcast_to(row, (peers, OCC)), ('cabs', 'aux'), 0, 0...]
    ppermute x14 -> x30, starting transfers between devices: 14.1 us -> 39.1 us  [the longest x16 14 us: occ_hop(): lax.ppermute(value, 'occ', [(o, partner(o, dy, flip)) for o in range(OCC)])]
    pallas_call x0 -> x6, Pallas kernels: none -> 11.8 us  [the longest x3 7.37 us: fit_sums(): pl.pallas_call(body, out_shape=tuple(shapes), in_specs=[SMEM] + [ANY] * c...]
    slice x8 -> x3, local copies, waits for them, and re-layouts: 7.83 us -> 0.02 us  [the longest x2 0.02 us: shards(): upper, lower = (z_hop(up[:cut], 1), z_hop(down[cut:], -1))]
  transfers between devices with their start and end apart: 22 -> 30, of which waited for: 20 -> 12; matrix products, arithmetic and copies ran while one was open for 5% -> 6% of each run, Pallas kernels for 0% -> 10%
where the time goes in v2:
time: 113 us
  starting transfers between devices  39.1 us (35%)
  blocking collectives  27.6 us (24%)
  waiting for transfers between devices  24.8 us (22%)
  Pallas kernels  11.8 us (10%)
  local copies, waits for them, and re-layouts  4.9 us (4%)
  other arithmetic  4.43 us (4%)
    all_to_all x1, blocking collectives, shards(): lax.all_to_all(jnp.broadcast_to(row, (peers, OCC)), ('cabs', 'aux'), 0, 0...  27.6 us
    ppermute x16, waiting for transfers between devices, occ_hop(): lax.ppermute(value, 'occ', [(o, partner(o, dy, flip)) for o in range(OCC)])  19.9 us
    ppermute x16, starting transfers between devices, occ_hop(): lax.ppermute(value, 'occ', [(o, partner(o, dy, flip)) for o in range(OCC)])  14 us
    ppermute x8, starting transfers between devices, z_hop(): lax.ppermute(value, 'cabs', [(c, (c // 2 + dz) % Z * 2 + c % 2) for c in...  13.8 us
    pallas_call x3, Pallas kernels, fit_sums(): pl.pallas_call(body, out_shape=tuple(shapes), in_specs=[SMEM] + [ANY] * c...  7.37 us
    ppermute x2, starting transfers between devices, aux_swap(): return lax.ppermute(value, 'aux', [(0, 1), (1, 0)])  5.91 us
    ppermute x2, starting transfers between devices, core_swap(): return lax.ppermute(value, 'cabs', [(c, c ^ 1) for c in range(2 * Z)])  4.48 us
    ppermute x2, waiting for transfers between devices, px_hop(): return lax.ppermute(value, 'occ', pairs)  3.59 us
  transfers between devices with their start and end apart: 30, of which 12 were waited for; matrix products, arithmetic and copies ran while one was open for 6% of the time, Pallas kernels for 10%

profile of v2, /device:TPU:1, one launch (start us, length us, event | category | flops | bytes accessed | tf_op | source)
XLA Modules:
  0.0 113.0 jit_solution(9406617269399368563)
XLA Ops:
  0.0 3.2 %collective-permute-start.4 = (bf16[4096,256]{1,0:T(8,128)(2,1)}, bf16[4096,256]{1,0:T(8,128)(2,1)S(1)}, u32[]{:S(2)}, u32[]{:S(2)}) collective-permute-start(bf16[4096,256]{1,0:T(8,128)(2,1)} %own_ref.1), channel_id=1, source_target_pairs={{0,2},{2,0},{4,6},{6,4},{8,10},{10,8},{12,14},{14,12},{16,18},{18,... | collective-permute-start | bytes 6291464 | tf_op jit(solution)/shard_map/ppermute | solution.py:44
  4.0 1.5 %collective-permute-start.2 = (bf16[80,2560]{1,0:T(8,128)(2,1)}, bf16[80,2560]{1,0:T(8,128)(2,1)S(1)}, u32[]{:S(2)}, u32[]{:S(2)}) collective-permute-start(bf16[80,2560]{1,0:T(8,128)(2,1)} %dynamic-slice_bitcast_fusion.refs_0_), channel_id=1, source_target_pairs={{0,192},{32,224},{64,0},{96,32},{128,64},{160,96},{192,128},{224,1... | collective-permute-start | bytes 1228808 | tf_op jit(solution)/shard_map/ppermute | solution.py:28
  5.5 1.2 %collective-permute-start = (bf16[80,2560]{1,0:T(8,128)(2,1)}, bf16[80,2560]{1,0:T(8,128)(2,1)}, u32[]{:S(2)}, u32[]{:S(2)}) collective-permute-start(bf16[80,2560]{1,0:T(8,128)(2,1)} %dynamic-slice_bitcast_fusion.refs_0_), channel_id=1, source_target_pairs={{0,32},{32,0},{64,96},{96,64},{128,160},{160,128},{192,224},{224,1... | collective-permute-start | bytes 1228808 | tf_op jit(solution)/shard_map/ppermute | solution.py:28
  6.7 1.2 %collective-permute-start.3 = (bf16[256,2560]{1,0:T(8,128)(2,1)}, bf16[256,2560]{1,0:T(8,128)(2,1)}, u32[]{:S(2)}, u32[]{:S(2)}) collective-permute-start(bf16[256,2560]{1,0:T(8,128)(2,1)} %bitcast.37), channel_id=1, source_target_pairs={{0,2},{2,0},{4,6},{6,4},{8,10},{10,8},{12,14},{14,12},{16,18},{18,... | collective-permute-start | bytes 3932168 | tf_op jit(solution)/shard_map/ppermute | solution.py:44
  9.0 1.3 %fusion.4 = s32[]{:T(128)} fusion(s32[8]{0:T(128)} %param.11, s32[]{:T(128)} %axis_index.36), kind=kLoop, calls=%fused_computation.27 | loop fusion | flops 23 | bytes 40 | tf_op jit(solution)/shard_map/reduce_sum | solution.py:253
  12.5 1.3 %copy-done.2 = bf16[1,256,2560]{2,1,0:T(8,128)(2,1)S(1)} copy-done((bf16[1,256,2560]{2,1,0:T(8,128)(2,1)S(1)}, bf16[1,256,2560]{2,1,0:T(8,128)(2,1)}, u32[]{:S(2)}) %copy-start.2) | copy-done | bytes 1310744
  13.8 2.0 %shard_map.73.refs_4_ = bf16[2560,512]{1,0:T(8,128)(2,1)S(1)} custom-call(bf16[256,2560]{1,0:T(8,128)(2,1)S(1)} %bitcast.38, bf16[256,2560]{1,0:T(8,128)(2,1)} %collective-permute-done.3.other_ref), custom_call_target="tpu_custom_call" | custom-call | bytes 5242880 | tf_op jit(solution)/shard_map/pallas_call | solution.py:66
  15.9 1.1 %collective-permute-done.1.refs_2_ = bf16[80,2560]{1,0:T(8,128)(2,1)} collective-permute-done((bf16[80,2560]{1,0:T(8,128)(2,1)}, bf16[80,2560]{1,0:T(8,128)(2,1)}, u32[]{:S(2)}, u32[]{:S(2)}) %collective-permute-start.1) | collective-permute-done | bytes 409632 | tf_op jit(solution)/shard_map/ppermute | solution.py:28
  17.1 1.9 %collective-permute-start.7 = (bf16[48,2560]{1,0:T(8,128)(2,1)S(1)}, bf16[48,2560]{1,0:T(8,128)(2,1)S(1)}, u32[]{:S(2)}, u32[]{:S(2)}) collective-permute-start(bf16[48,2560]{1,0:T(8,128)(2,1)S(1)} %constant_dynamic-slice_fusion.3), channel_id=1, source_target_pairs={{0,192},{32,224},{64,0},{96,32},{128,64},{160,96},{192,128},{224,1... | collective-permute-start | bytes 737288 | tf_op jit(solution)/shard_map/ppermute | solution.py:28
  22.2 2.9 %shard_map.74 = (f32[4,40,512]{2,1,0:T(8,128)S(1)}, f32[4,40,512]{2,1,0:T(8,128)S(1)}) custom-call(s32[4]{0:T(128)S(1)} %pad_add_fusion.place_ref, bf16[80,2560]{1,0:T(8,128)(2,1)} %dynamic-slice_bitcast_fusion.refs_0_, bf16[80,2560]{1,0:T(8,128)(2,1)} %collective-permute-done.refs_1_, bf16[80,2560]{1,0:T(8,128)(2,1)} %collective-permute-done.1.refs_2_, ...), custom_call_target="tpu_custom_call" | custom-call | flops 838860800 | bytes 5570560 | tf_op jit(solution)/shard_map/pallas_call | solution.py:122
  25.1 2.6 %collective-permute-start.9 = (f32[4,40,512]{2,1,0:T(8,128)S(1)}, f32[4,40,512]{2,1,0:T(8,128)S(1)}, u32[]{:S(2)}, u32[]{:S(2)}) collective-permute-start(f32[4,40,512]{2,1,0:T(8,128)S(1)} %get-tuple-element.58), channel_id=1, source_target_pairs={{0,1},{1,0},{2,3},{3,2},{4,5},{5,4},{6,7},{7,6},{8,9},{9,8},{10,11... | collective-permute-start | bytes 983048 | tf_op jit(solution)/shard_map/ppermute | solution.py:48
  27.6 2.2 %collective-permute-start.12 = (bf16[32,2560]{1,0:T(8,128)(2,1)S(1)}, bf16[32,2560]{1,0:T(8,128)(2,1)S(1)}, u32[]{:S(2)}, u32[]{:S(2)}) collective-permute-start(bf16[32,2560]{1,0:T(8,128)(2,1)S(1)} %constant_dynamic-slice_fusion.1), channel_id=1, source_target_pairs={{0,192},{32,224},{64,0},{96,32},{128,64},{160,96},{192,128},{224,1... | collective-permute-start | bytes 491528 | tf_op jit(solution)/shard_map/ppermute | solution.py:28
  30.1 1.7 %collective-permute-start.13 = (bf16[32,2560]{1,0:T(8,128)(2,1)S(1)}, bf16[32,2560]{1,0:T(8,128)(2,1)S(1)}, u32[]{:S(2)}, u32[]{:S(2)}) collective-permute-start(bf16[32,2560]{1,0:T(8,128)(2,1)S(1)} %constant_dynamic-slice_fusion), channel_id=1, source_target_pairs={{0,128},{32,160},{64,192},{96,224},{128,0},{160,32},{192,64},{224,... | collective-permute-start | bytes 491528 | tf_op jit(solution)/shard_map/ppermute | solution.py:28
  31.8 2.8 %collective-permute-done.6.refs_1_ = bf16[48,2560]{1,0:T(8,128)(2,1)S(1)} collective-permute-done((bf16[48,2560]{1,0:T(8,128)(2,1)S(1)}, bf16[48,2560]{1,0:T(8,128)(2,1)S(1)}, u32[]{:S(2)}, u32[]{:S(2)}) %collective-permute-start.6) | collective-permute-done | bytes 245792 | tf_op jit(solution)/shard_map/ppermute | solution.py:28
  34.6 2.6 %shard_map.75 = (f32[4,40,512]{2,1,0:T(8,128)S(1)}, f32[4,40,512]{2,1,0:T(8,128)S(1)}) custom-call(s32[4]{0:T(128)S(1)} %pad_add_fusion.place_ref, bf16[48,2560]{1,0:T(8,128)(2,1)S(1)} %collective-permute-done.5.refs_0_, bf16[48,2560]{1,0:T(8,128)(2,1)S(1)} %collective-permute-done.6.refs_1_, bf16[48,2560]{1,0:T(8,128)(2,1)S(1)} %collective-permute-done.7.refs_2_, ...), custom_call_target="tpu_custom_call" | custom-call | flops 503316480 | bytes 4390912 | tf_op jit(solution)/shard_map/pallas_call | solution.py:122
  37.2 3.3 %collective-permute-start.14 = (f32[4,40,512]{2,1,0:T(8,128)S(1)}, f32[4,40,512]{2,1,0:T(8,128)S(1)}, u32[]{:S(2)}, u32[]{:S(2)}) collective-permute-start(f32[4,40,512]{2,1,0:T(8,128)S(1)} %get-tuple-element.69), channel_id=1, source_target_pairs={{0,1},{1,0},{2,3},{3,2},{4,5},{5,4},{6,7},{7,6},{8,9},{9,8},{10,11... | collective-permute-start | bytes 983048 | tf_op jit(solution)/shard_map/ppermute | solution.py:48
  40.5 2.7 %collective-permute-done.11.refs_1_ = bf16[32,2560]{1,0:T(8,128)(2,1)S(1)} collective-permute-done((bf16[32,2560]{1,0:T(8,128)(2,1)S(1)}, bf16[32,2560]{1,0:T(8,128)(2,1)S(1)}, u32[]{:S(2)}, u32[]{:S(2)}) %collective-permute-start.11) | collective-permute-done | bytes 163872 | tf_op jit(solution)/shard_map/ppermute | solution.py:28
  43.6 1.9 %shard_map.76 = f32[4,40,512]{2,1,0:T(8,128)S(1)} custom-call(s32[4]{0:T(128)S(1)} %pad_add_fusion.place_ref, bf16[32,2560]{1,0:T(8,128)(2,1)S(1)} %collective-permute-done.10.refs_0_, bf16[32,2560]{1,0:T(8,128)(2,1)S(1)} %collective-permute-done.11.refs_1_, bf16[32,2560]{1,0:T(8,128)(2,1)S(1)} %collective-permute-done.12.refs_2_, ...), custom_call_target="tpu_custom_call" | custom-call | flops 335544320 | bytes 3801088 | tf_op jit(solution)/shard_map/pallas_call | solution.py:122
  45.5 2.4 %collective-permute-done.15.refs_1_ = bf16[40,512]{1,0:T(8,128)(2,1)S(1)} collective-permute-done((bf16[40,512]{1,0:T(8,128)(2,1)S(1)}, bf16[40,512]{1,0:T(8,128)(2,1)S(1)}, u32[]{:S(2)}, u32[]{:S(2)}) %collective-permute-start.15) | collective-permute-done | bytes 40992 | tf_op jit(solution)/shard_map/ppermute | solution.py:28
  48.0 1.7 %collective-permute-start.16 = (bf16[200,512]{1,0:T(8,128)(2,1)S(1)}, bf16[200,512]{1,0:T(8,128)(2,1)S(1)}, u32[]{:S(2)}, u32[]{:S(2)}) collective-permute-start(bf16[200,512]{1,0:T(8,128)(2,1)S(1)} %constant_dynamic-update-slice_fusion.refs_0_), channel_id=1, source_target_pairs={{0,4},{2,6},{4,8},{6,10},{8,12},{10,14},{12,16},{14,18},{16,20},{1... | collective-permute-start | bytes 614408 | tf_op jit(solution)/shard_map/ppermute | solution.py:40
  49.8 4.0 %collective-permute-start.17 = (bf16[200,512]{1,0:T(8,128)(2,1)S(1)}, bf16[200,512]{1,0:T(8,128)(2,1)S(1)}, u32[]{:S(2)}, u32[]{:S(2)}) collective-permute-start(bf16[200,512]{1,0:T(8,128)(2,1)S(1)} %constant_dynamic-update-slice_fusion.refs_0_), channel_id=1, source_target_pairs={{0,28},{2,30},{4,0},{6,2},{8,4},{10,6},{12,8},{14,10},{16,12},{18,... | collective-permute-start | bytes 614408 | tf_op jit(solution)/shard_map/ppermute | solution.py:40
  53.8 5.0 %collective-permute-done.18.refs_2_ = bf16[40,512]{1,0:T(8,128)(2,1)S(1)} collective-permute-done((bf16[40,512]{1,0:T(8,128)(2,1)S(1)}, bf16[40,512]{1,0:T(8,128)(2,1)S(1)}, u32[]{:S(2)}, u32[]{:S(2)}) %collective-permute-start.18) | collective-permute-done | bytes 40992 | tf_op jit(solution)/shard_map/ppermute | solution.py:28
  58.8 2.7 %collective-permute-start.20 = (bf16[200,512]{1,0:T(8,128)(2,1)S(1)}, bf16[200,512]{1,0:T(8,128)(2,1)S(1)}, u32[]{:S(2)}, u32[]{:S(2)}) collective-permute-start(bf16[200,512]{1,0:T(8,128)(2,1)S(1)} %collective-permute-done.17.refs_2_), channel_id=1, source_target_pairs={{0,28},{2,30},{4,0},{6,2},{8,4},{10,6},{12,8},{14,10},{16,12},{18,... | collective-permute-start | bytes 614408 | tf_op jit(solution)/shard_map/ppermute | solution.py:40
  61.8 2.5 %collective-permute-done.21.refs_3_ = bf16[40,512]{1,0:T(8,128)(2,1)S(1)} collective-permute-done((bf16[40,512]{1,0:T(8,128)(2,1)S(1)}, bf16[40,512]{1,0:T(8,128)(2,1)S(1)}, u32[]{:S(2)}, u32[]{:S(2)}) %collective-permute-start.21) | collective-permute-done | bytes 40992 | tf_op jit(solution)/shard_map/ppermute | solution.py:36
  65.1 2.1 %collective-permute-start.23 = (bf16[200,512]{1,0:T(8,128)(2,1)S(1)}, bf16[200,512]{1,0:T(8,128)(2,1)S(1)}, u32[]{:S(2)}, u32[]{:S(2)}) collective-permute-start(bf16[200,512]{1,0:T(8,128)(2,1)S(1)} %collective-permute-done.20.refs_4_), channel_id=1, source_target_pairs={{0,28},{2,30},{4,0},{6,2},{8,4},{10,6},{12,8},{14,10},{16,12},{18,... | collective-permute-start | bytes 614408 | tf_op jit(solution)/shard_map/ppermute | solution.py:40
  67.2 1.5 %collective-permute-start.24 = (bf16[40,512]{1,0:T(8,128)(2,1)S(1)}, bf16[40,512]{1,0:T(8,128)(2,1)S(1)}, u32[]{:S(2)}, u32[]{:S(2)}) collective-permute-start(bf16[40,512]{1,0:T(8,128)(2,1)S(1)} %get-tuple-element.83), channel_id=1, source_target_pairs={{0,160},{32,128},{64,224},{96,192},{128,32},{160,0},{192,96},{224,... | collective-permute-start | bytes 122888 | tf_op jit(solution)/shard_map/ppermute | solution.py:28
  68.8 3.7 %collective-permute-done.24.refs_4_ = bf16[40,512]{1,0:T(8,128)(2,1)S(1)} collective-permute-done((bf16[40,512]{1,0:T(8,128)(2,1)S(1)}, bf16[40,512]{1,0:T(8,128)(2,1)S(1)}, u32[]{:S(2)}, u32[]{:S(2)}) %collective-permute-start.24) | collective-permute-done | bytes 40992 | tf_op jit(solution)/shard_map/ppermute | solution.py:28
  72.9 2.4 %collective-permute-start.26 = (bf16[88,512]{1,0:T(8,128)(2,1)S(1)}, bf16[88,512]{1,0:T(8,128)(2,1)S(1)}, u32[]{:S(2)}, u32[]{:S(2)}) collective-permute-start(bf16[88,512]{1,0:T(8,128)(2,1)S(1)} %slice.15), channel_id=1, source_target_pairs={{0,28},{2,30},{4,0},{6,2},{8,4},{10,6},{12,8},{14,10},{16,12},{18,... | collective-permute-start | bytes 270344 | tf_op jit(solution)/shard_map/ppermute | solution.py:40
  75.3 1.5 %shard_map.77.applied_ref = f32[200,512]{1,0:T(8,128)S(1)} custom-call(s32[4]{0:T(128)S(1)} %pad_add_fusion.place_ref, bf16[200,512]{1,0:T(8,128)(2,1)S(1)} %constant_dynamic-update-slice_fusion.refs_0_, bf16[200,512]{1,0:T(8,128)(2,1)S(1)} %collective-permute-done.16.refs_1_, bf16[200,512]{1,0:T(8,128)(2,1)S(1)} %collective-permute-done.17.refs_2_, ...), custom_call_target="tpu_custom_call" | custom-call | flops 734003200 | bytes 5103616 | tf_op jit(solution)/shard_map/pallas_call | solution.py:173
  78.7 1.4 %collective-permute-start.27 = (f32[1,8]{1,0:T(1,128)S(1)}, f32[1,8]{1,0:T(1,128)S(1)}, u32[]{:S(2)}, u32[]{:S(2)}) collective-permute-start(f32[1,8]{1,0:T(1,128)S(1)} %get-tuple-element.92), channel_id=1, source_target_pairs={{0,192},{32,224},{64,0},{96,32},{128,64},{160,96},{192,128},{224,1... | collective-permute-start | bytes 104 | tf_op jit(solution)/shard_map/ppermute | solution.py:28
  81.4 2.3 %collective-permute-done.28 = f32[1,8]{1,0:T(1,128)S(1)} collective-permute-done((f32[1,8]{1,0:T(1,128)S(1)}, f32[1,8]{1,0:T(1,128)S(1)}, u32[]{:S(2)}, u32[]{:S(2)}) %collective-permute-start.28) | collective-permute-done | bytes 64 | tf_op jit(solution)/shard_map/ppermute | solution.py:28
  84.8 27.6 %all_to_all.6 = f32[32,1,8]{2,1,0:T(1,128)S(1)} all-to-all(f32[32,1,8]{2,1,0:T(1,128)S(1)} %broadcast_in_dim.63), channel_id=1, replica_groups=mesh['occ'=8,'cabs'=16,'aux'=2] {'cabs','aux'}, dimensions={0} | all-to-all | bytes 2048 | tf_op jit(solution)/shard_map/all_to_all | solution.py:326
  (73 shorter events, 14.4 us)
Async XLA Ops:
  0.0 3.2 %copy-start = (bf16[1,160,2560]{2,1,0:T(8,128)(2,1)S(1)}, bf16[1,160,2560]{2,1,0:T(8,128)(2,1)}, u32[]{:S(2)}) copy-start(bf16[1,160,2560]{2,1,0:T(8,128)(2,1)} %param.7) | copy-start | bytes 2457604
  0.0 17.0 %collective-permute-start.4 = (bf16[4096,256]{1,0:T(8,128)(2,1)}, bf16[4096,256]{1,0:T(8,128)(2,1)S(1)}, u32[]{:S(2)}, u32[]{:S(2)}) collective-permute-start(bf16[4096,256]{1,0:T(8,128)(2,1)} %own_ref.1), channel_id=1, source_target_pairs={{0,2},{2,0},{4,6},{6,4},{8,10},{10,8},{12,14},{14,12},{16,18},{18,... | collective-permute-start | bytes 6291464 | tf_op jit(solution)/shard_map/ppermute | solution.py:44
  4.0 11.9 %collective-permute-start.2 = (bf16[80,2560]{1,0:T(8,128)(2,1)}, bf16[80,2560]{1,0:T(8,128)(2,1)S(1)}, u32[]{:S(2)}, u32[]{:S(2)}) collective-permute-start(bf16[80,2560]{1,0:T(8,128)(2,1)} %dynamic-slice_bitcast_fusion.refs_0_), channel_id=1, source_target_pairs={{0,192},{32,224},{64,0},{96,32},{128,64},{160,96},{192,128},{224,1... | collective-permute-start | bytes 1228808 | tf_op jit(solution)/shard_map/ppermute | solution.py:28
  5.5 11.5 %collective-permute-start.1 = (bf16[80,2560]{1,0:T(8,128)(2,1)}, bf16[80,2560]{1,0:T(8,128)(2,1)}, u32[]{:S(2)}, u32[]{:S(2)}) collective-permute-start(bf16[80,2560]{1,0:T(8,128)(2,1)} %dynamic-slice_bitcast_fusion.refs_0_), channel_id=1, source_target_pairs={{0,64},{32,96},{64,128},{96,160},{128,192},{160,224},{192,0},{224,... | collective-permute-start | bytes 1228808 | tf_op jit(solution)/shard_map/ppermute | solution.py:28
  5.5 11.5 %collective-permute-start = (bf16[80,2560]{1,0:T(8,128)(2,1)}, bf16[80,2560]{1,0:T(8,128)(2,1)}, u32[]{:S(2)}, u32[]{:S(2)}) collective-permute-start(bf16[80,2560]{1,0:T(8,128)(2,1)} %dynamic-slice_bitcast_fusion.refs_0_), channel_id=1, source_target_pairs={{0,32},{32,0},{64,96},{96,64},{128,160},{160,128},{192,224},{224,1... | collective-permute-start | bytes 1228808 | tf_op jit(solution)/shard_map/ppermute | solution.py:28
  6.7 5.8 %collective-permute-start.3 = (bf16[256,2560]{1,0:T(8,128)(2,1)}, bf16[256,2560]{1,0:T(8,128)(2,1)}, u32[]{:S(2)}, u32[]{:S(2)}) collective-permute-start(bf16[256,2560]{1,0:T(8,128)(2,1)} %bitcast.37), channel_id=1, source_target_pairs={{0,2},{2,0},{4,6},{6,4},{8,10},{10,8},{12,14},{14,12},{16,18},{18,... | collective-permute-start | bytes 3932168 | tf_op jit(solution)/shard_map/ppermute | solution.py:44
  17.1 10.6 %collective-permute-start.7 = (bf16[48,2560]{1,0:T(8,128)(2,1)S(1)}, bf16[48,2560]{1,0:T(8,128)(2,1)S(1)}, u32[]{:S(2)}, u32[]{:S(2)}) collective-permute-start(bf16[48,2560]{1,0:T(8,128)(2,1)S(1)} %constant_dynamic-slice_fusion.3), channel_id=1, source_target_pairs={{0,192},{32,224},{64,0},{96,32},{128,64},{160,96},{192,128},{224,1... | collective-permute-start | bytes 737288 | tf_op jit(solution)/shard_map/ppermute | solution.py:28
  19.0 10.8 %collective-permute-start.5 = (bf16[48,2560]{1,0:T(8,128)(2,1)S(1)}, bf16[48,2560]{1,0:T(8,128)(2,1)S(1)}, u32[]{:S(2)}, u32[]{:S(2)}) collective-permute-start(bf16[48,2560]{1,0:T(8,128)(2,1)S(1)} %constant_dynamic-slice_fusion.3), channel_id=1, source_target_pairs={{0,32},{32,0},{64,96},{96,64},{128,160},{160,128},{192,224},{224,1... | collective-permute-start | bytes 737288 | tf_op jit(solution)/shard_map/ppermute | solution.py:28
  20.5 9.7 %collective-permute-start.8 = (bf16[48,2560]{1,0:T(8,128)(2,1)S(1)}, bf16[48,2560]{1,0:T(8,128)(2,1)S(1)}, u32[]{:S(2)}, u32[]{:S(2)}) collective-permute-start(bf16[48,2560]{1,0:T(8,128)(2,1)S(1)} %constant_dynamic-slice_fusion.2), channel_id=1, source_target_pairs={{0,128},{32,160},{64,192},{96,224},{128,0},{160,32},{192,64},{224,... | collective-permute-start | bytes 737288 | tf_op jit(solution)/shard_map/ppermute | solution.py:28
  20.6 14.0 %collective-permute-start.6 = (bf16[48,2560]{1,0:T(8,128)(2,1)S(1)}, bf16[48,2560]{1,0:T(8,128)(2,1)S(1)}, u32[]{:S(2)}, u32[]{:S(2)}) collective-permute-start(bf16[48,2560]{1,0:T(8,128)(2,1)S(1)} %constant_dynamic-slice_fusion.2), channel_id=1, source_target_pairs={{0,64},{32,96},{64,128},{96,160},{128,192},{160,224},{192,0},{224,... | collective-permute-start | bytes 737288 | tf_op jit(solution)/shard_map/ppermute | solution.py:28
  25.1 18.1 %collective-permute-start.9 = (f32[4,40,512]{2,1,0:T(8,128)S(1)}, f32[4,40,512]{2,1,0:T(8,128)S(1)}, u32[]{:S(2)}, u32[]{:S(2)}) collective-permute-start(f32[4,40,512]{2,1,0:T(8,128)S(1)} %get-tuple-element.58), channel_id=1, source_target_pairs={{0,1},{1,0},{2,3},{3,2},{4,5},{5,4},{6,7},{7,6},{8,9},{9,8},{10,11... | collective-permute-start | bytes 983048 | tf_op jit(solution)/shard_map/ppermute | solution.py:48
  27.6 9.5 %collective-permute-start.12 = (bf16[32,2560]{1,0:T(8,128)(2,1)S(1)}, bf16[32,2560]{1,0:T(8,128)(2,1)S(1)}, u32[]{:S(2)}, u32[]{:S(2)}) collective-permute-start(bf16[32,2560]{1,0:T(8,128)(2,1)S(1)} %constant_dynamic-slice_fusion.1), channel_id=1, source_target_pairs={{0,192},{32,224},{64,0},{96,32},{128,64},{160,96},{192,128},{224,1... | collective-permute-start | bytes 491528 | tf_op jit(solution)/shard_map/ppermute | solution.py:28
  29.8 10.7 %collective-permute-start.10 = (bf16[32,2560]{1,0:T(8,128)(2,1)S(1)}, bf16[32,2560]{1,0:T(8,128)(2,1)S(1)}, u32[]{:S(2)}, u32[]{:S(2)}) collective-permute-start(bf16[32,2560]{1,0:T(8,128)(2,1)S(1)} %constant_dynamic-slice_fusion.1), channel_id=1, source_target_pairs={{0,32},{32,0},{64,96},{96,64},{128,160},{160,128},{192,224},{224,1... | collective-permute-start | bytes 491528 | tf_op jit(solution)/shard_map/ppermute | solution.py:28
  30.1 10.4 %collective-permute-start.13 = (bf16[32,2560]{1,0:T(8,128)(2,1)S(1)}, bf16[32,2560]{1,0:T(8,128)(2,1)S(1)}, u32[]{:S(2)}, u32[]{:S(2)}) collective-permute-start(bf16[32,2560]{1,0:T(8,128)(2,1)S(1)} %constant_dynamic-slice_fusion), channel_id=1, source_target_pairs={{0,128},{32,160},{64,192},{96,224},{128,0},{160,32},{192,64},{224,... | collective-permute-start | bytes 491528 | tf_op jit(solution)/shard_map/ppermute | solution.py:28
  34.6 8.6 %collective-permute-start.11 = (bf16[32,2560]{1,0:T(8,128)(2,1)S(1)}, bf16[32,2560]{1,0:T(8,128)(2,1)S(1)}, u32[]{:S(2)}, u32[]{:S(2)}) collective-permute-start(bf16[32,2560]{1,0:T(8,128)(2,1)S(1)} %constant_dynamic-slice_fusion), channel_id=1, source_target_pairs={{0,64},{32,96},{64,128},{96,160},{128,192},{160,224},{192,0},{224,... | collective-permute-start | bytes 491528 | tf_op jit(solution)/shard_map/ppermute | solution.py:28
  37.2 10.7 %collective-permute-start.14 = (f32[4,40,512]{2,1,0:T(8,128)S(1)}, f32[4,40,512]{2,1,0:T(8,128)S(1)}, u32[]{:S(2)}, u32[]{:S(2)}) collective-permute-start(f32[4,40,512]{2,1,0:T(8,128)S(1)} %get-tuple-element.69), channel_id=1, source_target_pairs={{0,1},{1,0},{2,3},{3,2},{4,5},{5,4},{6,7},{7,6},{8,9},{9,8},{10,11... | collective-permute-start | bytes 983048 | tf_op jit(solution)/shard_map/ppermute | solution.py:48
  43.3 4.6 %collective-permute-start.15 = (bf16[40,512]{1,0:T(8,128)(2,1)S(1)}, bf16[40,512]{1,0:T(8,128)(2,1)S(1)}, u32[]{:S(2)}, u32[]{:S(2)}) collective-permute-start(bf16[40,512]{1,0:T(8,128)(2,1)S(1)} %slice_bitcast_fusion.3), channel_id=1, source_target_pairs={{0,64},{32,96},{64,128},{96,160},{128,192},{160,224},{192,0},{224,... | collective-permute-start | bytes 122888 | tf_op jit(solution)/shard_map/ppermute | solution.py:28
  43.6 31.7 %copy-start.1 = (bf16[4096,256]{1,0:T(8,128)(2,1)S(1)}, bf16[4096,256]{1,0:T(8,128)(2,1)}, u32[]{:S(2)}) copy-start(bf16[4096,256]{1,0:T(8,128)(2,1)} %own_ref.1) | copy-start | bytes 6291460
  48.0 10.7 %collective-permute-start.16 = (bf16[200,512]{1,0:T(8,128)(2,1)S(1)}, bf16[200,512]{1,0:T(8,128)(2,1)S(1)}, u32[]{:S(2)}, u32[]{:S(2)}) collective-permute-start(bf16[200,512]{1,0:T(8,128)(2,1)S(1)} %constant_dynamic-update-slice_fusion.refs_0_), channel_id=1, source_target_pairs={{0,4},{2,6},{4,8},{6,10},{8,12},{10,14},{12,16},{14,18},{16,20},{1... | collective-permute-start | bytes 614408 | tf_op jit(solution)/shard_map/ppermute | solution.py:40
  49.8 9.0 %collective-permute-start.17 = (bf16[200,512]{1,0:T(8,128)(2,1)S(1)}, bf16[200,512]{1,0:T(8,128)(2,1)S(1)}, u32[]{:S(2)}, u32[]{:S(2)}) collective-permute-start(bf16[200,512]{1,0:T(8,128)(2,1)S(1)} %constant_dynamic-update-slice_fusion.refs_0_), channel_id=1, source_target_pairs={{0,28},{2,30},{4,0},{6,2},{8,4},{10,6},{12,8},{14,10},{16,12},{18,... | collective-permute-start | bytes 614408 | tf_op jit(solution)/shard_map/ppermute | solution.py:40
  53.8 5.0 %collective-permute-start.18 = (bf16[40,512]{1,0:T(8,128)(2,1)S(1)}, bf16[40,512]{1,0:T(8,128)(2,1)S(1)}, u32[]{:S(2)}, u32[]{:S(2)}) collective-permute-start(bf16[40,512]{1,0:T(8,128)(2,1)S(1)} %get-tuple-element.73), channel_id=1, source_target_pairs={{0,96},{32,64},{64,160},{96,128},{128,224},{160,192},{192,32},{224... | collective-permute-start | bytes 122888 | tf_op jit(solution)/shard_map/ppermute | solution.py:28
  58.7 5.8 %collective-permute-start.19 = (bf16[200,512]{1,0:T(8,128)(2,1)S(1)}, bf16[200,512]{1,0:T(8,128)(2,1)S(1)}, u32[]{:S(2)}, u32[]{:S(2)}) collective-permute-start(bf16[200,512]{1,0:T(8,128)(2,1)S(1)} %collective-permute-done.16.refs_1_), channel_id=1, source_target_pairs={{0,4},{2,6},{4,8},{6,10},{8,12},{10,14},{12,16},{14,18},{16,20},{1... | collective-permute-start | bytes 614408 | tf_op jit(solution)/shard_map/ppermute | solution.py:40
  58.8 5.8 %collective-permute-start.20 = (bf16[200,512]{1,0:T(8,128)(2,1)S(1)}, bf16[200,512]{1,0:T(8,128)(2,1)S(1)}, u32[]{:S(2)}, u32[]{:S(2)}) collective-permute-start(bf16[200,512]{1,0:T(8,128)(2,1)S(1)} %collective-permute-done.17.refs_2_), channel_id=1, source_target_pairs={{0,28},{2,30},{4,0},{6,2},{8,4},{10,6},{12,8},{14,10},{16,12},{18,... | collective-permute-start | bytes 614408 | tf_op jit(solution)/shard_map/ppermute | solution.py:40
  61.4 2.9 %collective-permute-start.21 = (bf16[40,512]{1,0:T(8,128)(2,1)S(1)}, bf16[40,512]{1,0:T(8,128)(2,1)S(1)}, u32[]{:S(2)}, u32[]{:S(2)}) collective-permute-start(bf16[40,512]{1,0:T(8,128)(2,1)S(1)} %get-tuple-element.78), channel_id=1, source_target_pairs={{0,128},{32,0},{64,192},{96,64},{128,160},{160,32},{192,224},{224,... | collective-permute-start | bytes 122888 | tf_op jit(solution)/shard_map/ppermute | solution.py:36
  64.6 7.9 %collective-permute-start.22 = (bf16[200,512]{1,0:T(8,128)(2,1)S(1)}, bf16[200,512]{1,0:T(8,128)(2,1)S(1)}, u32[]{:S(2)}, u32[]{:S(2)}) collective-permute-start(bf16[200,512]{1,0:T(8,128)(2,1)S(1)} %collective-permute-done.19.refs_3_), channel_id=1, source_target_pairs={{0,4},{2,6},{4,8},{6,10},{8,12},{10,14},{12,16},{14,18},{16,20},{1... | collective-permute-start | bytes 614408 | tf_op jit(solution)/shard_map/ppermute | solution.py:40
  65.1 7.4 %collective-permute-start.23 = (bf16[200,512]{1,0:T(8,128)(2,1)S(1)}, bf16[200,512]{1,0:T(8,128)(2,1)S(1)}, u32[]{:S(2)}, u32[]{:S(2)}) collective-permute-start(bf16[200,512]{1,0:T(8,128)(2,1)S(1)} %collective-permute-done.20.refs_4_), channel_id=1, source_target_pairs={{0,28},{2,30},{4,0},{6,2},{8,4},{10,6},{12,8},{14,10},{16,12},{18,... | collective-permute-start | bytes 614408 | tf_op jit(solution)/shard_map/ppermute | solution.py:40
  67.2 5.3 %collective-permute-start.24 = (bf16[40,512]{1,0:T(8,128)(2,1)S(1)}, bf16[40,512]{1,0:T(8,128)(2,1)S(1)}, u32[]{:S(2)}, u32[]{:S(2)}) collective-permute-start(bf16[40,512]{1,0:T(8,128)(2,1)S(1)} %get-tuple-element.83), channel_id=1, source_target_pairs={{0,160},{32,128},{64,224},{96,192},{128,32},{160,0},{192,96},{224,... | collective-permute-start | bytes 122888 | tf_op jit(solution)/shard_map/ppermute | solution.py:28
  72.5 5.2 %collective-permute-start.25 = (bf16[112,512]{1,0:T(8,128)(2,1)S(1)}, bf16[112,512]{1,0:T(8,128)(2,1)S(1)}, u32[]{:S(2)}, u32[]{:S(2)}) collective-permute-start(bf16[112,512]{1,0:T(8,128)(2,1)S(1)} %slice.14), channel_id=1, source_target_pairs={{0,4},{2,6},{4,8},{6,10},{8,12},{10,14},{12,16},{14,18},{16,20},{1... | collective-permute-start | bytes 344072 | tf_op jit(solution)/shard_map/ppermute | solution.py:40
  72.9 4.0 %collective-permute-start.26 = (bf16[88,512]{1,0:T(8,128)(2,1)S(1)}, bf16[88,512]{1,0:T(8,128)(2,1)S(1)}, u32[]{:S(2)}, u32[]{:S(2)}) collective-permute-start(bf16[88,512]{1,0:T(8,128)(2,1)S(1)} %slice.15), channel_id=1, source_target_pairs={{0,28},{2,30},{4,0},{6,2},{8,4},{10,6},{12,8},{14,10},{16,12},{18,... | collective-permute-start | bytes 270344 | tf_op jit(solution)/shard_map/ppermute | solution.py:40
  78.7 2.7 %collective-permute-start.27 = (f32[1,8]{1,0:T(1,128)S(1)}, f32[1,8]{1,0:T(1,128)S(1)}, u32[]{:S(2)}, u32[]{:S(2)}) collective-permute-start(f32[1,8]{1,0:T(1,128)S(1)} %get-tuple-element.92), channel_id=1, source_target_pairs={{0,192},{32,224},{64,0},{96,32},{128,64},{160,96},{192,128},{224,1... | collective-permute-start | bytes 104 | tf_op jit(solution)/shard_map/ppermute | solution.py:28
  80.1 3.6 %collective-permute-start.28 = (f32[1,8]{1,0:T(1,128)S(1)}, f32[1,8]{1,0:T(1,128)S(1)}, u32[]{:S(2)}, u32[]{:S(2)}) collective-permute-start(f32[1,8]{1,0:T(1,128)S(1)} %get-tuple-element.93), channel_id=1, source_target_pairs={{0,224},{32,192},{64,32},{96,0},{128,96},{160,64},{192,160},{224,1... | collective-permute-start | bytes 104 | tf_op jit(solution)/shard_map/ppermute | solution.py:28
  80.9 3.9 %collective-permute-start.29 = (f32[1,8]{1,0:T(1,128)S(1)}, f32[1,8]{1,0:T(1,128)S(1)}, u32[]{:S(2)}, u32[]{:S(2)}) collective-permute-start(f32[1,8]{1,0:T(1,128)S(1)} %get-tuple-element.94), channel_id=1, source_target_pairs={{0,32},{32,160},{64,96},{96,224},{128,0},{160,128},{192,64},{224,1... | collective-permute-start | bytes 104 | tf_op jit(solution)/shard_map/ppermute | solution.py:36
  (1 other events, 1.3 us)

commit v3 on v2

v3 whole, which is shorter than its diff:
```python
import jax
import jax.numpy as jnp
from jax import lax
from jax.experimental import pallas as pl
from jax.experimental.pallas import tpu as pltpu
from jax.sharding import PartitionSpec as P

BF = jnp.bfloat16
F32 = jnp.float32
Y = 4
Z = 8
OCC = 2 * Y
KEPT = 40
STRIDE = 48
FOOT = 16
VMEM = pl.BlockSpec(memory_space=pltpu.VMEM)
SMEM = pl.BlockSpec(memory_space=pltpu.SMEM)
PARAMS = pltpu.CompilerParams(vmem_limit_bytes=8 * 2**20)

PLACES = ((0, 0), (0, 1), (-1, 0), (1, 0), (1, 1), (-1, 1), (2, 0), (2, 1))
LEFTS = ((0, 0), (0, 1), (-1, 0), (-1, 1), (2, 0), (2, 1))


def partner(me, dy, flip):
    return (((me >> 1) + dy) & (Y - 1)) * 2 + ((me & 1) ^ flip)


def occ_hop(value, dy, flip):
    return lax.ppermute(value, "occ", [(o, partner(o, dy, flip)) for o in range(OCC)])


def z_hop(value, dz):
    return lax.ppermute(value, "cabs", [(c, ((c // 2 + dz) % Z) * 2 + c % 2) for c in range(2 * Z)])


def core_swap(value):
    return lax.ppermute(value, "cabs", [(c, c ^ 1) for c in range(2 * Z)])


def aux_swap(value):
    return lax.ppermute(value, "aux", [(0, 1), (1, 0)])


def rows_dot(left, right):
    return lax.dot_general(left, right, (((1,), (1,)), ((), ())), preferred_element_type=F32)


def plain_dot(left, right):
    return lax.dot_general(left, right, (((1,), (0,)), ((), ())), preferred_element_type=F32)


def prepare(place, pair_block, block_rows, slab, slab_other):
    width, fit = slab.shape

    def body(place_ref, pair_ref, rows_ref, own_ref, other_ref, out_ref, mask_ref):
        out_ref[:, :width] = own_ref[...].T
        out_ref[:, width:] = other_ref[...].T
        me = place_ref[0]
        labels = rows_ref[pl.ds(place_ref[1], 1), :]
        first, second = labels[:, :width], labels[:, width:]
        swap = place_ref[2] == 1
        mine = jnp.where(swap, second, first)
        other = jnp.where(swap, first, second)
        for index, (dy, flip) in enumerate(PLACES):
            wanted = (pair_ref[me] + pair_ref[partner(me, dy, flip)]) & 1
            mask_ref[index : index + 1, :width] = jnp.where(mine == wanted, 1, 0)
            mask_ref[index : index + 1, width:] = jnp.where(other == wanted, 1, 0)

    return pl.pallas_call(
        body,
        out_shape=(
            jax.ShapeDtypeStruct((fit, 2 * width), BF),
            jax.ShapeDtypeStruct((len(PLACES), 2 * width), jnp.int32),
        ),
        in_specs=[SMEM, SMEM, VMEM, VMEM, VMEM],
        out_specs=(VMEM, VMEM),
        compiler_params=PARAMS,
        cost_estimate=pl.CostEstimate(
            flops=0, bytes_accessed=8 * fit * width, transcendentals=0
        ),
    )(place, pair_block, block_rows, slab, slab_other)


def fit_sums(place, parts, columns, scaled=False):
    count = len(parts)
    size = parts[0].shape[0]
    fit, width = columns.shape
    step = 2 * KEPT if size == 2 * KEPT else STRIDE
    shape = jax.ShapeDtypeStruct((count, KEPT, width), F32)
    if scaled:
        shapes = (jax.ShapeDtypeStruct((count * KEPT + FOOT, width), F32),)
    else:
        shapes = (shape, shape) if size == 2 * KEPT else (shape,)

    def body(place_ref, *refs):
        part_refs, columns_ref = refs[:count], refs[count]
        outs = refs[count + 1 : -2]
        stack_ref, total_ref = refs[-2:]
        for index in range(count):
            stack_ref[index * step : index * step + size, :] = part_refs[index][...]
        total_ref[...] = plain_dot(stack_ref[...], columns_ref[...])
        if size == 2 * KEPT:
            side = place_ref[3]
            for index in range(count):
                mine = pl.ds(pl.multiple_of(index * step + side * KEPT, 8), KEPT)
                other = pl.ds(pl.multiple_of(index * step + (1 - side) * KEPT, 8), KEPT)
                outs[0][index] = total_ref[mine, :]
                outs[1][index] = total_ref[other, :]
        elif not scaled:
            for index in range(count):
                outs[0][index] = total_ref[index * step : index * step + KEPT, :]
        else:
            blocks = [total_ref[index * step : index * step + KEPT, :] for index in range(count)]
            largest = jnp.max(jnp.abs(blocks[0]), axis=0, keepdims=True)
            for block in blocks[1:]:
                largest = jnp.maximum(largest, jnp.max(jnp.abs(block), axis=0, keepdims=True))
            largest = jnp.max(largest, axis=1, keepdims=True)
            exponent = jnp.floor(jnp.log2(jnp.maximum(largest, 1e-30)))
            scale = jnp.exp2(12.0 - exponent)
            for index in range(count):
                outs[0][index * KEPT : (index + 1) * KEPT, :] = blocks[index] * scale
            outs[0][count * KEPT :, :] = jnp.broadcast_to(exponent, (FOOT, width))

    return pl.pallas_call(
        body,
        out_shape=shapes,
        in_specs=[SMEM] + [VMEM] * (count + 1),
        out_specs=(VMEM,) * len(shapes),
        scratch_shapes=[pltpu.VMEM((count * step, fit), BF), pltpu.VMEM((count * step, width), F32)],
        compiler_params=PARAMS,
        cost_estimate=pl.CostEstimate(
            flops=2 * count * step * fit * width,
            bytes_accessed=2 * width * fit + 2 * count * size * fit + 8 * count * size * width,
            transcendentals=0,
        ),
    )(place, *parts, columns)


def apply_tile(place_ref, offset, block, own_ref, other_ref):
    width = own_ref.shape[1]
    own = other = None
    for index in range(2):
        row = (((place_ref[1] + offset) & (Z - 1)) * 2 + (place_ref[2] ^ index)) * width
        rows = pl.ds(pl.multiple_of(row, width), width)
        part = block[:, index * width : (index + 1) * width]
        to_own = plain_dot(part, own_ref[rows, :])
        to_other = plain_dot(part, other_ref[rows, :])
        own = to_own if own is None else own + to_own
        other = to_other if other is None else other + to_other
    return own, other


def apply_blocks(place, placed, fock, fock_other):
    offsets, blocks = zip(*placed)
    count = len(blocks)
    rows, columns = blocks[0].shape
    width = columns // 2

    def body(place_ref, *refs):
        own_ref, other_ref, out_ref = refs[count:]
        for index in range(count):
            own, other = apply_tile(
                place_ref, offsets[index], refs[index][...], own_ref, other_ref
            )
            if index == 0:
                out_ref[:, :width] = own
                out_ref[:, width:] = other
            else:
                out_ref[:, :width] += own
                out_ref[:, width:] += other

    return pl.pallas_call(
        body,
        out_shape=jax.ShapeDtypeStruct((rows, columns), F32),
        in_specs=[SMEM] + [VMEM] * (count + 2),
        out_specs=VMEM,
        compiler_params=PARAMS,
        cost_estimate=pl.CostEstimate(
            flops=2 * count * rows * columns * columns,
            bytes_accessed=2 * count * columns * (rows + columns),
            transcendentals=0,
        ),
    )(place, *blocks, fock, fock_other)


def apply_last(place, first_rows, applied, block, fock, fock_other, rights):
    rows, columns = applied.shape
    width = columns // 2

    def body(place_ref, first_ref, applied_ref, block_ref, own_ref, other_ref, *refs):
        right_refs, (row_ref, a_ref, pa_ref, sum_ref) = refs[:-4], refs[-4:]
        own, other = apply_tile(place_ref, Z // 2, block_ref[...], own_ref, other_ref)
        sum_ref[:, :width] = applied_ref[:, :width] + own
        sum_ref[:, width:] = applied_ref[:, width:] + other
        pieces = [ref[index] for ref in right_refs for index in range(ref.shape[0])]
        lefts = [
            ref[start : start + KEPT, :]
            for ref in (first_ref, sum_ref)
            for start in range(0, ref.shape[0], KEPT)
        ]
        sums = []
        for left, piece in zip(lefts, pieces):
            product = left * piece.astype(F32)
            sums.append(jnp.sum(jnp.sum(product, axis=0, keepdims=True), axis=1, keepdims=True))
        me = place_ref[0]
        lanes = lax.broadcasted_iota(jnp.int32, (1, OCC), 1)
        row = jnp.zeros((1, OCC), F32)
        for value, (dy, flip) in zip(sums, LEFTS):
            row += jnp.where(lanes == partner(me, dy, flip), value, 0.0)
        row_ref[...] = row
        here = lanes == me
        a_ref[...] = jnp.where(here, sums[2], 0.0)
        pa_ref[...] = jnp.where(here, sums[3], 0.0)

    shape = jax.ShapeDtypeStruct((1, OCC), F32)
    return pl.pallas_call(
        body,
        out_shape=(shape,) * 3,
        in_specs=[SMEM] + [VMEM] * (len(rights) + 5),
        out_specs=(VMEM,) * 3,
        scratch_shapes=[pltpu.VMEM((rows, columns), F32)],
        compiler_params=PARAMS,
        cost_estimate=pl.CostEstimate(
            flops=2 * rows * columns * columns,
            bytes_accessed=2 * columns * (rows + columns) + 6 * rows * columns,
            transcendentals=0,
        ),
    )(place, first_rows, applied, block, fock, fock_other, *rights)


def shards(occ_fit, cabs_fit, fock, cabs_block, pair_block):
    me = lax.axis_index("occ")
    cabs = lax.axis_index("cabs")
    side = lax.axis_index("aux")
    core = cabs & 1
    z = cabs >> 1
    place = jnp.stack([me, z, core, side]).astype(jnp.int32)
    m_rows = occ_fit.shape[1]
    width = cabs_fit.shape[1]
    half = m_rows // 2

    own = lax.dynamic_slice_in_dim(occ_fit[0], core * half, half, 0)
    slab_other = core_swap(cabs_fit[0])
    fock_other = core_swap(fock)

    p0, a, b = occ_hop(own, 0, 1), occ_hop(own, 1, 0), occ_hop(own, -1, 0)
    columns, keep_column = prepare(
        place, pair_block, cabs_block.reshape(Z, 2 * width), cabs_fit[0], slab_other
    )
    p0, a, b, columns, fock_other = lax.optimization_barrier((p0, a, b, columns, fock_other))

    def head(value):
        return lax.dynamic_slice_in_dim(value, (1 - side) * KEPT, KEPT, 0)

    def tail(value):
        return lax.dynamic_slice_in_dim(value, side * KEPT, KEPT, 0)

    def second_round(p0, b):
        return occ_hop(b, 0, 1), occ_hop(p0, 1, 0), occ_hop(b, -1, 0), occ_hop(p0, 2, 0)

    heads = second_round(head(p0), head(b))
    tails = second_round(tail(p0), tail(b))

    def masked(keep, got, first):
        whole = (keep + got).astype(BF)
        mask = keep_column[first : first + keep.shape[0]]
        return jnp.where(mask[:, None] != 0, whole, jnp.zeros_like(whole))

    keep, send = fit_sums(place, [own, p0, a, b], columns)
    keep, *heads = lax.optimization_barrier((keep, *heads))
    got = aux_swap(send)
    got, *tails = lax.optimization_barrier((got, *tails))
    near = masked(keep, got, 0)
    (send,) = fit_sums(place, heads, columns, True)
    got = aux_swap(send.astype(jnp.float16))
    (keep,) = fit_sums(place, tails, columns)
    unscale = jnp.exp2(got[-1:].astype(F32) - 12.0)
    got = (got[:-FOOT].astype(F32) * unscale).reshape(keep.shape)
    far = masked(keep, got, 4)

    first = jnp.concatenate([near[0], near[1], near[2]], 0)
    second = jnp.concatenate([far[1], far[2], far[3]], 0)
    first_blocks, second_blocks = [(0, first)], [(0, second)]

    def ring_step(step, up, down, blocks):
        up, down = z_hop(up, 1), z_hop(down, -1)
        blocks.extend([(-step, up), (step, down)])
        return up, down

    rights = [jnp.stack([near[1], far[0], far[3]])]
    moves = [(0, 1), (1, 0), (2, 0)]
    up_a = down_a = first
    up_b = down_b = second
    for step in range(1, Z // 2):
        up_a, down_a = ring_step(step, up_a, down_a, first_blocks)
        up_b, down_b, value = lax.optimization_barrier((up_b, down_b, rights[-1]))
        up_b, down_b = ring_step(step, up_b, down_b, second_blocks)
        value = occ_hop(value, *moves[step - 1])
        up_b, down_b, value = lax.optimization_barrier((up_b, down_b, value))
        rights[-1] = value
        if step == 1:
            rights.append(jnp.stack([near[3], value[1]]))
        elif step == 2:
            rights.append(jnp.stack([far[2], rights[0][2]]))
    first_blocks.append((Z // 2, z_hop(up_a, 1)))
    block = z_hop(down_b, -1)
    first = apply_blocks(place, first_blocks, fock, fock_other)
    second = apply_blocks(place, second_blocks, fock, fock_other)
    rights = [near[:1], rights[0][:1], *rights[1:]]
    row, to_a, to_pa = apply_last(place, first, second, block, fock, fock_other, rights)
    row += occ_hop(to_a, -1, 0) + occ_hop(to_pa, -1, 1)
    peers = 4 * Z
    spread = lax.all_to_all(
        jnp.broadcast_to(row, (peers, OCC)), ("cabs", "aux"), 0, 0, tiled=True
    )
    return jnp.sum(spread, axis=0)[None, :]


def solution(mesh):
    in_specs = (P("occ", None, "aux"), P("occ", "cabs", "aux"), P(None, "cabs"), P(), P())
    out_specs = P("occ", None)
    return jax.shard_map(shards, mesh=mesh, in_specs=in_specs, out_specs=out_specs, check_vma=False)
```

time: 113 us -> 108 us (0.956)
  waiting for transfers between devices: 24.8 us -> 19.4 us
  starting transfers between devices: 39.1 us -> 42.9 us
  other arithmetic: 4.43 us -> 0.9 us
  Pallas kernels: 11.8 us -> 10.3 us
  blocking collectives: 27.6 us -> 28.9 us
    ppermute x16, waiting for transfers between devices: 19.9 us -> 11.3 us  [occ_hop(): lax.ppermute(value, 'occ', [(o, partner(o, dy, flip)) for o in range(OCC)])]
    ppermute x16, starting transfers between devices: 14 us -> 18.2 us  [occ_hop(): lax.ppermute(value, 'occ', [(o, partner(o, dy, flip)) for o in range(OCC)])]
    ppermute x2 -> x0, waiting for transfers between devices: 3.59 us -> none  [px_hop(): return lax.ppermute(value, 'occ', pairs)]
    ppermute x8 -> x14, starting transfers between devices: 13.8 us -> 17.4 us  [z_hop(): lax.ppermute(value, 'cabs', [(c, (c // 2 + dz) % Z * 2 + c % 2) for c in...]
    ppermute x2, waiting for transfers between devices: 0.01 us -> 3.09 us  [aux_swap(): return lax.ppermute(value, 'aux', [(0, 1), (1, 0)])]
    reduce_sum x3 -> x0, other arithmetic: 2.22 us -> none  [the longest x1 1.29 us: shards(): mine = jnp.sum(jnp.where(lax.iota(jnp.int32, OCC) == me, pair_block, 0))]
    ppermute x8 -> x14, waiting for transfers between devices: 1.27 us -> 3.37 us  [z_hop(): lax.ppermute(value, 'cabs', [(c, (c // 2 + dz) % Z * 2 + c % 2) for c in...]
    ppermute x2, starting transfers between devices: 5.91 us -> 4.05 us  [aux_swap(): return lax.ppermute(value, 'aux', [(0, 1), (1, 0)])]
  transfers between devices with their start and end apart: 30 -> 34, of which waited for: 12 -> 13; matrix products, arithmetic and copies ran while one was open for 6% -> 2% of each run, Pallas kernels for 10% -> 9%
where the time goes in v3:
time: 108 us; the launch traced here: 107 us
  starting transfers between devices  42.9 us (40%)
  blocking collectives  28.9 us (27%)
  waiting for transfers between devices  19.4 us (18%)
  Pallas kernels  10.3 us (10%)
  local copies, waits for them, and re-layouts  4.68 us (4%)
    all_to_all x1, blocking collectives, shards(): lax.all_to_all(jnp.broadcast_to(row, (peers, OCC)), ('cabs', 'aux'), 0, 0...  28.9 us
    ppermute x16, starting transfers between devices, occ_hop(): lax.ppermute(value, 'occ', [(o, partner(o, dy, flip)) for o in range(OCC)])  18.2 us
    ppermute x14, starting transfers between devices, z_hop(): lax.ppermute(value, 'cabs', [(c, (c // 2 + dz) % Z * 2 + c % 2) for c in...  17.4 us
    ppermute x16, waiting for transfers between devices, occ_hop(): lax.ppermute(value, 'occ', [(o, partner(o, dy, flip)) for o in range(OCC)])  11.3 us
    pallas_call x3, Pallas kernels, fit_sums(): pl.pallas_call(body, out_shape=shapes, in_specs=[SMEM] + [VMEM] * (count...  4.88 us
    ppermute x2, starting transfers between devices, aux_swap(): return lax.ppermute(value, 'aux', [(0, 1), (1, 0)])  4.05 us
    ppermute x14, waiting for transfers between devices, z_hop(): lax.ppermute(value, 'cabs', [(c, (c // 2 + dz) % Z * 2 + c % 2) for c in...  3.37 us
    ppermute x2, starting transfers between devices, core_swap(): return lax.ppermute(value, 'cabs', [(c, c ^ 1) for c in range(2 * Z)])  3.24 us
  transfers between devices with their start and end apart: 34, of which 13 were waited for; matrix products, arithmetic and copies ran while one was open for 2% of the time, Pallas kernels for 9%

profile of v3, /device:TPU:1, one launch (start us, length us, event | category | flops | bytes accessed | tf_op | source)
XLA Modules:
  0.0 107.2 jit_solution(2541590007159768515)
XLA Ops:
  0.0 3.2 %collective-permute-start.4 = (bf16[4096,256]{1,0:T(8,128)(2,1)}, bf16[4096,256]{1,0:T(8,128)(2,1)S(1)}, u32[]{:S(2)}, u32[]{:S(2)}) collective-permute-start(bf16[4096,256]{1,0:T(8,128)(2,1)} %own_ref.1), channel_id=1, source_target_pairs={{0,2},{2,0},{4,6},{6,4},{8,10},{10,8},{12,14},{14,12},{16,18},{18,... | collective-permute-start | bytes 6291464 | tf_op jit(solution)/shard_map/ppermute | solution.py:37
  4.1 1.2 %collective-permute-start.2 = (bf16[80,2560]{1,0:T(8,128)(2,1)}, bf16[80,2560]{1,0:T(8,128)(2,1)}, u32[]{:S(2)}, u32[]{:S(2)}) collective-permute-start(bf16[80,2560]{1,0:T(8,128)(2,1)} %dynamic-slice_bitcast_fusion.refs_0_), channel_id=1, source_target_pairs={{0,64},{32,96},{64,128},{96,160},{128,192},{160,224},{192,0},{224,... | collective-permute-start | bytes 1228808 | tf_op jit(solution)/shard_map/ppermute | solution.py:29
  5.3 1.4 %collective-permute-start.3 = (bf16[80,2560]{1,0:T(8,128)(2,1)}, bf16[80,2560]{1,0:T(8,128)(2,1)}, u32[]{:S(2)}, u32[]{:S(2)}) collective-permute-start(bf16[80,2560]{1,0:T(8,128)(2,1)} %dynamic-slice_bitcast_fusion.refs_0_), channel_id=1, source_target_pairs={{0,192},{32,224},{64,0},{96,32},{128,64},{160,96},{192,128},{224,1... | collective-permute-start | bytes 1228808 | tf_op jit(solution)/shard_map/ppermute | solution.py:29
  7.5 1.6 %collective-permute-done.other_ref = bf16[256,2560]{1,0:T(8,128)(2,1)} collective-permute-done((bf16[256,2560]{1,0:T(8,128)(2,1)}, bf16[256,2560]{1,0:T(8,128)(2,1)}, u32[]{:S(2)}, u32[]{:S(2)}) %collective-permute-start) | collective-permute-done | bytes 1310752 | tf_op jit(solution)/shard_map/ppermute | solution.py:37
  9.1 1.3 %copy-done.2 = bf16[1,256,2560]{2,1,0:T(8,128)(2,1)S(1)} copy-done((bf16[1,256,2560]{2,1,0:T(8,128)(2,1)S(1)}, bf16[1,256,2560]{2,1,0:T(8,128)(2,1)}, u32[]{:S(2)}) %copy-start.2) | copy-done | bytes 1310744
  11.1 2.0 %shard_map.55 = (bf16[2560,512]{1,0:T(8,128)(2,1)S(1)}, s32[8,512]{1,0:T(8,128)S(1)}) custom-call(s32[4]{0:T(128)S(1)} %pad_add_fusion.place_ref, s32[8]{0:T(128)S(1)} %copy-done.3, s32[8,512]{1,0:T(8,128)S(1)} %reshape.17.rows_ref, bf16[256,2560]{1,0:T(8,128)(2,1)S(1)} %bitcast.25, bf16[256,2560]{1,0:T(8,128)(2,1)} %collective-permute-done.other_ref), custom_call_target="tpu_custom_call" | custom-call | bytes 5242880 | tf_op jit(solution)/shard_map/pallas_call | solution.py:69
  14.2 1.3 %collective-permute-done.2.refs_2_ = bf16[80,2560]{1,0:T(8,128)(2,1)} collective-permute-done((bf16[80,2560]{1,0:T(8,128)(2,1)}, bf16[80,2560]{1,0:T(8,128)(2,1)}, u32[]{:S(2)}, u32[]{:S(2)}) %collective-permute-start.2) | collective-permute-done | bytes 409632 | tf_op jit(solution)/shard_map/ppermute | solution.py:29
  16.5 1.2 %collective-permute-start.5 = (bf16[40,2560]{1,0:T(8,128)(2,1)S(1)}, bf16[40,2560]{1,0:T(8,128)(2,1)S(1)}, u32[]{:S(2)}, u32[]{:S(2)}) collective-permute-start(bf16[40,2560]{1,0:T(8,128)(2,1)S(1)} %get-tuple-element.86), channel_id=1, source_target_pairs={{0,32},{32,0},{64,96},{96,64},{128,160},{160,128},{192,224},{224,1... | collective-permute-start | bytes 614408 | tf_op jit(solution)/shard_map/ppermute | solution.py:29
  18.2 2.4 %collective-permute-start.7 = (bf16[40,2560]{1,0:T(8,128)(2,1)S(1)}, bf16[40,2560]{1,0:T(8,128)(2,1)S(1)}, u32[]{:S(2)}, u32[]{:S(2)}) collective-permute-start(bf16[40,2560]{1,0:T(8,128)(2,1)S(1)} %get-tuple-element.86), channel_id=1, source_target_pairs={{0,192},{32,224},{64,0},{96,32},{128,64},{160,96},{192,128},{224,1... | collective-permute-start | bytes 614408 | tf_op jit(solution)/shard_map/ppermute | solution.py:29
  21.5 2.3 %shard_map.56 = (f32[4,40,512]{2,1,0:T(8,128)S(1)}, f32[4,40,512]{2,1,0:T(8,128)S(1)}) custom-call(s32[4]{0:T(128)S(1)} %pad_add_fusion.place_ref, bf16[80,2560]{1,0:T(8,128)(2,1)} %dynamic-slice_bitcast_fusion.refs_0_, bf16[80,2560]{1,0:T(8,128)(2,1)S(1)} %collective-permute-done.1.refs_1_, bf16[80,2560]{1,0:T(8,128)(2,1)} %collective-permute-done.2.refs_2_, ...), custom_call_target="tpu_custom_call" | custom-call | flops 838860800 | bytes 5570560 | tf_op jit(solution)/shard_map/pallas_call | solution.py:124
  23.8 2.3 %collective-permute-start.9 = (f32[4,40,512]{2,1,0:T(8,128)S(1)}, f32[4,40,512]{2,1,0:T(8,128)S(1)}, u32[]{:S(2)}, u32[]{:S(2)}) collective-permute-start(f32[4,40,512]{2,1,0:T(8,128)S(1)} %get-tuple-element.52), channel_id=1, source_target_pairs={{0,1},{1,0},{2,3},{3,2},{4,5},{5,4},{6,7},{7,6},{8,9},{9,8},{10,11... | collective-permute-start | bytes 983048 | tf_op jit(solution)/shard_map/ppermute | solution.py:41
  27.9 2.1 %collective-permute-start.13 = (bf16[40,2560]{1,0:T(8,128)(2,1)S(1)}, bf16[40,2560]{1,0:T(8,128)(2,1)S(1)}, u32[]{:S(2)}, u32[]{:S(2)}) collective-permute-start(bf16[40,2560]{1,0:T(8,128)(2,1)S(1)} %get-tuple-element.83), channel_id=1, source_target_pairs={{0,128},{32,160},{64,192},{96,224},{128,0},{160,32},{192,64},{224,... | collective-permute-start | bytes 614408 | tf_op jit(solution)/shard_map/ppermute | solution.py:29
  30.0 1.3 %shard_map.59 = f32[176,512]{1,0:T(8,128)S(1)} custom-call(s32[4]{0:T(128)S(1)} %pad_add_fusion.place_ref, bf16[40,2560]{1,0:T(8,128)(2,1)S(1)} %collective-permute-done.5.refs_0_, bf16[40,2560]{1,0:T(8,128)(2,1)S(1)} %collective-permute-done.6.refs_1_, bf16[40,2560]{1,0:T(8,128)(2,1)S(1)} %collective-permute-done.7.refs_2_, ...), custom_call_target="tpu_custom_call" | custom-call | flops 503316480 | bytes 4096000 | tf_op jit(solution)/shard_map/pallas_call | solution.py:124
  31.4 3.9 %collective-permute-done.10.refs_0_ = bf16[40,2560]{1,0:T(8,128)(2,1)S(1)} collective-permute-done((bf16[40,2560]{1,0:T(8,128)(2,1)S(1)}, bf16[40,2560]{1,0:T(8,128)(2,1)S(1)}, u32[]{:S(2)}, u32[]{:S(2)}) %collective-permute-start.10) | collective-permute-done | bytes 204832 | tf_op jit(solution)/shard_map/ppermute | solution.py:29
  35.3 1.7 %collective-permute-start.21 = (f16[176,512]{1,0:T(8,128)(2,1)S(1)}, f16[176,512]{1,0:T(8,128)(2,1)S(1)}, u32[]{:S(2)}, u32[]{:S(2)}) collective-permute-start(f16[176,512]{1,0:T(8,128)(2,1)S(1)} %convert_element_type.16), channel_id=1, source_target_pairs={{0,1},{1,0},{2,3},{3,2},{4,5},{5,4},{6,7},{7,6},{8,9},{9,8},{10,11... | collective-permute-start | bytes 540680 | tf_op jit(solution)/shard_map/ppermute | solution.py:41
  37.0 1.2 %shard_map.58 = f32[4,40,512]{2,1,0:T(8,128)S(1)} custom-call(s32[4]{0:T(128)S(1)} %pad_add_fusion.place_ref, bf16[40,2560]{1,0:T(8,128)(2,1)S(1)} %collective-permute-done.10.refs_0_, bf16[40,2560]{1,0:T(8,128)(2,1)S(1)} %collective-permute-done.11.refs_1_, bf16[40,2560]{1,0:T(8,128)(2,1)S(1)} %collective-permute-done.12.refs_2_, ...), custom_call_target="tpu_custom_call" | custom-call | flops 503316480 | bytes 4096000 | tf_op jit(solution)/shard_map/pallas_call | solution.py:124
  38.3 3.1 %collective-permute-done.21 = f16[176,512]{1,0:T(8,128)(2,1)S(1)} collective-permute-done((f16[176,512]{1,0:T(8,128)(2,1)S(1)}, f16[176,512]{1,0:T(8,128)(2,1)S(1)}, u32[]{:S(2)}, u32[]{:S(2)}) %collective-permute-start.21) | collective-permute-done | bytes 180256 | tf_op jit(solution)/shard_map/ppermute | solution.py:41
  41.6 1.6 %collective-permute-start.22 = (bf16[120,512]{1,0:T(8,128)(2,1)S(1)}, bf16[120,512]{1,0:T(8,128)(2,1)S(1)}, u32[]{:S(2)}, u32[]{:S(2)}) collective-permute-start(bf16[120,512]{1,0:T(8,128)(2,1)S(1)} %pad_maximum_fusion.1.refs_0_), channel_id=1, source_target_pairs={{0,4},{2,6},{4,8},{6,10},{8,12},{10,14},{12,16},{14,18},{16,20},{1... | collective-permute-start | bytes 368648 | tf_op jit(solution)/shard_map/ppermute | solution.py:33
  43.2 4.0 %collective-permute-start.23 = (bf16[120,512]{1,0:T(8,128)(2,1)S(1)}, bf16[120,512]{1,0:T(8,128)(2,1)S(1)}, u32[]{:S(2)}, u32[]{:S(2)}) collective-permute-start(bf16[120,512]{1,0:T(8,128)(2,1)S(1)} %pad_maximum_fusion.1.refs_0_), channel_id=1, source_target_pairs={{0,28},{2,30},{4,0},{6,2},{8,4},{10,6},{12,8},{14,10},{16,12},{18,... | collective-permute-start | bytes 368648 | tf_op jit(solution)/shard_map/ppermute | solution.py:33
  48.5 2.7 %collective-permute-start.15 = (bf16[120,512]{1,0:T(8,128)(2,1)S(1)}, bf16[120,512]{1,0:T(8,128)(2,1)S(1)}, u32[]{:S(2)}, u32[]{:S(2)}) collective-permute-start(bf16[120,512]{1,0:T(8,128)(2,1)S(1)} %pad_maximum_fusion.refs_0_), channel_id=1, source_target_pairs={{0,28},{2,30},{4,0},{6,2},{8,4},{10,6},{12,8},{14,10},{16,12},{18,... | collective-permute-start | bytes 368648 | tf_op jit(solution)/shard_map/ppermute | solution.py:33
  51.2 2.2 %collective-permute-done.14.refs_1_ = bf16[120,512]{1,0:T(8,128)(2,1)S(1)} collective-permute-done((bf16[120,512]{1,0:T(8,128)(2,1)S(1)}, bf16[120,512]{1,0:T(8,128)(2,1)S(1)}, u32[]{:S(2)}, u32[]{:S(2)}) %collective-permute-start.14) | collective-permute-done | bytes 122912 | tf_op jit(solution)/shard_map/ppermute | solution.py:33
  53.5 2.7 %collective-permute-start.26 = (bf16[120,512]{1,0:T(8,128)(2,1)S(1)}, bf16[120,512]{1,0:T(8,128)(2,1)S(1)}, u32[]{:S(2)}, u32[]{:S(2)}) collective-permute-start(bf16[120,512]{1,0:T(8,128)(2,1)S(1)} %collective-permute-done.23.refs_2_), channel_id=1, source_target_pairs={{0,28},{2,30},{4,0},{6,2},{8,4},{10,6},{12,8},{14,10},{16,12},{18,... | collective-permute-start | bytes 368648 | tf_op jit(solution)/shard_map/ppermute | solution.py:33
  57.0 1.4 %collective-permute-start.17 = (bf16[120,512]{1,0:T(8,128)(2,1)S(1)}, bf16[120,512]{1,0:T(8,128)(2,1)S(1)}, u32[]{:S(2)}, u32[]{:S(2)}) collective-permute-start(bf16[120,512]{1,0:T(8,128)(2,1)S(1)} %collective-permute-done.15.refs_2_), channel_id=1, source_target_pairs={{0,28},{2,30},{4,0},{6,2},{8,4},{10,6},{12,8},{14,10},{16,12},{18,... | collective-permute-start | bytes 368648 | tf_op jit(solution)/shard_map/ppermute | solution.py:33
  58.5 2.6 %collective-permute-done.27.refs_2_ = bf16[2,40,512]{2,1,0:T(8,128)(2,1)S(1)} collective-permute-done((bf16[2,40,512]{2,1,0:T(8,128)(2,1)S(1)}, bf16[2,40,512]{2,1,0:T(8,128)(2,1)S(1)}, u32[]{:S(2)}, u32[]{:S(2)}) %collective-permute-start.27) | collective-permute-done | bytes 81952 | tf_op jit(solution)/shard_map/ppermute | solution.py:29
  61.1 2.7 %collective-permute-start.29 = (bf16[120,512]{1,0:T(8,128)(2,1)S(1)}, bf16[120,512]{1,0:T(8,128)(2,1)S(1)}, u32[]{:S(2)}, u32[]{:S(2)}) collective-permute-start(bf16[120,512]{1,0:T(8,128)(2,1)S(1)} %collective-permute-done.26.refs_4_), channel_id=1, source_target_pairs={{0,28},{2,30},{4,0},{6,2},{8,4},{10,6},{12,8},{14,10},{16,12},{18,... | collective-permute-start | bytes 368648 | tf_op jit(solution)/shard_map/ppermute | solution.py:33
  63.8 2.4 %collective-permute-start.30 = (bf16[2,40,512]{2,1,0:T(8,128)(2,1)S(1)}, bf16[2,40,512]{2,1,0:T(8,128)(2,1)S(1)}, u32[]{:S(2)}, u32[]{:S(2)}) collective-permute-start(bf16[2,40,512]{2,1,0:T(8,128)(2,1)S(1)} %pad_maximum_fusion.4), channel_id=1, source_target_pairs={{0,128},{32,160},{64,192},{96,224},{128,0},{160,32},{192,64},{224,... | collective-permute-start | bytes 245768 | tf_op jit(solution)/shard_map/ppermute | solution.py:29
  66.1 1.5 %collective-permute-start.20 = (bf16[120,512]{1,0:T(8,128)(2,1)S(1)}, bf16[120,512]{1,0:T(8,128)(2,1)S(1)}, u32[]{:S(2)}, u32[]{:S(2)}) collective-permute-start(bf16[120,512]{1,0:T(8,128)(2,1)S(1)} %collective-permute-done.18.refs_5_), channel_id=1, source_target_pairs={{0,4},{2,6},{4,8},{6,10},{8,12},{10,14},{12,16},{14,18},{16,20},{1... | collective-permute-start | bytes 368648 | tf_op jit(solution)/shard_map/ppermute | solution.py:33
  69.2 1.2 %shard_map.60.applied_ref = f32[120,512]{1,0:T(8,128)S(1)} custom-call(s32[4]{0:T(128)S(1)} %pad_add_fusion.place_ref, bf16[120,512]{1,0:T(8,128)(2,1)S(1)} %pad_maximum_fusion.1.refs_0_, bf16[120,512]{1,0:T(8,128)(2,1)S(1)} %collective-permute-done.22.refs_1_, bf16[120,512]{1,0:T(8,128)(2,1)S(1)} %collective-permute-done.23.refs_2_, ...), custom_call_target="tpu_custom_call" | custom-call | flops 440401920 | bytes 4530176 | tf_op jit(solution)/shard_map/pallas_call | solution.py:172
  71.2 1.3 %shard_map.57.first_ref = f32[120,512]{1,0:T(8,128)S(1)} custom-call(s32[4]{0:T(128)S(1)} %pad_add_fusion.place_ref, bf16[120,512]{1,0:T(8,128)(2,1)S(1)} %pad_maximum_fusion.refs_0_, bf16[120,512]{1,0:T(8,128)(2,1)S(1)} %collective-permute-done.14.refs_1_, bf16[120,512]{1,0:T(8,128)(2,1)S(1)} %collective-permute-done.15.refs_2_, ...), custom_call_target="tpu_custom_call" | custom-call | flops 503316480 | bytes 5177344 | tf_op jit(solution)/shard_map/pallas_call | solution.py:172
  74.5 1.7 %collective-permute-start.33 = (f32[1,8]{1,0:T(1,128)S(1)}, f32[1,8]{1,0:T(1,128)S(1)}, u32[]{:S(2)}, u32[]{:S(2)}) collective-permute-start(f32[1,8]{1,0:T(1,128)S(1)} %get-tuple-element.82), channel_id=1, source_target_pairs={{0,224},{32,192},{64,32},{96,0},{128,96},{160,64},{192,160},{224,1... | collective-permute-start | bytes 104 | tf_op jit(solution)/shard_map/ppermute | solution.py:29
  76.4 1.4 %collective-permute-done.33 = f32[1,8]{1,0:T(1,128)S(1)} collective-permute-done((f32[1,8]{1,0:T(1,128)S(1)}, f32[1,8]{1,0:T(1,128)S(1)}, u32[]{:S(2)}, u32[]{:S(2)}) %collective-permute-start.33) | collective-permute-done | bytes 64 | tf_op jit(solution)/shard_map/ppermute | solution.py:29
  77.8 28.9 %all_to_all.6 = f32[32,1,8]{2,1,0:T(1,128)S(1)} all-to-all(f32[32,1,8]{2,1,0:T(1,128)S(1)} %broadcast_in_dim.25), channel_id=1, replica_groups=mesh['occ'=8,'cabs'=16,'aux'=2] {'cabs','aux'}, dimensions={0} | all-to-all | bytes 2048 | tf_op jit(solution)/shard_map/all_to_all | solution.py:313
  (73 shorter events, 15.2 us)
Async XLA Ops:
  0.0 15.5 %collective-permute-start.4 = (bf16[4096,256]{1,0:T(8,128)(2,1)}, bf16[4096,256]{1,0:T(8,128)(2,1)S(1)}, u32[]{:S(2)}, u32[]{:S(2)}) collective-permute-start(bf16[4096,256]{1,0:T(8,128)(2,1)} %own_ref.1), channel_id=1, source_target_pairs={{0,2},{2,0},{4,6},{6,4},{8,10},{10,8},{12,14},{14,12},{16,18},{18,... | collective-permute-start | bytes 6291464 | tf_op jit(solution)/shard_map/ppermute | solution.py:37
  3.2 5.9 %collective-permute-start = (bf16[256,2560]{1,0:T(8,128)(2,1)}, bf16[256,2560]{1,0:T(8,128)(2,1)}, u32[]{:S(2)}, u32[]{:S(2)}) collective-permute-start(bf16[256,2560]{1,0:T(8,128)(2,1)} %bitcast.24), channel_id=1, source_target_pairs={{0,2},{2,0},{4,6},{6,4},{8,10},{10,8},{12,14},{14,12},{16,18},{18,... | collective-permute-start | bytes 3932168 | tf_op jit(solution)/shard_map/ppermute | solution.py:37
  4.1 10.1 %collective-permute-start.1 = (bf16[80,2560]{1,0:T(8,128)(2,1)}, bf16[80,2560]{1,0:T(8,128)(2,1)S(1)}, u32[]{:S(2)}, u32[]{:S(2)}) collective-permute-start(bf16[80,2560]{1,0:T(8,128)(2,1)} %dynamic-slice_bitcast_fusion.refs_0_), channel_id=1, source_target_pairs={{0,32},{32,0},{64,96},{96,64},{128,160},{160,128},{192,224},{224,1... | collective-permute-start | bytes 1228808 | tf_op jit(solution)/shard_map/ppermute | solution.py:29
  4.1 11.4 %collective-permute-start.2 = (bf16[80,2560]{1,0:T(8,128)(2,1)}, bf16[80,2560]{1,0:T(8,128)(2,1)}, u32[]{:S(2)}, u32[]{:S(2)}) collective-permute-start(bf16[80,2560]{1,0:T(8,128)(2,1)} %dynamic-slice_bitcast_fusion.refs_0_), channel_id=1, source_target_pairs={{0,64},{32,96},{64,128},{96,160},{128,192},{160,224},{192,0},{224,... | collective-permute-start | bytes 1228808 | tf_op jit(solution)/shard_map/ppermute | solution.py:29
  5.3 10.2 %collective-permute-start.3 = (bf16[80,2560]{1,0:T(8,128)(2,1)}, bf16[80,2560]{1,0:T(8,128)(2,1)}, u32[]{:S(2)}, u32[]{:S(2)}) collective-permute-start(bf16[80,2560]{1,0:T(8,128)(2,1)} %dynamic-slice_bitcast_fusion.refs_0_), channel_id=1, source_target_pairs={{0,192},{32,224},{64,0},{96,32},{128,64},{160,96},{192,128},{224,1... | collective-permute-start | bytes 1228808 | tf_op jit(solution)/shard_map/ppermute | solution.py:29
  16.5 9.6 %collective-permute-start.5 = (bf16[40,2560]{1,0:T(8,128)(2,1)S(1)}, bf16[40,2560]{1,0:T(8,128)(2,1)S(1)}, u32[]{:S(2)}, u32[]{:S(2)}) collective-permute-start(bf16[40,2560]{1,0:T(8,128)(2,1)S(1)} %get-tuple-element.86), channel_id=1, source_target_pairs={{0,32},{32,0},{64,96},{96,64},{128,160},{160,128},{192,224},{224,1... | collective-permute-start | bytes 614408 | tf_op jit(solution)/shard_map/ppermute | solution.py:29
  17.8 8.6 %collective-permute-start.6 = (bf16[40,2560]{1,0:T(8,128)(2,1)S(1)}, bf16[40,2560]{1,0:T(8,128)(2,1)S(1)}, u32[]{:S(2)}, u32[]{:S(2)}) collective-permute-start(bf16[40,2560]{1,0:T(8,128)(2,1)S(1)} %get-tuple-element.84), channel_id=1, source_target_pairs={{0,64},{32,96},{64,128},{96,160},{128,192},{160,224},{192,0},{224,... | collective-permute-start | bytes 614408 | tf_op jit(solution)/shard_map/ppermute | solution.py:29
  18.2 9.3 %collective-permute-start.7 = (bf16[40,2560]{1,0:T(8,128)(2,1)S(1)}, bf16[40,2560]{1,0:T(8,128)(2,1)S(1)}, u32[]{:S(2)}, u32[]{:S(2)}) collective-permute-start(bf16[40,2560]{1,0:T(8,128)(2,1)S(1)} %get-tuple-element.86), channel_id=1, source_target_pairs={{0,192},{32,224},{64,0},{96,32},{128,64},{160,96},{192,128},{224,1... | collective-permute-start | bytes 614408 | tf_op jit(solution)/shard_map/ppermute | solution.py:29
  20.6 7.3 %collective-permute-start.8 = (bf16[40,2560]{1,0:T(8,128)(2,1)S(1)}, bf16[40,2560]{1,0:T(8,128)(2,1)S(1)}, u32[]{:S(2)}, u32[]{:S(2)}) collective-permute-start(bf16[40,2560]{1,0:T(8,128)(2,1)S(1)} %get-tuple-element.84), channel_id=1, source_target_pairs={{0,128},{32,160},{64,192},{96,224},{128,0},{160,32},{192,64},{224,... | collective-permute-start | bytes 614408 | tf_op jit(solution)/shard_map/ppermute | solution.py:29
  23.8 13.2 %collective-permute-start.9 = (f32[4,40,512]{2,1,0:T(8,128)S(1)}, f32[4,40,512]{2,1,0:T(8,128)S(1)}, u32[]{:S(2)}, u32[]{:S(2)}) collective-permute-start(f32[4,40,512]{2,1,0:T(8,128)S(1)} %get-tuple-element.52), channel_id=1, source_target_pairs={{0,1},{1,0},{2,3},{3,2},{4,5},{5,4},{6,7},{7,6},{8,9},{9,8},{10,11... | collective-permute-start | bytes 983048 | tf_op jit(solution)/shard_map/ppermute | solution.py:41
  26.1 9.2 %collective-permute-start.10 = (bf16[40,2560]{1,0:T(8,128)(2,1)S(1)}, bf16[40,2560]{1,0:T(8,128)(2,1)S(1)}, u32[]{:S(2)}, u32[]{:S(2)}) collective-permute-start(bf16[40,2560]{1,0:T(8,128)(2,1)S(1)} %get-tuple-element.85), channel_id=1, source_target_pairs={{0,32},{32,0},{64,96},{96,64},{128,160},{160,128},{192,224},{224,1... | collective-permute-start | bytes 614408 | tf_op jit(solution)/shard_map/ppermute | solution.py:29
  26.4 10.6 %collective-permute-start.12 = (bf16[40,2560]{1,0:T(8,128)(2,1)S(1)}, bf16[40,2560]{1,0:T(8,128)(2,1)S(1)}, u32[]{:S(2)}, u32[]{:S(2)}) collective-permute-start(bf16[40,2560]{1,0:T(8,128)(2,1)S(1)} %get-tuple-element.85), channel_id=1, source_target_pairs={{0,192},{32,224},{64,0},{96,32},{128,64},{160,96},{192,128},{224,1... | collective-permute-start | bytes 614408 | tf_op jit(solution)/shard_map/ppermute | solution.py:29
  27.5 9.5 %collective-permute-start.11 = (bf16[40,2560]{1,0:T(8,128)(2,1)S(1)}, bf16[40,2560]{1,0:T(8,128)(2,1)S(1)}, u32[]{:S(2)}, u32[]{:S(2)}) collective-permute-start(bf16[40,2560]{1,0:T(8,128)(2,1)S(1)} %get-tuple-element.83), channel_id=1, source_target_pairs={{0,64},{32,96},{64,128},{96,160},{128,192},{160,224},{192,0},{224,... | collective-permute-start | bytes 614408 | tf_op jit(solution)/shard_map/ppermute | solution.py:29
  27.9 9.1 %collective-permute-start.13 = (bf16[40,2560]{1,0:T(8,128)(2,1)S(1)}, bf16[40,2560]{1,0:T(8,128)(2,1)S(1)}, u32[]{:S(2)}, u32[]{:S(2)}) collective-permute-start(bf16[40,2560]{1,0:T(8,128)(2,1)S(1)} %get-tuple-element.83), channel_id=1, source_target_pairs={{0,128},{32,160},{64,192},{96,224},{128,0},{160,32},{192,64},{224,... | collective-permute-start | bytes 614408 | tf_op jit(solution)/shard_map/ppermute | solution.py:29
  35.3 6.2 %collective-permute-start.21 = (f16[176,512]{1,0:T(8,128)(2,1)S(1)}, f16[176,512]{1,0:T(8,128)(2,1)S(1)}, u32[]{:S(2)}, u32[]{:S(2)}) collective-permute-start(f16[176,512]{1,0:T(8,128)(2,1)S(1)} %convert_element_type.16), channel_id=1, source_target_pairs={{0,1},{1,0},{2,3},{3,2},{4,5},{5,4},{6,7},{7,6},{8,9},{9,8},{10,11... | collective-permute-start | bytes 540680 | tf_op jit(solution)/shard_map/ppermute | solution.py:41
  41.6 9.5 %collective-permute-start.22 = (bf16[120,512]{1,0:T(8,128)(2,1)S(1)}, bf16[120,512]{1,0:T(8,128)(2,1)S(1)}, u32[]{:S(2)}, u32[]{:S(2)}) collective-permute-start(bf16[120,512]{1,0:T(8,128)(2,1)S(1)} %pad_maximum_fusion.1.refs_0_), channel_id=1, source_target_pairs={{0,4},{2,6},{4,8},{6,10},{8,12},{10,14},{12,16},{14,18},{16,20},{1... | collective-permute-start | bytes 368648 | tf_op jit(solution)/shard_map/ppermute | solution.py:33
  43.2 8.0 %collective-permute-start.23 = (bf16[120,512]{1,0:T(8,128)(2,1)S(1)}, bf16[120,512]{1,0:T(8,128)(2,1)S(1)}, u32[]{:S(2)}, u32[]{:S(2)}) collective-permute-start(bf16[120,512]{1,0:T(8,128)(2,1)S(1)} %pad_maximum_fusion.1.refs_0_), channel_id=1, source_target_pairs={{0,28},{2,30},{4,0},{6,2},{8,4},{10,6},{12,8},{14,10},{16,12},{18,... | collective-permute-start | bytes 368648 | tf_op jit(solution)/shard_map/ppermute | solution.py:33
  47.2 3.9 %collective-permute-start.24 = (bf16[3,40,512]{2,1,0:T(8,128)(2,1)S(1)}, bf16[3,40,512]{2,1,0:T(8,128)(2,1)S(1)}, u32[]{:S(2)}, u32[]{:S(2)}) collective-permute-start(bf16[3,40,512]{2,1,0:T(8,128)(2,1)S(1)} %pad_maximum_fusion.2), channel_id=1, source_target_pairs={{0,32},{32,0},{64,96},{96,64},{128,160},{160,128},{192,224},{224,1... | collective-permute-start | bytes 368648 | tf_op jit(solution)/shard_map/ppermute | solution.py:29
  48.4 5.0 %collective-permute-start.14 = (bf16[120,512]{1,0:T(8,128)(2,1)S(1)}, bf16[120,512]{1,0:T(8,128)(2,1)S(1)}, u32[]{:S(2)}, u32[]{:S(2)}) collective-permute-start(bf16[120,512]{1,0:T(8,128)(2,1)S(1)} %pad_maximum_fusion.refs_0_), channel_id=1, source_target_pairs={{0,4},{2,6},{4,8},{6,10},{8,12},{10,14},{12,16},{14,18},{16,20},{1... | collective-permute-start | bytes 368648 | tf_op jit(solution)/shard_map/ppermute | solution.py:33
  48.5 8.5 %collective-permute-start.15 = (bf16[120,512]{1,0:T(8,128)(2,1)S(1)}, bf16[120,512]{1,0:T(8,128)(2,1)S(1)}, u32[]{:S(2)}, u32[]{:S(2)}) collective-permute-start(bf16[120,512]{1,0:T(8,128)(2,1)S(1)} %pad_maximum_fusion.refs_0_), channel_id=1, source_target_pairs={{0,28},{2,30},{4,0},{6,2},{8,4},{10,6},{12,8},{14,10},{16,12},{18,... | collective-permute-start | bytes 368648 | tf_op jit(solution)/shard_map/ppermute | solution.py:33
  53.4 5.0 %collective-permute-start.16 = (bf16[120,512]{1,0:T(8,128)(2,1)S(1)}, bf16[120,512]{1,0:T(8,128)(2,1)S(1)}, u32[]{:S(2)}, u32[]{:S(2)}) collective-permute-start(bf16[120,512]{1,0:T(8,128)(2,1)S(1)} %collective-permute-done.14.refs_1_), channel_id=1, source_target_pairs={{0,4},{2,6},{4,8},{6,10},{8,12},{10,14},{12,16},{14,18},{16,20},{1... | collective-permute-start | bytes 368648 | tf_op jit(solution)/shard_map/ppermute | solution.py:33
  53.4 7.6 %collective-permute-start.25 = (bf16[120,512]{1,0:T(8,128)(2,1)S(1)}, bf16[120,512]{1,0:T(8,128)(2,1)S(1)}, u32[]{:S(2)}, u32[]{:S(2)}) collective-permute-start(bf16[120,512]{1,0:T(8,128)(2,1)S(1)} %collective-permute-done.22.refs_1_), channel_id=1, source_target_pairs={{0,4},{2,6},{4,8},{6,10},{8,12},{10,14},{12,16},{14,18},{16,20},{1... | collective-permute-start | bytes 368648 | tf_op jit(solution)/shard_map/ppermute | solution.py:33
  53.5 7.6 %collective-permute-start.26 = (bf16[120,512]{1,0:T(8,128)(2,1)S(1)}, bf16[120,512]{1,0:T(8,128)(2,1)S(1)}, u32[]{:S(2)}, u32[]{:S(2)}) collective-permute-start(bf16[120,512]{1,0:T(8,128)(2,1)S(1)} %collective-permute-done.23.refs_2_), channel_id=1, source_target_pairs={{0,28},{2,30},{4,0},{6,2},{8,4},{10,6},{12,8},{14,10},{16,12},{18,... | collective-permute-start | bytes 368648 | tf_op jit(solution)/shard_map/ppermute | solution.py:33
  56.3 4.8 %collective-permute-start.27 = (bf16[2,40,512]{2,1,0:T(8,128)(2,1)S(1)}, bf16[2,40,512]{2,1,0:T(8,128)(2,1)S(1)}, u32[]{:S(2)}, u32[]{:S(2)}) collective-permute-start(bf16[2,40,512]{2,1,0:T(8,128)(2,1)S(1)} %pad_maximum_fusion.3), channel_id=1, source_target_pairs={{0,64},{32,96},{64,128},{96,160},{128,192},{160,224},{192,0},{224,... | collective-permute-start | bytes 245768 | tf_op jit(solution)/shard_map/ppermute | solution.py:29
  57.0 9.1 %collective-permute-start.17 = (bf16[120,512]{1,0:T(8,128)(2,1)S(1)}, bf16[120,512]{1,0:T(8,128)(2,1)S(1)}, u32[]{:S(2)}, u32[]{:S(2)}) collective-permute-start(bf16[120,512]{1,0:T(8,128)(2,1)S(1)} %collective-permute-done.15.refs_2_), channel_id=1, source_target_pairs={{0,28},{2,30},{4,0},{6,2},{8,4},{10,6},{12,8},{14,10},{16,12},{18,... | collective-permute-start | bytes 368648 | tf_op jit(solution)/shard_map/ppermute | solution.py:33
  58.4 7.7 %collective-permute-start.18 = (bf16[120,512]{1,0:T(8,128)(2,1)S(1)}, bf16[120,512]{1,0:T(8,128)(2,1)S(1)}, u32[]{:S(2)}, u32[]{:S(2)}) collective-permute-start(bf16[120,512]{1,0:T(8,128)(2,1)S(1)} %collective-permute-done.16.refs_3_), channel_id=1, source_target_pairs={{0,4},{2,6},{4,8},{6,10},{8,12},{10,14},{12,16},{14,18},{16,20},{1... | collective-permute-start | bytes 368648 | tf_op jit(solution)/shard_map/ppermute | solution.py:33
  61.1 7.5 %collective-permute-start.28 = (bf16[120,512]{1,0:T(8,128)(2,1)S(1)}, bf16[120,512]{1,0:T(8,128)(2,1)S(1)}, u32[]{:S(2)}, u32[]{:S(2)}) collective-permute-start(bf16[120,512]{1,0:T(8,128)(2,1)S(1)} %collective-permute-done.25.refs_3_), channel_id=1, source_target_pairs={{0,4},{2,6},{4,8},{6,10},{8,12},{10,14},{12,16},{14,18},{16,20},{1... | collective-permute-start | bytes 368648 | tf_op jit(solution)/shard_map/ppermute | solution.py:33
  61.1 7.5 %collective-permute-start.29 = (bf16[120,512]{1,0:T(8,128)(2,1)S(1)}, bf16[120,512]{1,0:T(8,128)(2,1)S(1)}, u32[]{:S(2)}, u32[]{:S(2)}) collective-permute-start(bf16[120,512]{1,0:T(8,128)(2,1)S(1)} %collective-permute-done.26.refs_4_), channel_id=1, source_target_pairs={{0,28},{2,30},{4,0},{6,2},{8,4},{10,6},{12,8},{14,10},{16,12},{18,... | collective-permute-start | bytes 368648 | tf_op jit(solution)/shard_map/ppermute | solution.py:33
  63.8 4.8 %collective-permute-start.30 = (bf16[2,40,512]{2,1,0:T(8,128)(2,1)S(1)}, bf16[2,40,512]{2,1,0:T(8,128)(2,1)S(1)}, u32[]{:S(2)}, u32[]{:S(2)}) collective-permute-start(bf16[2,40,512]{2,1,0:T(8,128)(2,1)S(1)} %pad_maximum_fusion.4), channel_id=1, source_target_pairs={{0,128},{32,160},{64,192},{96,224},{128,0},{160,32},{192,64},{224,... | collective-permute-start | bytes 245768 | tf_op jit(solution)/shard_map/ppermute | solution.py:29
  66.1 5.0 %collective-permute-start.19 = (bf16[120,512]{1,0:T(8,128)(2,1)S(1)}, bf16[120,512]{1,0:T(8,128)(2,1)S(1)}, u32[]{:S(2)}, u32[]{:S(2)}) collective-permute-start(bf16[120,512]{1,0:T(8,128)(2,1)S(1)} %collective-permute-done.17.refs_4_), channel_id=1, source_target_pairs={{0,28},{2,30},{4,0},{6,2},{8,4},{10,6},{12,8},{14,10},{16,12},{18,... | collective-permute-start | bytes 368648 | tf_op jit(solution)/shard_map/ppermute | solution.py:33
  66.1 5.0 %collective-permute-start.20 = (bf16[120,512]{1,0:T(8,128)(2,1)S(1)}, bf16[120,512]{1,0:T(8,128)(2,1)S(1)}, u32[]{:S(2)}, u32[]{:S(2)}) collective-permute-start(bf16[120,512]{1,0:T(8,128)(2,1)S(1)} %collective-permute-done.18.refs_5_), channel_id=1, source_target_pairs={{0,4},{2,6},{4,8},{6,10},{8,12},{10,14},{12,16},{14,18},{16,20},{1... | collective-permute-start | bytes 368648 | tf_op jit(solution)/shard_map/ppermute | solution.py:33
  68.6 4.2 %collective-permute-start.31 = (bf16[120,512]{1,0:T(8,128)(2,1)S(1)}, bf16[120,512]{1,0:T(8,128)(2,1)S(1)}, u32[]{:S(2)}, u32[]{:S(2)}) collective-permute-start(bf16[120,512]{1,0:T(8,128)(2,1)S(1)} %collective-permute-done.29.refs_6_), channel_id=1, source_target_pairs={{0,28},{2,30},{4,0},{6,2},{8,4},{10,6},{12,8},{14,10},{16,12},{18,... | collective-permute-start | bytes 368648 | tf_op jit(solution)/shard_map/ppermute | solution.py:33
  (6 other events, 42.2 us)

commit v4 on v3

--- a/solution.py
+++ b/solution.py
@@ -18,7 +18,8 @@
 PARAMS = pltpu.CompilerParams(vmem_limit_bytes=8 * 2**20)
 
 PLACES = ((0, 0), (0, 1), (-1, 0), (1, 0), (1, 1), (-1, 1), (2, 0), (2, 1))
-LEFTS = ((0, 0), (0, 1), (-1, 0), (-1, 1), (2, 0), (2, 1))
+FIRST = ((0, 1), (-1, 0), (-1, 1))
+SECOND = ((0, 0), (2, 0), (2, 1))
 
 
 def partner(me, dy, flip):
@@ -183,49 +184,58 @@
     )(place, *blocks, fock, fock_other)
 
 
-def apply_last(place, first_rows, applied, block, fock, fock_other, rights):
-    rows, columns = applied.shape
+def contract(place, applied, placed, fock, fock_other, rights, pairs, mirrored):
+    offsets, blocks = zip(*placed)
+    rows, columns = blocks[0].shape
     width = columns // 2
-
-    def body(place_ref, first_ref, applied_ref, block_ref, own_ref, other_ref, *refs):
-        right_refs, (row_ref, a_ref, pa_ref, sum_ref) = refs[:-4], refs[-4:]
-        own, other = apply_tile(place_ref, Z // 2, block_ref[...], own_ref, other_ref)
-        sum_ref[:, :width] = applied_ref[:, :width] + own
-        sum_ref[:, width:] = applied_ref[:, width:] + other
+    count = len(blocks)
+    known = [] if applied is None else [applied]
+
+    def body(place_ref, *refs):
+        block_refs, (own_ref, other_ref) = refs[:count], refs[count : count + 2]
+        known_refs = refs[count + 2 : count + 2 + len(known)]
+        right_refs = refs[count + 2 + len(known) : count + 2 + len(known) + len(rights)]
+        outs, sum_ref = refs[count + 2 + len(known) + len(rights) : -1], refs[-1]
+        for index in range(count):
+            own, other = apply_tile(
+                place_ref, offsets[index], block_refs[index][...], own_ref, other_ref
+            )
+            if index == 0 and known:
+                own += known_refs[0][:, :width]
+                other += known_refs[0][:, width:]
+            elif index > 0:
+                own += sum_ref[:, :width]
+                other += sum_ref[:, width:]
+            sum_ref[:, :width] = own
+            sum_ref[:, width:] = other
         pieces = [ref[index] for ref in right_refs for index in range(ref.shape[0])]
-        lefts = [
-            ref[start : start + KEPT, :]
-            for ref in (first_ref, sum_ref)
-            for start in range(0, ref.shape[0], KEPT)
-        ]
         sums = []
-        for left, piece in zip(lefts, pieces):
-            product = left * piece.astype(F32)
+        for index, piece in enumerate(pieces):
+            product = sum_ref[index * KEPT : (index + 1) * KEPT, :] * piece.astype(F32)
             sums.append(jnp.sum(jnp.sum(product, axis=0, keepdims=True), axis=1, keepdims=True))
         me = place_ref[0]
         lanes = lax.broadcasted_iota(jnp.int32, (1, OCC), 1)
         row = jnp.zeros((1, OCC), F32)
-        for value, (dy, flip) in zip(sums, LEFTS):
+        for value, (dy, flip) in zip(sums, pairs):
             row += jnp.where(lanes == partner(me, dy, flip), value, 0.0)
-        row_ref[...] = row
-        here = lanes == me
-        a_ref[...] = jnp.where(here, sums[2], 0.0)
-        pa_ref[...] = jnp.where(here, sums[3], 0.0)
-
-    shape = jax.ShapeDtypeStruct((1, OCC), F32)
+        outs[0][...] = row
+        for out, index in zip(outs[1:], mirrored):
+            out[...] = jnp.where(lanes == me, sums[index], 0.0)
+
+    shapes = (jax.ShapeDtypeStruct((1, OCC), F32),) * (1 + len(mirrored))
     return pl.pallas_call(
         body,
-        out_shape=(shape,) * 3,
-        in_specs=[SMEM] + [VMEM] * (len(rights) + 5),
-        out_specs=(VMEM,) * 3,
+        out_shape=shapes,
+        in_specs=[SMEM] + [VMEM] * (count + 2 + len(known) + len(rights)),
+        out_specs=(VMEM,) * len(shapes),
         scratch_shapes=[pltpu.VMEM((rows, columns), F32)],
         compiler_params=PARAMS,
         cost_estimate=pl.CostEstimate(
-            flops=2 * rows * columns * columns,
-            bytes_accessed=2 * columns * (rows + columns) + 6 * rows * columns,
+            flops=2 * count * rows * columns * columns,
+            bytes_accessed=2 * count * columns * (rows + columns) + 6 * rows * columns,
             transcendentals=0,
         ),
-    )(place, first_rows, applied, block, fock, fock_other, *rights)
+    )(place, *blocks, fock, fock_other, *known, *rights)
 
 
 def shards(occ_fit, cabs_fit, fock, cabs_block, pair_block):
@@ -278,8 +288,8 @@
     got = (got[:-FOOT].astype(F32) * unscale).reshape(keep.shape)
     far = masked(keep, got, 4)
 
-    first = jnp.concatenate([near[0], near[1], near[2]], 0)
-    second = jnp.concatenate([far[1], far[2], far[3]], 0)
+    first = jnp.concatenate([near[1], near[2], far[1]], 0)
+    second = jnp.concatenate([near[0], far[2], far[3]], 0)
     first_blocks, second_blocks = [(0, first)], [(0, second)]
 
     def ring_step(step, up, down, blocks):
@@ -292,23 +302,26 @@
     up_a = down_a = first
     up_b = down_b = second
     for step in range(1, Z // 2):
+        up_a, down_a, value = lax.optimization_barrier((up_a, down_a, rights[-1]))
         up_a, down_a = ring_step(step, up_a, down_a, first_blocks)
-        up_b, down_b, value = lax.optimization_barrier((up_b, down_b, rights[-1]))
+        value = occ_hop(value, *moves[step - 1])
+        up_a, down_a, value = lax.optimization_barrier((up_a, down_a, value))
         up_b, down_b = ring_step(step, up_b, down_b, second_blocks)
-        value = occ_hop(value, *moves[step - 1])
-        up_b, down_b, value = lax.optimization_barrier((up_b, down_b, value))
         rights[-1] = value
         if step == 1:
             rights.append(jnp.stack([near[3], value[1]]))
         elif step == 2:
             rights.append(jnp.stack([far[2], rights[0][2]]))
     first_blocks.append((Z // 2, z_hop(up_a, 1)))
-    block = z_hop(down_b, -1)
-    first = apply_blocks(place, first_blocks, fock, fock_other)
+    last_block = [(Z // 2, z_hop(down_b, -1))]
+    row, to_a, to_pa = contract(
+        place, None, first_blocks, fock, fock_other, [rights[0][:1], rights[1]], FIRST, (1, 2)
+    )
     second = apply_blocks(place, second_blocks, fock, fock_other)
-    rights = [near[:1], rights[0][:1], *rights[1:]]
-    row, to_a, to_pa = apply_last(place, first, second, block, fock, fock_other, rights)
-    row += occ_hop(to_a, -1, 0) + occ_hop(to_pa, -1, 1)
+    (rest,) = contract(
+        place, second, last_block, fock, fock_other, [near[:1], rights[2]], SECOND, ()
+    )
+    row += rest + occ_hop(to_a, -1, 0) + occ_hop(to_pa, -1, 1)
     peers = 4 * Z
     spread = lax.all_to_all(
         jnp.broadcast_to(row, (peers, OCC)), ("cabs", "aux"), 0, 0, tiled=True

time: 108 us -> 106 us (0.981)
  waiting for transfers between devices: 19.4 us -> 17.6 us
  starting transfers between devices: 42.9 us -> 44.1 us
    ppermute x14, waiting for transfers between devices: 3.37 us -> 1.05 us  [z_hop(): lax.ppermute(value, 'cabs', [(c, (c // 2 + dz) % Z * 2 + c % 2) for c in...]
    ppermute x14, starting transfers between devices: 17.4 us -> 18.9 us  [z_hop(): lax.ppermute(value, 'cabs', [(c, (c // 2 + dz) % Z * 2 + c % 2) for c in...]
    pallas_call x1 -> x2, Pallas kernels: 0.88 us -> 2.22 us  [contract(): pl.pallas_call(body, out_shape=shapes, in_specs=[SMEM] + [VMEM] * (count...]
    pallas_call x2 -> x1, Pallas kernels: 2.45 us -> 1.19 us  [apply_blocks(): pl.pallas_call(body, out_shape=jax.ShapeDtypeStruct((rows, columns), F32)...]
  transfers between devices with their start and end apart: 34 -> 34, of which waited for: 13 -> 11; matrix products, arithmetic and copies ran while one was open for 2% -> 2% of each run, Pallas kernels for 9% -> 10%
where the time goes in v4:
time: 106 us
  starting transfers between devices  44.1 us (42%)
  blocking collectives  27.9 us (26%)
  waiting for transfers between devices  17.6 us (17%)
  Pallas kernels  10.3 us (10%)
  local copies, waits for them, and re-layouts  4.68 us (4%)
    all_to_all x1, blocking collectives, shards(): lax.all_to_all(jnp.broadcast_to(row, (peers, OCC)), ('cabs', 'aux'), 0, 0...  27.9 us
    ppermute x14, starting transfers between devices, z_hop(): lax.ppermute(value, 'cabs', [(c, (c // 2 + dz) % Z * 2 + c % 2) for c in...  18.9 us
    ppermute x16, starting transfers between devices, occ_hop(): lax.ppermute(value, 'occ', [(o, partner(o, dy, flip)) for o in range(OCC)])  17.9 us
    ppermute x16, waiting for transfers between devices, occ_hop(): lax.ppermute(value, 'occ', [(o, partner(o, dy, flip)) for o in range(OCC)])  11.9 us
    pallas_call x3, Pallas kernels, fit_sums(): pl.pallas_call(body, out_shape=shapes, in_specs=[SMEM] + [VMEM] * (count...  4.88 us
    ppermute x2, starting transfers between devices, aux_swap(): return lax.ppermute(value, 'aux', [(0, 1), (1, 0)])  4.05 us
    ppermute x2, starting transfers between devices, core_swap(): return lax.ppermute(value, 'cabs', [(c, c ^ 1) for c in range(2 * Z)])  3.24 us
    ppermute x2, waiting for transfers between devices, aux_swap(): return lax.ppermute(value, 'aux', [(0, 1), (1, 0)])  3.09 us
  transfers between devices with their start and end apart: 34, of which 11 were waited for; matrix products, arithmetic and copies ran while one was open for 2% of the time, Pallas kernels for 10%

profile of v4, /device:TPU:1, one launch (start us, length us, event | category | flops | bytes accessed | tf_op | source)
XLA Modules:
  0.0 105.8 jit_solution(1115642094689056721)
XLA Ops:
  0.0 3.2 %collective-permute-start.4 = (bf16[4096,256]{1,0:T(8,128)(2,1)}, bf16[4096,256]{1,0:T(8,128)(2,1)S(1)}, u32[]{:S(2)}, u32[]{:S(2)}) collective-permute-start(bf16[4096,256]{1,0:T(8,128)(2,1)} %refs_1_.1), channel_id=1, source_target_pairs={{0,2},{2,0},{4,6},{6,4},{8,10},{10,8},{12,14},{14,12},{16,18},{18,... | collective-permute-start | bytes 6291464 | tf_op jit(solution)/shard_map/ppermute | solution.py:38
  4.1 1.2 %collective-permute-start.2 = (bf16[80,2560]{1,0:T(8,128)(2,1)}, bf16[80,2560]{1,0:T(8,128)(2,1)}, u32[]{:S(2)}, u32[]{:S(2)}) collective-permute-start(bf16[80,2560]{1,0:T(8,128)(2,1)} %dynamic-slice_bitcast_fusion.refs_0_), channel_id=1, source_target_pairs={{0,64},{32,96},{64,128},{96,160},{128,192},{160,224},{192,0},{224,... | collective-permute-start | bytes 1228808 | tf_op jit(solution)/shard_map/ppermute | solution.py:30
  5.3 1.4 %collective-permute-start.3 = (bf16[80,2560]{1,0:T(8,128)(2,1)}, bf16[80,2560]{1,0:T(8,128)(2,1)}, u32[]{:S(2)}, u32[]{:S(2)}) collective-permute-start(bf16[80,2560]{1,0:T(8,128)(2,1)} %dynamic-slice_bitcast_fusion.refs_0_), channel_id=1, source_target_pairs={{0,192},{32,224},{64,0},{96,32},{128,64},{160,96},{192,128},{224,1... | collective-permute-start | bytes 1228808 | tf_op jit(solution)/shard_map/ppermute | solution.py:30
  7.5 1.6 %collective-permute-done.other_ref = bf16[256,2560]{1,0:T(8,128)(2,1)} collective-permute-done((bf16[256,2560]{1,0:T(8,128)(2,1)}, bf16[256,2560]{1,0:T(8,128)(2,1)}, u32[]{:S(2)}, u32[]{:S(2)}) %collective-permute-start) | collective-permute-done | bytes 1310752 | tf_op jit(solution)/shard_map/ppermute | solution.py:38
  9.1 1.3 %copy-done.2 = bf16[1,256,2560]{2,1,0:T(8,128)(2,1)S(1)} copy-done((bf16[1,256,2560]{2,1,0:T(8,128)(2,1)S(1)}, bf16[1,256,2560]{2,1,0:T(8,128)(2,1)}, u32[]{:S(2)}) %copy-start.2) | copy-done | bytes 1310744
  11.1 2.0 %shard_map.55 = (bf16[2560,512]{1,0:T(8,128)(2,1)S(1)}, s32[8,512]{1,0:T(8,128)S(1)}) custom-call(s32[4]{0:T(128)S(1)} %pad_add_fusion.place_ref, s32[8]{0:T(128)S(1)} %copy-done.3, s32[8,512]{1,0:T(8,128)S(1)} %reshape.17.rows_ref, bf16[256,2560]{1,0:T(8,128)(2,1)S(1)} %bitcast.25, bf16[256,2560]{1,0:T(8,128)(2,1)} %collective-permute-done.other_ref), custom_call_target="tpu_custom_call" | custom-call | bytes 5242880 | tf_op jit(solution)/shard_map/pallas_call | solution.py:70
  14.2 1.3 %collective-permute-done.2.refs_2_ = bf16[80,2560]{1,0:T(8,128)(2,1)} collective-permute-done((bf16[80,2560]{1,0:T(8,128)(2,1)}, bf16[80,2560]{1,0:T(8,128)(2,1)}, u32[]{:S(2)}, u32[]{:S(2)}) %collective-permute-start.2) | collective-permute-done | bytes 409632 | tf_op jit(solution)/shard_map/ppermute | solution.py:30
  16.5 1.2 %collective-permute-start.5 = (bf16[40,2560]{1,0:T(8,128)(2,1)S(1)}, bf16[40,2560]{1,0:T(8,128)(2,1)S(1)}, u32[]{:S(2)}, u32[]{:S(2)}) collective-permute-start(bf16[40,2560]{1,0:T(8,128)(2,1)S(1)} %get-tuple-element.85), channel_id=1, source_target_pairs={{0,32},{32,0},{64,96},{96,64},{128,160},{160,128},{192,224},{224,1... | collective-permute-start | bytes 614408 | tf_op jit(solution)/shard_map/ppermute | solution.py:30
  18.2 2.4 %collective-permute-start.7 = (bf16[40,2560]{1,0:T(8,128)(2,1)S(1)}, bf16[40,2560]{1,0:T(8,128)(2,1)S(1)}, u32[]{:S(2)}, u32[]{:S(2)}) collective-permute-start(bf16[40,2560]{1,0:T(8,128)(2,1)S(1)} %get-tuple-element.85), channel_id=1, source_target_pairs={{0,192},{32,224},{64,0},{96,32},{128,64},{160,96},{192,128},{224,1... | collective-permute-start | bytes 614408 | tf_op jit(solution)/shard_map/ppermute | solution.py:30
  21.5 2.3 %shard_map.56 = (f32[4,40,512]{2,1,0:T(8,128)S(1)}, f32[4,40,512]{2,1,0:T(8,128)S(1)}) custom-call(s32[4]{0:T(128)S(1)} %pad_add_fusion.place_ref, bf16[80,2560]{1,0:T(8,128)(2,1)} %dynamic-slice_bitcast_fusion.refs_0_, bf16[80,2560]{1,0:T(8,128)(2,1)S(1)} %collective-permute-done.1.refs_1_, bf16[80,2560]{1,0:T(8,128)(2,1)} %collective-permute-done.2.refs_2_, ...), custom_call_target="tpu_custom_call" | custom-call | flops 838860800 | bytes 5570560 | tf_op jit(solution)/shard_map/pallas_call | solution.py:125
  23.8 2.3 %collective-permute-start.9 = (f32[4,40,512]{2,1,0:T(8,128)S(1)}, f32[4,40,512]{2,1,0:T(8,128)S(1)}, u32[]{:S(2)}, u32[]{:S(2)}) collective-permute-start(f32[4,40,512]{2,1,0:T(8,128)S(1)} %get-tuple-element.52), channel_id=1, source_target_pairs={{0,1},{1,0},{2,3},{3,2},{4,5},{5,4},{6,7},{7,6},{8,9},{9,8},{10,11... | collective-permute-start | bytes 983048 | tf_op jit(solution)/shard_map/ppermute | solution.py:42
  27.9 2.1 %collective-permute-start.13 = (bf16[40,2560]{1,0:T(8,128)(2,1)S(1)}, bf16[40,2560]{1,0:T(8,128)(2,1)S(1)}, u32[]{:S(2)}, u32[]{:S(2)}) collective-permute-start(bf16[40,2560]{1,0:T(8,128)(2,1)S(1)} %get-tuple-element.84), channel_id=1, source_target_pairs={{0,128},{32,160},{64,192},{96,224},{128,0},{160,32},{192,64},{224,... | collective-permute-start | bytes 614408 | tf_op jit(solution)/shard_map/ppermute | solution.py:30
  30.0 1.3 %shard_map.58 = f32[176,512]{1,0:T(8,128)S(1)} custom-call(s32[4]{0:T(128)S(1)} %pad_add_fusion.place_ref, bf16[40,2560]{1,0:T(8,128)(2,1)S(1)} %collective-permute-done.5.refs_0_, bf16[40,2560]{1,0:T(8,128)(2,1)S(1)} %collective-permute-done.6.refs_1_, bf16[40,2560]{1,0:T(8,128)(2,1)S(1)} %collective-permute-done.7.refs_2_, ...), custom_call_target="tpu_custom_call" | custom-call | flops 503316480 | bytes 4096000 | tf_op jit(solution)/shard_map/pallas_call | solution.py:125
  31.4 3.9 %collective-permute-done.10.refs_0_ = bf16[40,2560]{1,0:T(8,128)(2,1)S(1)} collective-permute-done((bf16[40,2560]{1,0:T(8,128)(2,1)S(1)}, bf16[40,2560]{1,0:T(8,128)(2,1)S(1)}, u32[]{:S(2)}, u32[]{:S(2)}) %collective-permute-start.10) | collective-permute-done | bytes 204832 | tf_op jit(solution)/shard_map/ppermute | solution.py:30
  35.3 1.7 %collective-permute-start.14 = (f16[176,512]{1,0:T(8,128)(2,1)S(1)}, f16[176,512]{1,0:T(8,128)(2,1)S(1)}, u32[]{:S(2)}, u32[]{:S(2)}) collective-permute-start(f16[176,512]{1,0:T(8,128)(2,1)S(1)} %convert_element_type.16), channel_id=1, source_target_pairs={{0,1},{1,0},{2,3},{3,2},{4,5},{5,4},{6,7},{7,6},{8,9},{9,8},{10,11... | collective-permute-start | bytes 540680 | tf_op jit(solution)/shard_map/ppermute | solution.py:42
  37.0 1.2 %shard_map.57 = f32[4,40,512]{2,1,0:T(8,128)S(1)} custom-call(s32[4]{0:T(128)S(1)} %pad_add_fusion.place_ref, bf16[40,2560]{1,0:T(8,128)(2,1)S(1)} %collective-permute-done.10.refs_0_, bf16[40,2560]{1,0:T(8,128)(2,1)S(1)} %collective-permute-done.11.refs_1_, bf16[40,2560]{1,0:T(8,128)(2,1)S(1)} %collective-permute-done.12.refs_2_, ...), custom_call_target="tpu_custom_call" | custom-call | flops 503316480 | bytes 4096000 | tf_op jit(solution)/shard_map/pallas_call | solution.py:125
  38.3 3.1 %collective-permute-done.14 = f16[176,512]{1,0:T(8,128)(2,1)S(1)} collective-permute-done((f16[176,512]{1,0:T(8,128)(2,1)S(1)}, f16[176,512]{1,0:T(8,128)(2,1)S(1)}, u32[]{:S(2)}, u32[]{:S(2)}) %collective-permute-start.14) | collective-permute-done | bytes 180256 | tf_op jit(solution)/shard_map/ppermute | solution.py:42
  41.6 1.6 %collective-permute-start.15 = (bf16[120,512]{1,0:T(8,128)(2,1)S(1)}, bf16[120,512]{1,0:T(8,128)(2,1)S(1)}, u32[]{:S(2)}, u32[]{:S(2)}) collective-permute-start(bf16[120,512]{1,0:T(8,128)(2,1)S(1)} %pad_maximum_fusion.refs_0_), channel_id=1, source_target_pairs={{0,4},{2,6},{4,8},{6,10},{8,12},{10,14},{12,16},{14,18},{16,20},{1... | collective-permute-start | bytes 368648 | tf_op jit(solution)/shard_map/ppermute | solution.py:34
  43.2 4.0 %collective-permute-start.16 = (bf16[120,512]{1,0:T(8,128)(2,1)S(1)}, bf16[120,512]{1,0:T(8,128)(2,1)S(1)}, u32[]{:S(2)}, u32[]{:S(2)}) collective-permute-start(bf16[120,512]{1,0:T(8,128)(2,1)S(1)} %pad_maximum_fusion.refs_0_), channel_id=1, source_target_pairs={{0,28},{2,30},{4,0},{6,2},{8,4},{10,6},{12,8},{14,10},{16,12},{18,... | collective-permute-start | bytes 368648 | tf_op jit(solution)/shard_map/ppermute | solution.py:34
  48.4 1.5 %collective-permute-start.25 = (bf16[120,512]{1,0:T(8,128)(2,1)S(1)}, bf16[120,512]{1,0:T(8,128)(2,1)S(1)}, u32[]{:S(2)}, u32[]{:S(2)}) collective-permute-start(bf16[120,512]{1,0:T(8,128)(2,1)S(1)} %pad_maximum_fusion.2.refs_0_), channel_id=1, source_target_pairs={{0,28},{2,30},{4,0},{6,2},{8,4},{10,6},{12,8},{14,10},{16,12},{18,... | collective-permute-start | bytes 368648 | tf_op jit(solution)/shard_map/ppermute | solution.py:34
  51.1 2.7 %collective-permute-start.19 = (bf16[120,512]{1,0:T(8,128)(2,1)S(1)}, bf16[120,512]{1,0:T(8,128)(2,1)S(1)}, u32[]{:S(2)}, u32[]{:S(2)}) collective-permute-start(bf16[120,512]{1,0:T(8,128)(2,1)S(1)} %collective-permute-done.16.refs_2_), channel_id=1, source_target_pairs={{0,28},{2,30},{4,0},{6,2},{8,4},{10,6},{12,8},{14,10},{16,12},{18,... | collective-permute-start | bytes 368648 | tf_op jit(solution)/shard_map/ppermute | solution.py:34
  56.0 2.3 %collective-permute-done.20.refs_11_ = bf16[2,40,512]{2,1,0:T(8,128)(2,1)S(1)} collective-permute-done((bf16[2,40,512]{2,1,0:T(8,128)(2,1)S(1)}, bf16[2,40,512]{2,1,0:T(8,128)(2,1)S(1)}, u32[]{:S(2)}, u32[]{:S(2)}) %collective-permute-start.20) | collective-permute-done | bytes 81952 | tf_op jit(solution)/shard_map/ppermute | solution.py:30
  58.3 2.7 %collective-permute-start.22 = (bf16[120,512]{1,0:T(8,128)(2,1)S(1)}, bf16[120,512]{1,0:T(8,128)(2,1)S(1)}, u32[]{:S(2)}, u32[]{:S(2)}) collective-permute-start(bf16[120,512]{1,0:T(8,128)(2,1)S(1)} %collective-permute-done.19.refs_4_), channel_id=1, source_target_pairs={{0,28},{2,30},{4,0},{6,2},{8,4},{10,6},{12,8},{14,10},{16,12},{18,... | collective-permute-start | bytes 368648 | tf_op jit(solution)/shard_map/ppermute | solution.py:34
  60.9 1.5 %collective-permute-start.23 = (bf16[2,40,512]{2,1,0:T(8,128)(2,1)S(1)}, bf16[2,40,512]{2,1,0:T(8,128)(2,1)S(1)}, u32[]{:S(2)}, u32[]{:S(2)}) collective-permute-start(bf16[2,40,512]{2,1,0:T(8,128)(2,1)S(1)} %pad_maximum_fusion.4), channel_id=1, source_target_pairs={{0,128},{32,160},{64,192},{96,224},{128,0},{160,32},{192,64},{224,... | collective-permute-start | bytes 245768 | tf_op jit(solution)/shard_map/ppermute | solution.py:30
  62.5 1.3 %collective-permute-start.27 = (bf16[120,512]{1,0:T(8,128)(2,1)S(1)}, bf16[120,512]{1,0:T(8,128)(2,1)S(1)}, u32[]{:S(2)}, u32[]{:S(2)}) collective-permute-start(bf16[120,512]{1,0:T(8,128)(2,1)S(1)} %collective-permute-done.26.refs_4_), channel_id=1, source_target_pairs={{0,28},{2,30},{4,0},{6,2},{8,4},{10,6},{12,8},{14,10},{16,12},{18,... | collective-permute-start | bytes 368648 | tf_op jit(solution)/shard_map/ppermute | solution.py:34
  64.0 1.8 %collective-permute-done.23.refs_5_ = bf16[2,40,512]{2,1,0:T(8,128)(2,1)S(1)} collective-permute-done((bf16[2,40,512]{2,1,0:T(8,128)(2,1)S(1)}, bf16[2,40,512]{2,1,0:T(8,128)(2,1)S(1)}, u32[]{:S(2)}, u32[]{:S(2)}) %collective-permute-start.23) | collective-permute-done | bytes 81952 | tf_op jit(solution)/shard_map/ppermute | solution.py:30
  66.3 3.4 %collective-permute-start.28 = (bf16[120,512]{1,0:T(8,128)(2,1)S(1)}, bf16[120,512]{1,0:T(8,128)(2,1)S(1)}, u32[]{:S(2)}, u32[]{:S(2)}) collective-permute-start(bf16[120,512]{1,0:T(8,128)(2,1)S(1)} %collective-permute-done.27.refs_6_), channel_id=1, source_target_pairs={{0,28},{2,30},{4,0},{6,2},{8,4},{10,6},{12,8},{14,10},{16,12},{18,... | collective-permute-start | bytes 368648 | tf_op jit(solution)/shard_map/ppermute | solution.py:34
  69.7 1.2 %shard_map.60.refs_3_ = f32[120,512]{1,0:T(8,128)S(1)} custom-call(s32[4]{0:T(128)S(1)} %pad_add_fusion.place_ref, bf16[120,512]{1,0:T(8,128)(2,1)S(1)} %pad_maximum_fusion.2.refs_0_, bf16[120,512]{1,0:T(8,128)(2,1)S(1)} %collective-permute-done.29.refs_1_, bf16[120,512]{1,0:T(8,128)(2,1)S(1)} %collective-permute-done.25.refs_2_, ...), custom_call_target="tpu_custom_call" | custom-call | flops 440401920 | bytes 4530176 | tf_op jit(solution)/shard_map/pallas_call | solution.py:173
  71.4 1.3 %shard_map.59 = (f32[1,8]{1,0:T(1,128)S(1)}, f32[1,8]{1,0:T(1,128)S(1)}, f32[1,8]{1,0:T(1,128)S(1)}) custom-call(s32[4]{0:T(128)S(1)} %pad_add_fusion.place_ref, bf16[120,512]{1,0:T(8,128)(2,1)S(1)} %pad_maximum_fusion.refs_0_, bf16[120,512]{1,0:T(8,128)(2,1)S(1)} %collective-permute-done.15.refs_1_, bf16[120,512]{1,0:T(8,128)(2,1)S(1)} %collective-permute-done.16.refs_2_, ...), custom_call_target="tpu_custom_call" | custom-call | flops 503316480 | bytes 5545984 | tf_op jit(solution)/shard_map/pallas_call | solution.py:226
  72.7 1.9 %collective-permute-start.33 = (f32[1,8]{1,0:T(1,128)S(1)}, f32[1,8]{1,0:T(1,128)S(1)}, u32[]{:S(2)}, u32[]{:S(2)}) collective-permute-start(f32[1,8]{1,0:T(1,128)S(1)} %get-tuple-element.82), channel_id=1, source_target_pairs={{0,224},{32,192},{64,32},{96,0},{128,96},{160,64},{192,160},{224,1... | collective-permute-start | bytes 104 | tf_op jit(solution)/shard_map/ppermute | solution.py:30
  74.6 1.2 %collective-permute-start.32 = (f32[1,8]{1,0:T(1,128)S(1)}, f32[1,8]{1,0:T(1,128)S(1)}, u32[]{:S(2)}, u32[]{:S(2)}) collective-permute-start(f32[1,8]{1,0:T(1,128)S(1)} %get-tuple-element.81), channel_id=1, source_target_pairs={{0,192},{32,224},{64,0},{96,32},{128,64},{160,96},{192,128},{224,1... | collective-permute-start | bytes 104 | tf_op jit(solution)/shard_map/ppermute | solution.py:30
  77.3 27.9 %all_to_all.6 = f32[32,1,8]{2,1,0:T(1,128)S(1)} all-to-all(f32[32,1,8]{2,1,0:T(1,128)S(1)} %broadcast_in_dim.25), channel_id=1, replica_groups=mesh['occ'=8,'cabs'=16,'aux'=2] {'cabs','aux'}, dimensions={0} | all-to-all | bytes 2048 | tf_op jit(solution)/shard_map/all_to_all | solution.py:326
  (73 shorter events, 15.7 us)
Async XLA Ops:
  0.0 15.5 %collective-permute-start.4 = (bf16[4096,256]{1,0:T(8,128)(2,1)}, bf16[4096,256]{1,0:T(8,128)(2,1)S(1)}, u32[]{:S(2)}, u32[]{:S(2)}) collective-permute-start(bf16[4096,256]{1,0:T(8,128)(2,1)} %refs_1_.1), channel_id=1, source_target_pairs={{0,2},{2,0},{4,6},{6,4},{8,10},{10,8},{12,14},{14,12},{16,18},{18,... | collective-permute-start | bytes 6291464 | tf_op jit(solution)/shard_map/ppermute | solution.py:38
  3.2 5.9 %collective-permute-start = (bf16[256,2560]{1,0:T(8,128)(2,1)}, bf16[256,2560]{1,0:T(8,128)(2,1)}, u32[]{:S(2)}, u32[]{:S(2)}) collective-permute-start(bf16[256,2560]{1,0:T(8,128)(2,1)} %bitcast.24), channel_id=1, source_target_pairs={{0,2},{2,0},{4,6},{6,4},{8,10},{10,8},{12,14},{14,12},{16,18},{18,... | collective-permute-start | bytes 3932168 | tf_op jit(solution)/shard_map/ppermute | solution.py:38
  4.1 10.1 %collective-permute-start.1 = (bf16[80,2560]{1,0:T(8,128)(2,1)}, bf16[80,2560]{1,0:T(8,128)(2,1)S(1)}, u32[]{:S(2)}, u32[]{:S(2)}) collective-permute-start(bf16[80,2560]{1,0:T(8,128)(2,1)} %dynamic-slice_bitcast_fusion.refs_0_), channel_id=1, source_target_pairs={{0,32},{32,0},{64,96},{96,64},{128,160},{160,128},{192,224},{224,1... | collective-permute-start | bytes 1228808 | tf_op jit(solution)/shard_map/ppermute | solution.py:30
  4.1 11.4 %collective-permute-start.2 = (bf16[80,2560]{1,0:T(8,128)(2,1)}, bf16[80,2560]{1,0:T(8,128)(2,1)}, u32[]{:S(2)}, u32[]{:S(2)}) collective-permute-start(bf16[80,2560]{1,0:T(8,128)(2,1)} %dynamic-slice_bitcast_fusion.refs_0_), channel_id=1, source_target_pairs={{0,64},{32,96},{64,128},{96,160},{128,192},{160,224},{192,0},{224,... | collective-permute-start | bytes 1228808 | tf_op jit(solution)/shard_map/ppermute | solution.py:30
  5.3 10.2 %collective-permute-start.3 = (bf16[80,2560]{1,0:T(8,128)(2,1)}, bf16[80,2560]{1,0:T(8,128)(2,1)}, u32[]{:S(2)}, u32[]{:S(2)}) collective-permute-start(bf16[80,2560]{1,0:T(8,128)(2,1)} %dynamic-slice_bitcast_fusion.refs_0_), channel_id=1, source_target_pairs={{0,192},{32,224},{64,0},{96,32},{128,64},{160,96},{192,128},{224,1... | collective-permute-start | bytes 1228808 | tf_op jit(solution)/shard_map/ppermute | solution.py:30
  16.5 9.6 %collective-permute-start.5 = (bf16[40,2560]{1,0:T(8,128)(2,1)S(1)}, bf16[40,2560]{1,0:T(8,128)(2,1)S(1)}, u32[]{:S(2)}, u32[]{:S(2)}) collective-permute-start(bf16[40,2560]{1,0:T(8,128)(2,1)S(1)} %get-tuple-element.85), channel_id=1, source_target_pairs={{0,32},{32,0},{64,96},{96,64},{128,160},{160,128},{192,224},{224,1... | collective-permute-start | bytes 614408 | tf_op jit(solution)/shard_map/ppermute | solution.py:30
  17.8 8.6 %collective-permute-start.6 = (bf16[40,2560]{1,0:T(8,128)(2,1)S(1)}, bf16[40,2560]{1,0:T(8,128)(2,1)S(1)}, u32[]{:S(2)}, u32[]{:S(2)}) collective-permute-start(bf16[40,2560]{1,0:T(8,128)(2,1)S(1)} %get-tuple-element.83), channel_id=1, source_target_pairs={{0,64},{32,96},{64,128},{96,160},{128,192},{160,224},{192,0},{224,... | collective-permute-start | bytes 614408 | tf_op jit(solution)/shard_map/ppermute | solution.py:30
  18.2 9.3 %collective-permute-start.7 = (bf16[40,2560]{1,0:T(8,128)(2,1)S(1)}, bf16[40,2560]{1,0:T(8,128)(2,1)S(1)}, u32[]{:S(2)}, u32[]{:S(2)}) collective-permute-start(bf16[40,2560]{1,0:T(8,128)(2,1)S(1)} %get-tuple-element.85), channel_id=1, source_target_pairs={{0,192},{32,224},{64,0},{96,32},{128,64},{160,96},{192,128},{224,1... | collective-permute-start | bytes 614408 | tf_op jit(solution)/shard_map/ppermute | solution.py:30
  20.6 7.3 %collective-permute-start.8 = (bf16[40,2560]{1,0:T(8,128)(2,1)S(1)}, bf16[40,2560]{1,0:T(8,128)(2,1)S(1)}, u32[]{:S(2)}, u32[]{:S(2)}) collective-permute-start(bf16[40,2560]{1,0:T(8,128)(2,1)S(1)} %get-tuple-element.83), channel_id=1, source_target_pairs={{0,128},{32,160},{64,192},{96,224},{128,0},{160,32},{192,64},{224,... | collective-permute-start | bytes 614408 | tf_op jit(solution)/shard_map/ppermute | solution.py:30
  23.8 13.2 %collective-permute-start.9 = (f32[4,40,512]{2,1,0:T(8,128)S(1)}, f32[4,40,512]{2,1,0:T(8,128)S(1)}, u32[]{:S(2)}, u32[]{:S(2)}) collective-permute-start(f32[4,40,512]{2,1,0:T(8,128)S(1)} %get-tuple-element.52), channel_id=1, source_target_pairs={{0,1},{1,0},{2,3},{3,2},{4,5},{5,4},{6,7},{7,6},{8,9},{9,8},{10,11... | collective-permute-start | bytes 983048 | tf_op jit(solution)/shard_map/ppermute | solution.py:42
  26.1 9.2 %collective-permute-start.10 = (bf16[40,2560]{1,0:T(8,128)(2,1)S(1)}, bf16[40,2560]{1,0:T(8,128)(2,1)S(1)}, u32[]{:S(2)}, u32[]{:S(2)}) collective-permute-start(bf16[40,2560]{1,0:T(8,128)(2,1)S(1)} %get-tuple-element.86), channel_id=1, source_target_pairs={{0,32},{32,0},{64,96},{96,64},{128,160},{160,128},{192,224},{224,1... | collective-permute-start | bytes 614408 | tf_op jit(solution)/shard_map/ppermute | solution.py:30
  26.4 10.6 %collective-permute-start.12 = (bf16[40,2560]{1,0:T(8,128)(2,1)S(1)}, bf16[40,2560]{1,0:T(8,128)(2,1)S(1)}, u32[]{:S(2)}, u32[]{:S(2)}) collective-permute-start(bf16[40,2560]{1,0:T(8,128)(2,1)S(1)} %get-tuple-element.86), channel_id=1, source_target_pairs={{0,192},{32,224},{64,0},{96,32},{128,64},{160,96},{192,128},{224,1... | collective-permute-start | bytes 614408 | tf_op jit(solution)/shard_map/ppermute | solution.py:30
  27.5 9.5 %collective-permute-start.11 = (bf16[40,2560]{1,0:T(8,128)(2,1)S(1)}, bf16[40,2560]{1,0:T(8,128)(2,1)S(1)}, u32[]{:S(2)}, u32[]{:S(2)}) collective-permute-start(bf16[40,2560]{1,0:T(8,128)(2,1)S(1)} %get-tuple-element.84), channel_id=1, source_target_pairs={{0,64},{32,96},{64,128},{96,160},{128,192},{160,224},{192,0},{224,... | collective-permute-start | bytes 614408 | tf_op jit(solution)/shard_map/ppermute | solution.py:30
  27.9 9.1 %collective-permute-start.13 = (bf16[40,2560]{1,0:T(8,128)(2,1)S(1)}, bf16[40,2560]{1,0:T(8,128)(2,1)S(1)}, u32[]{:S(2)}, u32[]{:S(2)}) collective-permute-start(bf16[40,2560]{1,0:T(8,128)(2,1)S(1)} %get-tuple-element.84), channel_id=1, source_target_pairs={{0,128},{32,160},{64,192},{96,224},{128,0},{160,32},{192,64},{224,... | collective-permute-start | bytes 614408 | tf_op jit(solution)/shard_map/ppermute | solution.py:30
  35.3 6.2 %collective-permute-start.14 = (f16[176,512]{1,0:T(8,128)(2,1)S(1)}, f16[176,512]{1,0:T(8,128)(2,1)S(1)}, u32[]{:S(2)}, u32[]{:S(2)}) collective-permute-start(f16[176,512]{1,0:T(8,128)(2,1)S(1)} %convert_element_type.16), channel_id=1, source_target_pairs={{0,1},{1,0},{2,3},{3,2},{4,5},{5,4},{6,7},{7,6},{8,9},{9,8},{10,11... | collective-permute-start | bytes 540680 | tf_op jit(solution)/shard_map/ppermute | solution.py:42
  41.6 8.3 %collective-permute-start.15 = (bf16[120,512]{1,0:T(8,128)(2,1)S(1)}, bf16[120,512]{1,0:T(8,128)(2,1)S(1)}, u32[]{:S(2)}, u32[]{:S(2)}) collective-permute-start(bf16[120,512]{1,0:T(8,128)(2,1)S(1)} %pad_maximum_fusion.refs_0_), channel_id=1, source_target_pairs={{0,4},{2,6},{4,8},{6,10},{8,12},{10,14},{12,16},{14,18},{16,20},{1... | collective-permute-start | bytes 368648 | tf_op jit(solution)/shard_map/ppermute | solution.py:34
  43.2 6.8 %collective-permute-start.16 = (bf16[120,512]{1,0:T(8,128)(2,1)S(1)}, bf16[120,512]{1,0:T(8,128)(2,1)S(1)}, u32[]{:S(2)}, u32[]{:S(2)}) collective-permute-start(bf16[120,512]{1,0:T(8,128)(2,1)S(1)} %pad_maximum_fusion.refs_0_), channel_id=1, source_target_pairs={{0,28},{2,30},{4,0},{6,2},{8,4},{10,6},{12,8},{14,10},{16,12},{18,... | collective-permute-start | bytes 368648 | tf_op jit(solution)/shard_map/ppermute | solution.py:34
  48.4 6.1 %collective-permute-start.25 = (bf16[120,512]{1,0:T(8,128)(2,1)S(1)}, bf16[120,512]{1,0:T(8,128)(2,1)S(1)}, u32[]{:S(2)}, u32[]{:S(2)}) collective-permute-start(bf16[120,512]{1,0:T(8,128)(2,1)S(1)} %pad_maximum_fusion.2.refs_0_), channel_id=1, source_target_pairs={{0,28},{2,30},{4,0},{6,2},{8,4},{10,6},{12,8},{14,10},{16,12},{18,... | collective-permute-start | bytes 368648 | tf_op jit(solution)/shard_map/ppermute | solution.py:34
  49.9 5.1 %collective-permute-start.29 = (bf16[120,512]{1,0:T(8,128)(2,1)S(1)}, bf16[120,512]{1,0:T(8,128)(2,1)S(1)}, u32[]{:S(2)}, u32[]{:S(2)}) collective-permute-start(bf16[120,512]{1,0:T(8,128)(2,1)S(1)} %pad_maximum_fusion.2.refs_0_), channel_id=1, source_target_pairs={{0,4},{2,6},{4,8},{6,10},{8,12},{10,14},{12,16},{14,18},{16,20},{1... | collective-permute-start | bytes 368648 | tf_op jit(solution)/shard_map/ppermute | solution.py:34
  51.0 7.3 %collective-permute-start.18 = (bf16[120,512]{1,0:T(8,128)(2,1)S(1)}, bf16[120,512]{1,0:T(8,128)(2,1)S(1)}, u32[]{:S(2)}, u32[]{:S(2)}) collective-permute-start(bf16[120,512]{1,0:T(8,128)(2,1)S(1)} %collective-permute-done.15.refs_1_), channel_id=1, source_target_pairs={{0,4},{2,6},{4,8},{6,10},{8,12},{10,14},{12,16},{14,18},{16,20},{1... | collective-permute-start | bytes 368648 | tf_op jit(solution)/shard_map/ppermute | solution.py:34
  51.1 7.2 %collective-permute-start.19 = (bf16[120,512]{1,0:T(8,128)(2,1)S(1)}, bf16[120,512]{1,0:T(8,128)(2,1)S(1)}, u32[]{:S(2)}, u32[]{:S(2)}) collective-permute-start(bf16[120,512]{1,0:T(8,128)(2,1)S(1)} %collective-permute-done.16.refs_2_), channel_id=1, source_target_pairs={{0,28},{2,30},{4,0},{6,2},{8,4},{10,6},{12,8},{14,10},{16,12},{18,... | collective-permute-start | bytes 368648 | tf_op jit(solution)/shard_map/ppermute | solution.py:34
  53.7 4.5 %collective-permute-start.20 = (bf16[2,40,512]{2,1,0:T(8,128)(2,1)S(1)}, bf16[2,40,512]{2,1,0:T(8,128)(2,1)S(1)}, u32[]{:S(2)}, u32[]{:S(2)}) collective-permute-start(bf16[2,40,512]{2,1,0:T(8,128)(2,1)S(1)} %pad_maximum_fusion.3), channel_id=1, source_target_pairs={{0,64},{32,96},{64,128},{96,160},{128,192},{160,224},{192,0},{224,... | collective-permute-start | bytes 245768 | tf_op jit(solution)/shard_map/ppermute | solution.py:30
  54.5 8.0 %collective-permute-start.26 = (bf16[120,512]{1,0:T(8,128)(2,1)S(1)}, bf16[120,512]{1,0:T(8,128)(2,1)S(1)}, u32[]{:S(2)}, u32[]{:S(2)}) collective-permute-start(bf16[120,512]{1,0:T(8,128)(2,1)S(1)} %collective-permute-done.25.refs_2_), channel_id=1, source_target_pairs={{0,28},{2,30},{4,0},{6,2},{8,4},{10,6},{12,8},{14,10},{16,12},{18,... | collective-permute-start | bytes 368648 | tf_op jit(solution)/shard_map/ppermute | solution.py:34
  55.0 8.9 %collective-permute-start.30 = (bf16[120,512]{1,0:T(8,128)(2,1)S(1)}, bf16[120,512]{1,0:T(8,128)(2,1)S(1)}, u32[]{:S(2)}, u32[]{:S(2)}) collective-permute-start(bf16[120,512]{1,0:T(8,128)(2,1)S(1)} %collective-permute-done.29.refs_1_), channel_id=1, source_target_pairs={{0,4},{2,6},{4,8},{6,10},{8,12},{10,14},{12,16},{14,18},{16,20},{1... | collective-permute-start | bytes 368648 | tf_op jit(solution)/shard_map/ppermute | solution.py:34
  58.3 7.5 %collective-permute-start.21 = (bf16[120,512]{1,0:T(8,128)(2,1)S(1)}, bf16[120,512]{1,0:T(8,128)(2,1)S(1)}, u32[]{:S(2)}, u32[]{:S(2)}) collective-permute-start(bf16[120,512]{1,0:T(8,128)(2,1)S(1)} %collective-permute-done.18.refs_3_), channel_id=1, source_target_pairs={{0,4},{2,6},{4,8},{6,10},{8,12},{10,14},{12,16},{14,18},{16,20},{1... | collective-permute-start | bytes 368648 | tf_op jit(solution)/shard_map/ppermute | solution.py:34
  58.3 7.5 %collective-permute-start.22 = (bf16[120,512]{1,0:T(8,128)(2,1)S(1)}, bf16[120,512]{1,0:T(8,128)(2,1)S(1)}, u32[]{:S(2)}, u32[]{:S(2)}) collective-permute-start(bf16[120,512]{1,0:T(8,128)(2,1)S(1)} %collective-permute-done.19.refs_4_), channel_id=1, source_target_pairs={{0,28},{2,30},{4,0},{6,2},{8,4},{10,6},{12,8},{14,10},{16,12},{18,... | collective-permute-start | bytes 368648 | tf_op jit(solution)/shard_map/ppermute | solution.py:34
  60.9 4.8 %collective-permute-start.23 = (bf16[2,40,512]{2,1,0:T(8,128)(2,1)S(1)}, bf16[2,40,512]{2,1,0:T(8,128)(2,1)S(1)}, u32[]{:S(2)}, u32[]{:S(2)}) collective-permute-start(bf16[2,40,512]{2,1,0:T(8,128)(2,1)S(1)} %pad_maximum_fusion.4), channel_id=1, source_target_pairs={{0,128},{32,160},{64,192},{96,224},{128,0},{160,32},{192,64},{224,... | collective-permute-start | bytes 245768 | tf_op jit(solution)/shard_map/ppermute | solution.py:30
  62.5 3.8 %collective-permute-start.27 = (bf16[120,512]{1,0:T(8,128)(2,1)S(1)}, bf16[120,512]{1,0:T(8,128)(2,1)S(1)}, u32[]{:S(2)}, u32[]{:S(2)}) collective-permute-start(bf16[120,512]{1,0:T(8,128)(2,1)S(1)} %collective-permute-done.26.refs_4_), channel_id=1, source_target_pairs={{0,28},{2,30},{4,0},{6,2},{8,4},{10,6},{12,8},{14,10},{16,12},{18,... | collective-permute-start | bytes 368648 | tf_op jit(solution)/shard_map/ppermute | solution.py:34
  63.8 5.9 %collective-permute-start.31 = (bf16[120,512]{1,0:T(8,128)(2,1)S(1)}, bf16[120,512]{1,0:T(8,128)(2,1)S(1)}, u32[]{:S(2)}, u32[]{:S(2)}) collective-permute-start(bf16[120,512]{1,0:T(8,128)(2,1)S(1)} %collective-permute-done.30.refs_3_), channel_id=1, source_target_pairs={{0,4},{2,6},{4,8},{6,10},{8,12},{10,14},{12,16},{14,18},{16,20},{1... | collective-permute-start | bytes 368648 | tf_op jit(solution)/shard_map/ppermute | solution.py:34
  65.7 5.7 %collective-permute-start.24 = (bf16[120,512]{1,0:T(8,128)(2,1)S(1)}, bf16[120,512]{1,0:T(8,128)(2,1)S(1)}, u32[]{:S(2)}, u32[]{:S(2)}) collective-permute-start(bf16[120,512]{1,0:T(8,128)(2,1)S(1)} %collective-permute-done.21.refs_5_), channel_id=1, source_target_pairs={{0,4},{2,6},{4,8},{6,10},{8,12},{10,14},{12,16},{14,18},{16,20},{1... | collective-permute-start | bytes 368648 | tf_op jit(solution)/shard_map/ppermute | solution.py:34
  66.3 9.6 %collective-permute-start.28 = (bf16[120,512]{1,0:T(8,128)(2,1)S(1)}, bf16[120,512]{1,0:T(8,128)(2,1)S(1)}, u32[]{:S(2)}, u32[]{:S(2)}) collective-permute-start(bf16[120,512]{1,0:T(8,128)(2,1)S(1)} %collective-permute-done.27.refs_6_), channel_id=1, source_target_pairs={{0,28},{2,30},{4,0},{6,2},{8,4},{10,6},{12,8},{14,10},{16,12},{18,... | collective-permute-start | bytes 368648 | tf_op jit(solution)/shard_map/ppermute | solution.py:34
  72.7 4.0 %collective-permute-start.33 = (f32[1,8]{1,0:T(1,128)S(1)}, f32[1,8]{1,0:T(1,128)S(1)}, u32[]{:S(2)}, u32[]{:S(2)}) collective-permute-start(f32[1,8]{1,0:T(1,128)S(1)} %get-tuple-element.82), channel_id=1, source_target_pairs={{0,224},{32,192},{64,32},{96,0},{128,96},{160,64},{192,160},{224,1... | collective-permute-start | bytes 104 | tf_op jit(solution)/shard_map/ppermute | solution.py:30
  (6 other events, 43.1 us)

commit v5 on v4

--- a/solution.py
+++ b/solution.py
@@ -48,6 +48,26 @@
 
 def plain_dot(left, right):
     return lax.dot_general(left, right, (((1,), (0,)), ((), ())), preferred_element_type=F32)
+
+
+def own_rows(place, occ_fit, size):
+    fit = occ_fit.shape[2]
+
+    def body(place_ref, rows_ref, out_ref, sem):
+        first = pl.multiple_of(place_ref[2] * size, 16)
+        copy = pltpu.make_async_copy(rows_ref.at[0, pl.ds(first, size), :], out_ref, sem)
+        copy.start()
+        copy.wait()
+
+    return pl.pallas_call(
+        body,
+        out_shape=jax.ShapeDtypeStruct((size, fit), BF),
+        in_specs=[SMEM, pl.BlockSpec(memory_space=pl.ANY)],
+        out_specs=VMEM,
+        scratch_shapes=[pltpu.SemaphoreType.DMA],
+        compiler_params=PARAMS,
+        cost_estimate=pl.CostEstimate(flops=0, bytes_accessed=4 * size * fit, transcendentals=0),
+    )(place, occ_fit)
 
 
 def prepare(place, pair_block, block_rows, slab, slab_other):
@@ -249,7 +269,7 @@
     width = cabs_fit.shape[1]
     half = m_rows // 2
 
-    own = lax.dynamic_slice_in_dim(occ_fit[0], core * half, half, 0)
+    own = own_rows(place, occ_fit, half)
     slab_other = core_swap(cabs_fit[0])
     fock_other = core_swap(fock)
 

time: 106 us -> 106 us (level)
  waiting for transfers between devices: 17.6 us -> 20.2 us
  starting transfers between devices: 44.1 us -> 41.6 us
    ppermute x16, waiting for transfers between devices: 11.9 us -> 15.5 us  [occ_hop(): lax.ppermute(value, 'occ', [(o, partner(o, dy, flip)) for o in range(OCC)])]
    ppermute x14, starting transfers between devices: 18.9 us -> 17 us  [z_hop(): lax.ppermute(value, 'cabs', [(c, (c // 2 + dz) % Z * 2 + c % 2) for c in...]
    ppermute x2, waiting for transfers between devices: 1.57 us -> 0.3 us  [core_swap(): return lax.ppermute(value, 'cabs', [(c, c ^ 1) for c in range(2 * Z)])]
    unnamed x8, local copies, waits for them, and re-layouts: 1.98 us -> 3.12 us
  transfers between devices with their start and end apart: 34 -> 34, of which waited for: 11 -> 12; matrix products, arithmetic and copies ran while one was open for 2% -> 1% of each run, Pallas kernels for 10% -> 10%
where the time goes in v5:
time: 106 us; the launch traced here: 105 us
  starting transfers between devices  41.6 us (39%)
  blocking collectives  27.5 us (26%)
  waiting for transfers between devices  20.2 us (19%)
  Pallas kernels  10.9 us (10%)
  local copies, waits for them, and re-layouts  3.99 us (4%)
    all_to_all x1, blocking collectives, shards(): lax.all_to_all(jnp.broadcast_to(row, (peers, OCC)), ('cabs', 'aux'), 0, 0...  27.5 us
    ppermute x16, starting transfers between devices, occ_hop(): lax.ppermute(value, 'occ', [(o, partner(o, dy, flip)) for o in range(OCC)])  17.1 us
    ppermute x14, starting transfers between devices, z_hop(): lax.ppermute(value, 'cabs', [(c, (c // 2 + dz) % Z * 2 + c % 2) for c in...  17 us
    ppermute x16, waiting for transfers between devices, occ_hop(): lax.ppermute(value, 'occ', [(o, partner(o, dy, flip)) for o in range(OCC)])  15.5 us
    pallas_call x3, Pallas kernels, fit_sums(): pl.pallas_call(body, out_shape=shapes, in_specs=[SMEM] + [VMEM] * (count...  4.65 us
    ppermute x2, starting transfers between devices, aux_swap(): return lax.ppermute(value, 'aux', [(0, 1), (1, 0)])  4.24 us
    ppermute x2, starting transfers between devices, core_swap(): return lax.ppermute(value, 'cabs', [(c, c ^ 1) for c in range(2 * Z)])  3.24 us
    unnamed x8, local copies, waits for them, and re-layouts  3.12 us
  transfers between devices with their start and end apart: 34, of which 12 were waited for; matrix products, arithmetic and copies ran while one was open for 1% of the time, Pallas kernels for 10%

profile of v5, /device:TPU:1, one launch (start us, length us, event | category | flops | bytes accessed | tf_op | source)
XLA Modules:
  0.0 105.3 jit_solution(17742512537235880842)
XLA Ops:
  0.0 3.2 %collective-permute-start.4 = (bf16[4096,256]{1,0:T(8,128)(2,1)}, bf16[4096,256]{1,0:T(8,128)(2,1)S(1)}, u32[]{:S(2)}, u32[]{:S(2)}) collective-permute-start(bf16[4096,256]{1,0:T(8,128)(2,1)} %refs_1_.1), channel_id=1, source_target_pairs={{0,2},{2,0},{4,6},{6,4},{8,10},{10,8},{12,14},{14,12},{16,18},{18,... | collective-permute-start | bytes 6291464 | tf_op jit(solution)/shard_map/ppermute | solution.py:38
  3.3 1.1 %copy-done.2 = bf16[1,160,2560]{2,1,0:T(8,128)(2,1)S(1)} copy-done((bf16[1,160,2560]{2,1,0:T(8,128)(2,1)S(1)}, bf16[1,160,2560]{2,1,0:T(8,128)(2,1)}, u32[]{:S(2)}) %copy-start.2) | copy-done | bytes 819224
  6.1 2.0 %collective-permute-start.3 = (bf16[80,2560]{1,0:T(8,128)(2,1)S(1)}, bf16[80,2560]{1,0:T(8,128)(2,1)S(1)}, u32[]{:S(2)}, u32[]{:S(2)}) collective-permute-start(bf16[80,2560]{1,0:T(8,128)(2,1)S(1)} %shard_map.56.refs_0_), channel_id=1, source_target_pairs={{0,192},{32,224},{64,0},{96,32},{128,64},{160,96},{192,128},{224,1... | collective-permute-start | bytes 1228808 | tf_op jit(solution)/shard_map/ppermute | solution.py:30
  9.1 1.3 %copy-done.1 = bf16[1,256,2560]{2,1,0:T(8,128)(2,1)S(1)} copy-done((bf16[1,256,2560]{2,1,0:T(8,128)(2,1)S(1)}, bf16[1,256,2560]{2,1,0:T(8,128)(2,1)}, u32[]{:S(2)}) %copy-start.1) | copy-done | bytes 1310744
  11.1 2.0 %shard_map.55 = (bf16[2560,512]{1,0:T(8,128)(2,1)S(1)}, s32[8,512]{1,0:T(8,128)S(1)}) custom-call(s32[4]{0:T(128)S(1)} %pad_add_fusion.place_ref, s32[8]{0:T(128)S(1)} %copy-done.3, s32[8,512]{1,0:T(8,128)S(1)} %reshape.16.rows_ref, bf16[256,2560]{1,0:T(8,128)(2,1)S(1)} %bitcast.23, bf16[256,2560]{1,0:T(8,128)(2,1)} %collective-permute-done.other_ref), custom_call_target="tpu_custom_call" | custom-call | bytes 5242880 | tf_op jit(solution)/shard_map/pallas_call | solution.py:90
  13.1 2.8 %collective-permute-done.1.refs_1_ = bf16[80,2560]{1,0:T(8,128)(2,1)S(1)} collective-permute-done((bf16[80,2560]{1,0:T(8,128)(2,1)S(1)}, bf16[80,2560]{1,0:T(8,128)(2,1)S(1)}, u32[]{:S(2)}, u32[]{:S(2)}) %collective-permute-start.1) | collective-permute-done | bytes 409632 | tf_op jit(solution)/shard_map/ppermute | solution.py:30
  16.0 1.3 %collective-permute-done.2.refs_2_ = bf16[80,2560]{1,0:T(8,128)(2,1)} collective-permute-done((bf16[80,2560]{1,0:T(8,128)(2,1)S(1)}, bf16[80,2560]{1,0:T(8,128)(2,1)}, u32[]{:S(2)}, u32[]{:S(2)}) %collective-permute-start.2) | collective-permute-done | bytes 409632 | tf_op jit(solution)/shard_map/ppermute | solution.py:30
  17.3 1.1 %collective-permute-start.5 = (bf16[40,2560]{1,0:T(8,128)(2,1)S(1)}, bf16[40,2560]{1,0:T(8,128)(2,1)S(1)}, u32[]{:S(2)}, u32[]{:S(2)}) collective-permute-start(bf16[40,2560]{1,0:T(8,128)(2,1)S(1)} %get-tuple-element.85), channel_id=1, source_target_pairs={{0,32},{32,0},{64,96},{96,64},{128,160},{160,128},{192,224},{224,1... | collective-permute-start | bytes 614408 | tf_op jit(solution)/shard_map/ppermute | solution.py:30
  18.6 2.7 %collective-permute-start.7 = (bf16[40,2560]{1,0:T(8,128)(2,1)S(1)}, bf16[40,2560]{1,0:T(8,128)(2,1)S(1)}, u32[]{:S(2)}, u32[]{:S(2)}) collective-permute-start(bf16[40,2560]{1,0:T(8,128)(2,1)S(1)} %get-tuple-element.85), channel_id=1, source_target_pairs={{0,192},{32,224},{64,0},{96,32},{128,64},{160,96},{192,128},{224,1... | collective-permute-start | bytes 614408 | tf_op jit(solution)/shard_map/ppermute | solution.py:30
  22.0 2.1 %shard_map.57 = (f32[4,40,512]{2,1,0:T(8,128)S(1)}, f32[4,40,512]{2,1,0:T(8,128)S(1)}) custom-call(s32[4]{0:T(128)S(1)} %pad_add_fusion.place_ref, bf16[80,2560]{1,0:T(8,128)(2,1)S(1)} %shard_map.56.refs_0_, bf16[80,2560]{1,0:T(8,128)(2,1)S(1)} %collective-permute-done.1.refs_1_, bf16[80,2560]{1,0:T(8,128)(2,1)} %collective-permute-done.2.refs_2_, ...), custom_call_target="tpu_custom_call" | custom-call | flops 838860800 | bytes 5570560 | tf_op jit(solution)/shard_map/pallas_call | solution.py:145
  24.1 1.5 %collective-permute-start.9 = (f32[4,40,512]{2,1,0:T(8,128)S(1)}, f32[4,40,512]{2,1,0:T(8,128)S(1)}, u32[]{:S(2)}, u32[]{:S(2)}) collective-permute-start(f32[4,40,512]{2,1,0:T(8,128)S(1)} %get-tuple-element.52), channel_id=1, source_target_pairs={{0,1},{1,0},{2,3},{3,2},{4,5},{5,4},{6,7},{7,6},{8,9},{9,8},{10,11... | collective-permute-start | bytes 983048 | tf_op jit(solution)/shard_map/ppermute | solution.py:42
  25.9 1.1 %collective-permute-start.12 = (bf16[40,2560]{1,0:T(8,128)(2,1)S(1)}, bf16[40,2560]{1,0:T(8,128)(2,1)S(1)}, u32[]{:S(2)}, u32[]{:S(2)}) collective-permute-start(bf16[40,2560]{1,0:T(8,128)(2,1)S(1)} %get-tuple-element.86), channel_id=1, source_target_pairs={{0,192},{32,224},{64,0},{96,32},{128,64},{160,96},{192,128},{224,1... | collective-permute-start | bytes 614408 | tf_op jit(solution)/shard_map/ppermute | solution.py:30
  27.4 1.7 %collective-permute-done.8.refs_3_ = bf16[40,2560]{1,0:T(8,128)(2,1)S(1)} collective-permute-done((bf16[40,2560]{1,0:T(8,128)(2,1)S(1)}, bf16[40,2560]{1,0:T(8,128)(2,1)S(1)}, u32[]{:S(2)}, u32[]{:S(2)}) %collective-permute-start.8) | collective-permute-done | bytes 204832 | tf_op jit(solution)/shard_map/ppermute | solution.py:30
  29.6 1.4 %shard_map.59 = f32[176,512]{1,0:T(8,128)S(1)} custom-call(s32[4]{0:T(128)S(1)} %pad_add_fusion.place_ref, bf16[40,2560]{1,0:T(8,128)(2,1)S(1)} %collective-permute-done.5.refs_0_, bf16[40,2560]{1,0:T(8,128)(2,1)S(1)} %collective-permute-done.6.refs_1_, bf16[40,2560]{1,0:T(8,128)(2,1)S(1)} %collective-permute-done.7.refs_2_, ...), custom_call_target="tpu_custom_call" | custom-call | flops 503316480 | bytes 4096000 | tf_op jit(solution)/shard_map/pallas_call | solution.py:145
  31.0 4.0 %collective-permute-done.10.refs_0_ = bf16[40,2560]{1,0:T(8,128)(2,1)S(1)} collective-permute-done((bf16[40,2560]{1,0:T(8,128)(2,1)S(1)}, bf16[40,2560]{1,0:T(8,128)(2,1)S(1)}, u32[]{:S(2)}, u32[]{:S(2)}) %collective-permute-start.10) | collective-permute-done | bytes 204832 | tf_op jit(solution)/shard_map/ppermute | solution.py:30
  35.0 2.7 %collective-permute-start.14 = (f16[176,512]{1,0:T(8,128)(2,1)S(1)}, f16[176,512]{1,0:T(8,128)(2,1)S(1)}, u32[]{:S(2)}, u32[]{:S(2)}) collective-permute-start(f16[176,512]{1,0:T(8,128)(2,1)S(1)} %convert_element_type.16), channel_id=1, source_target_pairs={{0,1},{1,0},{2,3},{3,2},{4,5},{5,4},{6,7},{7,6},{8,9},{9,8},{10,11... | collective-permute-start | bytes 540680 | tf_op jit(solution)/shard_map/ppermute | solution.py:42
  37.8 1.2 %shard_map.58 = f32[4,40,512]{2,1,0:T(8,128)S(1)} custom-call(s32[4]{0:T(128)S(1)} %pad_add_fusion.place_ref, bf16[40,2560]{1,0:T(8,128)(2,1)S(1)} %collective-permute-done.10.refs_0_, bf16[40,2560]{1,0:T(8,128)(2,1)S(1)} %collective-permute-done.11.refs_1_, bf16[40,2560]{1,0:T(8,128)(2,1)S(1)} %collective-permute-done.12.refs_2_, ...), custom_call_target="tpu_custom_call" | custom-call | flops 503316480 | bytes 4096000 | tf_op jit(solution)/shard_map/pallas_call | solution.py:145
  39.1 2.6 %collective-permute-done.14 = f16[176,512]{1,0:T(8,128)(2,1)S(1)} collective-permute-done((f16[176,512]{1,0:T(8,128)(2,1)S(1)}, f16[176,512]{1,0:T(8,128)(2,1)S(1)}, u32[]{:S(2)}, u32[]{:S(2)}) %collective-permute-start.14) | collective-permute-done | bytes 180256 | tf_op jit(solution)/shard_map/ppermute | solution.py:42
  43.0 4.0 %collective-permute-start.16 = (bf16[120,512]{1,0:T(8,128)(2,1)S(1)}, bf16[120,512]{1,0:T(8,128)(2,1)S(1)}, u32[]{:S(2)}, u32[]{:S(2)}) collective-permute-start(bf16[120,512]{1,0:T(8,128)(2,1)S(1)} %pad_maximum_fusion.refs_0_), channel_id=1, source_target_pairs={{0,28},{2,30},{4,0},{6,2},{8,4},{10,6},{12,8},{14,10},{16,12},{18,... | collective-permute-start | bytes 368648 | tf_op jit(solution)/shard_map/ppermute | solution.py:34
  47.0 1.2 %collective-permute-start.17 = (bf16[3,40,512]{2,1,0:T(8,128)(2,1)S(1)}, bf16[3,40,512]{2,1,0:T(8,128)(2,1)S(1)}, u32[]{:S(2)}, u32[]{:S(2)}) collective-permute-start(bf16[3,40,512]{2,1,0:T(8,128)(2,1)S(1)} %pad_maximum_fusion.1), channel_id=1, source_target_pairs={{0,32},{32,0},{64,96},{96,64},{128,160},{160,128},{192,224},{224,1... | collective-permute-start | bytes 368648 | tf_op jit(solution)/shard_map/ppermute | solution.py:30
  48.2 1.5 %collective-permute-start.25 = (bf16[120,512]{1,0:T(8,128)(2,1)S(1)}, bf16[120,512]{1,0:T(8,128)(2,1)S(1)}, u32[]{:S(2)}, u32[]{:S(2)}) collective-permute-start(bf16[120,512]{1,0:T(8,128)(2,1)S(1)} %pad_maximum_fusion.2.refs_0_), channel_id=1, source_target_pairs={{0,28},{2,30},{4,0},{6,2},{8,4},{10,6},{12,8},{14,10},{16,12},{18,... | collective-permute-start | bytes 368648 | tf_op jit(solution)/shard_map/ppermute | solution.py:34
  50.9 2.7 %collective-permute-start.19 = (bf16[120,512]{1,0:T(8,128)(2,1)S(1)}, bf16[120,512]{1,0:T(8,128)(2,1)S(1)}, u32[]{:S(2)}, u32[]{:S(2)}) collective-permute-start(bf16[120,512]{1,0:T(8,128)(2,1)S(1)} %collective-permute-done.16.refs_2_), channel_id=1, source_target_pairs={{0,28},{2,30},{4,0},{6,2},{8,4},{10,6},{12,8},{14,10},{16,12},{18,... | collective-permute-start | bytes 368648 | tf_op jit(solution)/shard_map/ppermute | solution.py:34
  55.5 2.5 %collective-permute-done.20.refs_11_ = bf16[2,40,512]{2,1,0:T(8,128)(2,1)S(1)} collective-permute-done((bf16[2,40,512]{2,1,0:T(8,128)(2,1)S(1)}, bf16[2,40,512]{2,1,0:T(8,128)(2,1)S(1)}, u32[]{:S(2)}, u32[]{:S(2)}) %collective-permute-start.20) | collective-permute-done | bytes 81952 | tf_op jit(solution)/shard_map/ppermute | solution.py:30
  58.1 2.6 %collective-permute-start.22 = (bf16[120,512]{1,0:T(8,128)(2,1)S(1)}, bf16[120,512]{1,0:T(8,128)(2,1)S(1)}, u32[]{:S(2)}, u32[]{:S(2)}) collective-permute-start(bf16[120,512]{1,0:T(8,128)(2,1)S(1)} %collective-permute-done.19.refs_4_), channel_id=1, source_target_pairs={{0,28},{2,30},{4,0},{6,2},{8,4},{10,6},{12,8},{14,10},{16,12},{18,... | collective-permute-start | bytes 368648 | tf_op jit(solution)/shard_map/ppermute | solution.py:34
  60.7 1.4 %collective-permute-start.23 = (bf16[2,40,512]{2,1,0:T(8,128)(2,1)S(1)}, bf16[2,40,512]{2,1,0:T(8,128)(2,1)S(1)}, u32[]{:S(2)}, u32[]{:S(2)}) collective-permute-start(bf16[2,40,512]{2,1,0:T(8,128)(2,1)S(1)} %pad_maximum_fusion.4), channel_id=1, source_target_pairs={{0,128},{32,160},{64,192},{96,224},{128,0},{160,32},{192,64},{224,... | collective-permute-start | bytes 245768 | tf_op jit(solution)/shard_map/ppermute | solution.py:30
  63.6 2.2 %collective-permute-done.23.refs_5_ = bf16[2,40,512]{2,1,0:T(8,128)(2,1)S(1)} collective-permute-done((bf16[2,40,512]{2,1,0:T(8,128)(2,1)S(1)}, bf16[2,40,512]{2,1,0:T(8,128)(2,1)S(1)}, u32[]{:S(2)}, u32[]{:S(2)}) %collective-permute-start.23) | collective-permute-done | bytes 81952 | tf_op jit(solution)/shard_map/ppermute | solution.py:30
  66.5 2.7 %collective-permute-start.28 = (bf16[120,512]{1,0:T(8,128)(2,1)S(1)}, bf16[120,512]{1,0:T(8,128)(2,1)S(1)}, u32[]{:S(2)}, u32[]{:S(2)}) collective-permute-start(bf16[120,512]{1,0:T(8,128)(2,1)S(1)} %collective-permute-done.27.refs_6_), channel_id=1, source_target_pairs={{0,28},{2,30},{4,0},{6,2},{8,4},{10,6},{12,8},{14,10},{16,12},{18,... | collective-permute-start | bytes 368648 | tf_op jit(solution)/shard_map/ppermute | solution.py:34
  69.2 1.2 %shard_map.61.refs_3_ = f32[120,512]{1,0:T(8,128)S(1)} custom-call(s32[4]{0:T(128)S(1)} %pad_add_fusion.place_ref, bf16[120,512]{1,0:T(8,128)(2,1)S(1)} %pad_maximum_fusion.2.refs_0_, bf16[120,512]{1,0:T(8,128)(2,1)S(1)} %collective-permute-done.29.refs_1_, bf16[120,512]{1,0:T(8,128)(2,1)S(1)} %collective-permute-done.25.refs_2_, ...), custom_call_target="tpu_custom_call" | custom-call | flops 440401920 | bytes 4530176 | tf_op jit(solution)/shard_map/pallas_call | solution.py:193
  70.7 1.3 %shard_map.60 = (f32[1,8]{1,0:T(1,128)S(1)}, f32[1,8]{1,0:T(1,128)S(1)}, f32[1,8]{1,0:T(1,128)S(1)}) custom-call(s32[4]{0:T(128)S(1)} %pad_add_fusion.place_ref, bf16[120,512]{1,0:T(8,128)(2,1)S(1)} %pad_maximum_fusion.refs_0_, bf16[120,512]{1,0:T(8,128)(2,1)S(1)} %collective-permute-done.15.refs_1_, bf16[120,512]{1,0:T(8,128)(2,1)S(1)} %collective-permute-done.16.refs_2_, ...), custom_call_target="tpu_custom_call" | custom-call | flops 503316480 | bytes 5545984 | tf_op jit(solution)/shard_map/pallas_call | solution.py:246
  72.0 1.7 %collective-permute-start.33 = (f32[1,8]{1,0:T(1,128)S(1)}, f32[1,8]{1,0:T(1,128)S(1)}, u32[]{:S(2)}, u32[]{:S(2)}) collective-permute-start(f32[1,8]{1,0:T(1,128)S(1)} %get-tuple-element.82), channel_id=1, source_target_pairs={{0,224},{32,192},{64,32},{96,0},{128,96},{160,64},{192,160},{224,1... | collective-permute-start | bytes 104 | tf_op jit(solution)/shard_map/ppermute | solution.py:30
  73.8 2.6 %collective-permute-start.32 = (f32[1,8]{1,0:T(1,128)S(1)}, f32[1,8]{1,0:T(1,128)S(1)}, u32[]{:S(2)}, u32[]{:S(2)}) collective-permute-start(f32[1,8]{1,0:T(1,128)S(1)} %get-tuple-element.81), channel_id=1, source_target_pairs={{0,192},{32,224},{64,0},{96,32},{128,64},{160,96},{192,128},{224,1... | collective-permute-start | bytes 104 | tf_op jit(solution)/shard_map/ppermute | solution.py:30
  77.2 27.5 %all_to_all.6 = f32[32,1,8]{2,1,0:T(1,128)S(1)} all-to-all(f32[32,1,8]{2,1,0:T(1,128)S(1)} %broadcast_in_dim.25), channel_id=1, replica_groups=mesh['occ'=8,'cabs'=16,'aux'=2] {'cabs','aux'}, dimensions={0} | all-to-all | bytes 2048 | tf_op jit(solution)/shard_map/all_to_all | solution.py:346
  (73 shorter events, 14.1 us)
Async XLA Ops:
  0.0 17.3 %collective-permute-start.4 = (bf16[4096,256]{1,0:T(8,128)(2,1)}, bf16[4096,256]{1,0:T(8,128)(2,1)S(1)}, u32[]{:S(2)}, u32[]{:S(2)}) collective-permute-start(bf16[4096,256]{1,0:T(8,128)(2,1)} %refs_1_.1), channel_id=1, source_target_pairs={{0,2},{2,0},{4,6},{6,4},{8,10},{10,8},{12,14},{14,12},{16,18},{18,... | collective-permute-start | bytes 6291464 | tf_op jit(solution)/shard_map/ppermute | solution.py:38
  3.2 5.9 %collective-permute-start = (bf16[256,2560]{1,0:T(8,128)(2,1)}, bf16[256,2560]{1,0:T(8,128)(2,1)}, u32[]{:S(2)}, u32[]{:S(2)}) collective-permute-start(bf16[256,2560]{1,0:T(8,128)(2,1)} %bitcast.22), channel_id=1, source_target_pairs={{0,2},{2,0},{4,6},{6,4},{8,10},{10,8},{12,14},{14,12},{16,18},{18,... | collective-permute-start | bytes 3932168 | tf_op jit(solution)/shard_map/ppermute | solution.py:38
  5.2 10.7 %collective-permute-start.1 = (bf16[80,2560]{1,0:T(8,128)(2,1)S(1)}, bf16[80,2560]{1,0:T(8,128)(2,1)S(1)}, u32[]{:S(2)}, u32[]{:S(2)}) collective-permute-start(bf16[80,2560]{1,0:T(8,128)(2,1)S(1)} %shard_map.56.refs_0_), channel_id=1, source_target_pairs={{0,32},{32,0},{64,96},{96,64},{128,160},{160,128},{192,224},{224,1... | collective-permute-start | bytes 1228808 | tf_op jit(solution)/shard_map/ppermute | solution.py:30
  5.3 11.9 %collective-permute-start.2 = (bf16[80,2560]{1,0:T(8,128)(2,1)S(1)}, bf16[80,2560]{1,0:T(8,128)(2,1)}, u32[]{:S(2)}, u32[]{:S(2)}) collective-permute-start(bf16[80,2560]{1,0:T(8,128)(2,1)S(1)} %shard_map.56.refs_0_), channel_id=1, source_target_pairs={{0,64},{32,96},{64,128},{96,160},{128,192},{160,224},{192,0},{224,... | collective-permute-start | bytes 1228808 | tf_op jit(solution)/shard_map/ppermute | solution.py:30
  6.1 11.2 %collective-permute-start.3 = (bf16[80,2560]{1,0:T(8,128)(2,1)S(1)}, bf16[80,2560]{1,0:T(8,128)(2,1)S(1)}, u32[]{:S(2)}, u32[]{:S(2)}) collective-permute-start(bf16[80,2560]{1,0:T(8,128)(2,1)S(1)} %shard_map.56.refs_0_), channel_id=1, source_target_pairs={{0,192},{32,224},{64,0},{96,32},{128,64},{160,96},{192,128},{224,1... | collective-permute-start | bytes 1228808 | tf_op jit(solution)/shard_map/ppermute | solution.py:30
  17.3 8.3 %collective-permute-start.5 = (bf16[40,2560]{1,0:T(8,128)(2,1)S(1)}, bf16[40,2560]{1,0:T(8,128)(2,1)S(1)}, u32[]{:S(2)}, u32[]{:S(2)}) collective-permute-start(bf16[40,2560]{1,0:T(8,128)(2,1)S(1)} %get-tuple-element.85), channel_id=1, source_target_pairs={{0,32},{32,0},{64,96},{96,64},{128,160},{160,128},{192,224},{224,1... | collective-permute-start | bytes 614408 | tf_op jit(solution)/shard_map/ppermute | solution.py:30
  18.5 7.4 %collective-permute-start.6 = (bf16[40,2560]{1,0:T(8,128)(2,1)S(1)}, bf16[40,2560]{1,0:T(8,128)(2,1)S(1)}, u32[]{:S(2)}, u32[]{:S(2)}) collective-permute-start(bf16[40,2560]{1,0:T(8,128)(2,1)S(1)} %get-tuple-element.83), channel_id=1, source_target_pairs={{0,64},{32,96},{64,128},{96,160},{128,192},{160,224},{192,0},{224,... | collective-permute-start | bytes 614408 | tf_op jit(solution)/shard_map/ppermute | solution.py:30
  18.6 8.4 %collective-permute-start.7 = (bf16[40,2560]{1,0:T(8,128)(2,1)S(1)}, bf16[40,2560]{1,0:T(8,128)(2,1)S(1)}, u32[]{:S(2)}, u32[]{:S(2)}) collective-permute-start(bf16[40,2560]{1,0:T(8,128)(2,1)S(1)} %get-tuple-element.85), channel_id=1, source_target_pairs={{0,192},{32,224},{64,0},{96,32},{128,64},{160,96},{192,128},{224,1... | collective-permute-start | bytes 614408 | tf_op jit(solution)/shard_map/ppermute | solution.py:30
  21.2 7.9 %collective-permute-start.8 = (bf16[40,2560]{1,0:T(8,128)(2,1)S(1)}, bf16[40,2560]{1,0:T(8,128)(2,1)S(1)}, u32[]{:S(2)}, u32[]{:S(2)}) collective-permute-start(bf16[40,2560]{1,0:T(8,128)(2,1)S(1)} %get-tuple-element.83), channel_id=1, source_target_pairs={{0,128},{32,160},{64,192},{96,224},{128,0},{160,32},{192,64},{224,... | collective-permute-start | bytes 614408 | tf_op jit(solution)/shard_map/ppermute | solution.py:30
  24.1 13.7 %collective-permute-start.9 = (f32[4,40,512]{2,1,0:T(8,128)S(1)}, f32[4,40,512]{2,1,0:T(8,128)S(1)}, u32[]{:S(2)}, u32[]{:S(2)}) collective-permute-start(f32[4,40,512]{2,1,0:T(8,128)S(1)} %get-tuple-element.52), channel_id=1, source_target_pairs={{0,1},{1,0},{2,3},{3,2},{4,5},{5,4},{6,7},{7,6},{8,9},{9,8},{10,11... | collective-permute-start | bytes 983048 | tf_op jit(solution)/shard_map/ppermute | solution.py:42
  25.6 9.4 %collective-permute-start.10 = (bf16[40,2560]{1,0:T(8,128)(2,1)S(1)}, bf16[40,2560]{1,0:T(8,128)(2,1)S(1)}, u32[]{:S(2)}, u32[]{:S(2)}) collective-permute-start(bf16[40,2560]{1,0:T(8,128)(2,1)S(1)} %get-tuple-element.86), channel_id=1, source_target_pairs={{0,32},{32,0},{64,96},{96,64},{128,160},{160,128},{192,224},{224,1... | collective-permute-start | bytes 614408 | tf_op jit(solution)/shard_map/ppermute | solution.py:30
  25.9 11.9 %collective-permute-start.12 = (bf16[40,2560]{1,0:T(8,128)(2,1)S(1)}, bf16[40,2560]{1,0:T(8,128)(2,1)S(1)}, u32[]{:S(2)}, u32[]{:S(2)}) collective-permute-start(bf16[40,2560]{1,0:T(8,128)(2,1)S(1)} %get-tuple-element.86), channel_id=1, source_target_pairs={{0,192},{32,224},{64,0},{96,32},{128,64},{160,96},{192,128},{224,1... | collective-permute-start | bytes 614408 | tf_op jit(solution)/shard_map/ppermute | solution.py:30
  27.0 10.8 %collective-permute-start.11 = (bf16[40,2560]{1,0:T(8,128)(2,1)S(1)}, bf16[40,2560]{1,0:T(8,128)(2,1)S(1)}, u32[]{:S(2)}, u32[]{:S(2)}) collective-permute-start(bf16[40,2560]{1,0:T(8,128)(2,1)S(1)} %get-tuple-element.84), channel_id=1, source_target_pairs={{0,64},{32,96},{64,128},{96,160},{128,192},{160,224},{192,0},{224,... | collective-permute-start | bytes 614408 | tf_op jit(solution)/shard_map/ppermute | solution.py:30
  29.1 8.7 %collective-permute-start.13 = (bf16[40,2560]{1,0:T(8,128)(2,1)S(1)}, bf16[40,2560]{1,0:T(8,128)(2,1)S(1)}, u32[]{:S(2)}, u32[]{:S(2)}) collective-permute-start(bf16[40,2560]{1,0:T(8,128)(2,1)S(1)} %get-tuple-element.84), channel_id=1, source_target_pairs={{0,128},{32,160},{64,192},{96,224},{128,0},{160,32},{192,64},{224,... | collective-permute-start | bytes 614408 | tf_op jit(solution)/shard_map/ppermute | solution.py:30
  35.0 6.7 %collective-permute-start.14 = (f16[176,512]{1,0:T(8,128)(2,1)S(1)}, f16[176,512]{1,0:T(8,128)(2,1)S(1)}, u32[]{:S(2)}, u32[]{:S(2)}) collective-permute-start(f16[176,512]{1,0:T(8,128)(2,1)S(1)} %convert_element_type.16), channel_id=1, source_target_pairs={{0,1},{1,0},{2,3},{3,2},{4,5},{5,4},{6,7},{7,6},{8,9},{9,8},{10,11... | collective-permute-start | bytes 540680 | tf_op jit(solution)/shard_map/ppermute | solution.py:42
  41.9 7.8 %collective-permute-start.15 = (bf16[120,512]{1,0:T(8,128)(2,1)S(1)}, bf16[120,512]{1,0:T(8,128)(2,1)S(1)}, u32[]{:S(2)}, u32[]{:S(2)}) collective-permute-start(bf16[120,512]{1,0:T(8,128)(2,1)S(1)} %pad_maximum_fusion.refs_0_), channel_id=1, source_target_pairs={{0,4},{2,6},{4,8},{6,10},{8,12},{10,14},{12,16},{14,18},{16,20},{1... | collective-permute-start | bytes 368648 | tf_op jit(solution)/shard_map/ppermute | solution.py:34
  43.0 6.7 %collective-permute-start.16 = (bf16[120,512]{1,0:T(8,128)(2,1)S(1)}, bf16[120,512]{1,0:T(8,128)(2,1)S(1)}, u32[]{:S(2)}, u32[]{:S(2)}) collective-permute-start(bf16[120,512]{1,0:T(8,128)(2,1)S(1)} %pad_maximum_fusion.refs_0_), channel_id=1, source_target_pairs={{0,28},{2,30},{4,0},{6,2},{8,4},{10,6},{12,8},{14,10},{16,12},{18,... | collective-permute-start | bytes 368648 | tf_op jit(solution)/shard_map/ppermute | solution.py:34
  48.2 5.9 %collective-permute-start.25 = (bf16[120,512]{1,0:T(8,128)(2,1)S(1)}, bf16[120,512]{1,0:T(8,128)(2,1)S(1)}, u32[]{:S(2)}, u32[]{:S(2)}) collective-permute-start(bf16[120,512]{1,0:T(8,128)(2,1)S(1)} %pad_maximum_fusion.2.refs_0_), channel_id=1, source_target_pairs={{0,28},{2,30},{4,0},{6,2},{8,4},{10,6},{12,8},{14,10},{16,12},{18,... | collective-permute-start | bytes 368648 | tf_op jit(solution)/shard_map/ppermute | solution.py:34
  49.6 5.6 %collective-permute-start.29 = (bf16[120,512]{1,0:T(8,128)(2,1)S(1)}, bf16[120,512]{1,0:T(8,128)(2,1)S(1)}, u32[]{:S(2)}, u32[]{:S(2)}) collective-permute-start(bf16[120,512]{1,0:T(8,128)(2,1)S(1)} %pad_maximum_fusion.2.refs_0_), channel_id=1, source_target_pairs={{0,4},{2,6},{4,8},{6,10},{8,12},{10,14},{12,16},{14,18},{16,20},{1... | collective-permute-start | bytes 368648 | tf_op jit(solution)/shard_map/ppermute | solution.py:34
  50.8 7.3 %collective-permute-start.18 = (bf16[120,512]{1,0:T(8,128)(2,1)S(1)}, bf16[120,512]{1,0:T(8,128)(2,1)S(1)}, u32[]{:S(2)}, u32[]{:S(2)}) collective-permute-start(bf16[120,512]{1,0:T(8,128)(2,1)S(1)} %collective-permute-done.15.refs_1_), channel_id=1, source_target_pairs={{0,4},{2,6},{4,8},{6,10},{8,12},{10,14},{12,16},{14,18},{16,20},{1... | collective-permute-start | bytes 368648 | tf_op jit(solution)/shard_map/ppermute | solution.py:34
  50.9 7.2 %collective-permute-start.19 = (bf16[120,512]{1,0:T(8,128)(2,1)S(1)}, bf16[120,512]{1,0:T(8,128)(2,1)S(1)}, u32[]{:S(2)}, u32[]{:S(2)}) collective-permute-start(bf16[120,512]{1,0:T(8,128)(2,1)S(1)} %collective-permute-done.16.refs_2_), channel_id=1, source_target_pairs={{0,28},{2,30},{4,0},{6,2},{8,4},{10,6},{12,8},{14,10},{16,12},{18,... | collective-permute-start | bytes 368648 | tf_op jit(solution)/shard_map/ppermute | solution.py:34
  53.5 4.5 %collective-permute-start.20 = (bf16[2,40,512]{2,1,0:T(8,128)(2,1)S(1)}, bf16[2,40,512]{2,1,0:T(8,128)(2,1)S(1)}, u32[]{:S(2)}, u32[]{:S(2)}) collective-permute-start(bf16[2,40,512]{2,1,0:T(8,128)(2,1)S(1)} %pad_maximum_fusion.3), channel_id=1, source_target_pairs={{0,64},{32,96},{64,128},{96,160},{128,192},{160,224},{192,0},{224,... | collective-permute-start | bytes 245768 | tf_op jit(solution)/shard_map/ppermute | solution.py:30
  54.1 8.0 %collective-permute-start.26 = (bf16[120,512]{1,0:T(8,128)(2,1)S(1)}, bf16[120,512]{1,0:T(8,128)(2,1)S(1)}, u32[]{:S(2)}, u32[]{:S(2)}) collective-permute-start(bf16[120,512]{1,0:T(8,128)(2,1)S(1)} %collective-permute-done.25.refs_2_), channel_id=1, source_target_pairs={{0,28},{2,30},{4,0},{6,2},{8,4},{10,6},{12,8},{14,10},{16,12},{18,... | collective-permute-start | bytes 368648 | tf_op jit(solution)/shard_map/ppermute | solution.py:34
  55.2 7.7 %collective-permute-start.30 = (bf16[120,512]{1,0:T(8,128)(2,1)S(1)}, bf16[120,512]{1,0:T(8,128)(2,1)S(1)}, u32[]{:S(2)}, u32[]{:S(2)}) collective-permute-start(bf16[120,512]{1,0:T(8,128)(2,1)S(1)} %collective-permute-done.29.refs_1_), channel_id=1, source_target_pairs={{0,4},{2,6},{4,8},{6,10},{8,12},{10,14},{12,16},{14,18},{16,20},{1... | collective-permute-start | bytes 368648 | tf_op jit(solution)/shard_map/ppermute | solution.py:34
  58.0 7.7 %collective-permute-start.21 = (bf16[120,512]{1,0:T(8,128)(2,1)S(1)}, bf16[120,512]{1,0:T(8,128)(2,1)S(1)}, u32[]{:S(2)}, u32[]{:S(2)}) collective-permute-start(bf16[120,512]{1,0:T(8,128)(2,1)S(1)} %collective-permute-done.18.refs_3_), channel_id=1, source_target_pairs={{0,4},{2,6},{4,8},{6,10},{8,12},{10,14},{12,16},{14,18},{16,20},{1... | collective-permute-start | bytes 368648 | tf_op jit(solution)/shard_map/ppermute | solution.py:34
  58.1 7.7 %collective-permute-start.22 = (bf16[120,512]{1,0:T(8,128)(2,1)S(1)}, bf16[120,512]{1,0:T(8,128)(2,1)S(1)}, u32[]{:S(2)}, u32[]{:S(2)}) collective-permute-start(bf16[120,512]{1,0:T(8,128)(2,1)S(1)} %collective-permute-done.19.refs_4_), channel_id=1, source_target_pairs={{0,28},{2,30},{4,0},{6,2},{8,4},{10,6},{12,8},{14,10},{16,12},{18,... | collective-permute-start | bytes 368648 | tf_op jit(solution)/shard_map/ppermute | solution.py:34
  60.7 5.0 %collective-permute-start.23 = (bf16[2,40,512]{2,1,0:T(8,128)(2,1)S(1)}, bf16[2,40,512]{2,1,0:T(8,128)(2,1)S(1)}, u32[]{:S(2)}, u32[]{:S(2)}) collective-permute-start(bf16[2,40,512]{2,1,0:T(8,128)(2,1)S(1)} %pad_maximum_fusion.4), channel_id=1, source_target_pairs={{0,128},{32,160},{64,192},{96,224},{128,0},{160,32},{192,64},{224,... | collective-permute-start | bytes 245768 | tf_op jit(solution)/shard_map/ppermute | solution.py:30
  62.1 4.4 %collective-permute-start.27 = (bf16[120,512]{1,0:T(8,128)(2,1)S(1)}, bf16[120,512]{1,0:T(8,128)(2,1)S(1)}, u32[]{:S(2)}, u32[]{:S(2)}) collective-permute-start(bf16[120,512]{1,0:T(8,128)(2,1)S(1)} %collective-permute-done.26.refs_4_), channel_id=1, source_target_pairs={{0,28},{2,30},{4,0},{6,2},{8,4},{10,6},{12,8},{14,10},{16,12},{18,... | collective-permute-start | bytes 368648 | tf_op jit(solution)/shard_map/ppermute | solution.py:34
  63.0 6.2 %collective-permute-start.31 = (bf16[120,512]{1,0:T(8,128)(2,1)S(1)}, bf16[120,512]{1,0:T(8,128)(2,1)S(1)}, u32[]{:S(2)}, u32[]{:S(2)}) collective-permute-start(bf16[120,512]{1,0:T(8,128)(2,1)S(1)} %collective-permute-done.30.refs_3_), channel_id=1, source_target_pairs={{0,4},{2,6},{4,8},{6,10},{8,12},{10,14},{12,16},{14,18},{16,20},{1... | collective-permute-start | bytes 368648 | tf_op jit(solution)/shard_map/ppermute | solution.py:34
  65.8 4.9 %collective-permute-start.24 = (bf16[120,512]{1,0:T(8,128)(2,1)S(1)}, bf16[120,512]{1,0:T(8,128)(2,1)S(1)}, u32[]{:S(2)}, u32[]{:S(2)}) collective-permute-start(bf16[120,512]{1,0:T(8,128)(2,1)S(1)} %collective-permute-done.21.refs_5_), channel_id=1, source_target_pairs={{0,4},{2,6},{4,8},{6,10},{8,12},{10,14},{12,16},{14,18},{16,20},{1... | collective-permute-start | bytes 368648 | tf_op jit(solution)/shard_map/ppermute | solution.py:34
  66.5 9.8 %collective-permute-start.28 = (bf16[120,512]{1,0:T(8,128)(2,1)S(1)}, bf16[120,512]{1,0:T(8,128)(2,1)S(1)}, u32[]{:S(2)}, u32[]{:S(2)}) collective-permute-start(bf16[120,512]{1,0:T(8,128)(2,1)S(1)} %collective-permute-done.27.refs_6_), channel_id=1, source_target_pairs={{0,28},{2,30},{4,0},{6,2},{8,4},{10,6},{12,8},{14,10},{16,12},{18,... | collective-permute-start | bytes 368648 | tf_op jit(solution)/shard_map/ppermute | solution.py:34
  72.0 5.2 %collective-permute-start.33 = (f32[1,8]{1,0:T(1,128)S(1)}, f32[1,8]{1,0:T(1,128)S(1)}, u32[]{:S(2)}, u32[]{:S(2)}) collective-permute-start(f32[1,8]{1,0:T(1,128)S(1)} %get-tuple-element.82), channel_id=1, source_target_pairs={{0,224},{32,192},{64,32},{96,0},{128,96},{160,64},{192,160},{224,1... | collective-permute-start | bytes 104 | tf_op jit(solution)/shard_map/ppermute | solution.py:30
  (6 other events, 40.5 us)

commit v6 on v5

--- a/solution.py
+++ b/solution.py
@@ -325,7 +325,8 @@
         up_a, down_a, value = lax.optimization_barrier((up_a, down_a, rights[-1]))
         up_a, down_a = ring_step(step, up_a, down_a, first_blocks)
         value = occ_hop(value, *moves[step - 1])
-        up_a, down_a, value = lax.optimization_barrier((up_a, down_a, value))
+        if step < Z // 2 - 1:
+            up_a, down_a, value = lax.optimization_barrier((up_a, down_a, value))
         up_b, down_b = ring_step(step, up_b, down_b, second_blocks)
         rights[-1] = value
         if step == 1:

time: 106 us -> 103 us (0.972)
  blocking collectives: 27.5 us -> 26 us
  waiting for transfers between devices: 20.2 us -> 19.1 us
    ppermute x14, starting transfers between devices: 17 us -> 19.7 us  [z_hop(): lax.ppermute(value, 'cabs', [(c, (c // 2 + dz) % Z * 2 + c % 2) for c in...]
    ppermute x16, starting transfers between devices: 17.1 us -> 14.8 us  [occ_hop(): lax.ppermute(value, 'occ', [(o, partner(o, dy, flip)) for o in range(OCC)])]
    all_to_all x1, blocking collectives: 27.5 us -> 26 us  [shards(): lax.all_to_all(jnp.broadcast_to(row, (peers, OCC)), ('cabs', 'aux'), 0, 0...]
    ppermute x16, waiting for transfers between devices: 15.5 us -> 14.3 us  [occ_hop(): lax.ppermute(value, 'occ', [(o, partner(o, dy, flip)) for o in range(OCC)])]
  transfers between devices with their start and end apart: 34 -> 34, of which waited for: 12 -> 11; matrix products, arithmetic and copies ran while one was open for 1% -> 1% of each run, Pallas kernels for 10% -> 11%
where the time goes in v6:
time: 103 us
  starting transfers between devices  42 us (41%)
  blocking collectives  26 us (25%)
  waiting for transfers between devices  19.1 us (19%)
  Pallas kernels  10.9 us (11%)
  local copies, waits for them, and re-layouts  3.99 us (4%)
    all_to_all x1, blocking collectives, shards(): lax.all_to_all(jnp.broadcast_to(row, (peers, OCC)), ('cabs', 'aux'), 0, 0...  26 us
    ppermute x14, starting transfers between devices, z_hop(): lax.ppermute(value, 'cabs', [(c, (c // 2 + dz) % Z * 2 + c % 2) for c in...  19.7 us
    ppermute x16, starting transfers between devices, occ_hop(): lax.ppermute(value, 'occ', [(o, partner(o, dy, flip)) for o in range(OCC)])  14.8 us
    ppermute x16, waiting for transfers between devices, occ_hop(): lax.ppermute(value, 'occ', [(o, partner(o, dy, flip)) for o in range(OCC)])  14.3 us
    pallas_call x3, Pallas kernels, fit_sums(): pl.pallas_call(body, out_shape=shapes, in_specs=[SMEM] + [VMEM] * (count...  4.65 us
    ppermute x2, starting transfers between devices, aux_swap(): return lax.ppermute(value, 'aux', [(0, 1), (1, 0)])  4.24 us
    ppermute x2, starting transfers between devices, core_swap(): return lax.ppermute(value, 'cabs', [(c, c ^ 1) for c in range(2 * Z)])  3.24 us
    unnamed x8, local copies, waits for them, and re-layouts  3.12 us
  transfers between devices with their start and end apart: 34, of which 11 were waited for; matrix products, arithmetic and copies ran while one was open for 1% of the time, Pallas kernels for 11%

profile of v6, /device:TPU:1, one launch (start us, length us, event | category | flops | bytes accessed | tf_op | source)
XLA Modules:
  0.0 103.1 jit_solution(15107090320072086583)
XLA Ops:
  0.0 3.2 %collective-permute-start.4 = (bf16[4096,256]{1,0:T(8,128)(2,1)}, bf16[4096,256]{1,0:T(8,128)(2,1)S(1)}, u32[]{:S(2)}, u32[]{:S(2)}) collective-permute-start(bf16[4096,256]{1,0:T(8,128)(2,1)} %refs_1_.1), channel_id=1, source_target_pairs={{0,2},{2,0},{4,6},{6,4},{8,10},{10,8},{12,14},{14,12},{16,18},{18,... | collective-permute-start | bytes 6291464 | tf_op jit(solution)/shard_map/ppermute | solution.py:38
  3.3 1.1 %copy-done.2 = bf16[1,160,2560]{2,1,0:T(8,128)(2,1)S(1)} copy-done((bf16[1,160,2560]{2,1,0:T(8,128)(2,1)S(1)}, bf16[1,160,2560]{2,1,0:T(8,128)(2,1)}, u32[]{:S(2)}) %copy-start.2) | copy-done | bytes 819224
  6.1 2.0 %collective-permute-start.3 = (bf16[80,2560]{1,0:T(8,128)(2,1)S(1)}, bf16[80,2560]{1,0:T(8,128)(2,1)S(1)}, u32[]{:S(2)}, u32[]{:S(2)}) collective-permute-start(bf16[80,2560]{1,0:T(8,128)(2,1)S(1)} %shard_map.56.refs_0_), channel_id=1, source_target_pairs={{0,192},{32,224},{64,0},{96,32},{128,64},{160,96},{192,128},{224,1... | collective-permute-start | bytes 1228808 | tf_op jit(solution)/shard_map/ppermute | solution.py:30
  9.1 1.3 %copy-done.1 = bf16[1,256,2560]{2,1,0:T(8,128)(2,1)S(1)} copy-done((bf16[1,256,2560]{2,1,0:T(8,128)(2,1)S(1)}, bf16[1,256,2560]{2,1,0:T(8,128)(2,1)}, u32[]{:S(2)}) %copy-start.1) | copy-done | bytes 1310744
  11.1 2.0 %shard_map.55 = (bf16[2560,512]{1,0:T(8,128)(2,1)S(1)}, s32[8,512]{1,0:T(8,128)S(1)}) custom-call(s32[4]{0:T(128)S(1)} %pad_add_fusion.place_ref, s32[8]{0:T(128)S(1)} %copy-done.3, s32[8,512]{1,0:T(8,128)S(1)} %reshape.16.rows_ref, bf16[256,2560]{1,0:T(8,128)(2,1)S(1)} %bitcast.23, bf16[256,2560]{1,0:T(8,128)(2,1)} %collective-permute-done.other_ref), custom_call_target="tpu_custom_call" | custom-call | bytes 5242880 | tf_op jit(solution)/shard_map/pallas_call | solution.py:90
  13.1 2.8 %collective-permute-done.1.refs_1_ = bf16[80,2560]{1,0:T(8,128)(2,1)S(1)} collective-permute-done((bf16[80,2560]{1,0:T(8,128)(2,1)S(1)}, bf16[80,2560]{1,0:T(8,128)(2,1)S(1)}, u32[]{:S(2)}, u32[]{:S(2)}) %collective-permute-start.1) | collective-permute-done | bytes 409632 | tf_op jit(solution)/shard_map/ppermute | solution.py:30
  16.0 1.3 %collective-permute-done.2.refs_2_ = bf16[80,2560]{1,0:T(8,128)(2,1)} collective-permute-done((bf16[80,2560]{1,0:T(8,128)(2,1)S(1)}, bf16[80,2560]{1,0:T(8,128)(2,1)}, u32[]{:S(2)}, u32[]{:S(2)}) %collective-permute-start.2) | collective-permute-done | bytes 409632 | tf_op jit(solution)/shard_map/ppermute | solution.py:30
  17.3 1.1 %collective-permute-start.5 = (bf16[40,2560]{1,0:T(8,128)(2,1)S(1)}, bf16[40,2560]{1,0:T(8,128)(2,1)S(1)}, u32[]{:S(2)}, u32[]{:S(2)}) collective-permute-start(bf16[40,2560]{1,0:T(8,128)(2,1)S(1)} %get-tuple-element.81), channel_id=1, source_target_pairs={{0,32},{32,0},{64,96},{96,64},{128,160},{160,128},{192,224},{224,1... | collective-permute-start | bytes 614408 | tf_op jit(solution)/shard_map/ppermute | solution.py:30
  18.6 2.7 %collective-permute-start.7 = (bf16[40,2560]{1,0:T(8,128)(2,1)S(1)}, bf16[40,2560]{1,0:T(8,128)(2,1)S(1)}, u32[]{:S(2)}, u32[]{:S(2)}) collective-permute-start(bf16[40,2560]{1,0:T(8,128)(2,1)S(1)} %get-tuple-element.81), channel_id=1, source_target_pairs={{0,192},{32,224},{64,0},{96,32},{128,64},{160,96},{192,128},{224,1... | collective-permute-start | bytes 614408 | tf_op jit(solution)/shard_map/ppermute | solution.py:30
  22.0 2.1 %shard_map.57 = (f32[4,40,512]{2,1,0:T(8,128)S(1)}, f32[4,40,512]{2,1,0:T(8,128)S(1)}) custom-call(s32[4]{0:T(128)S(1)} %pad_add_fusion.place_ref, bf16[80,2560]{1,0:T(8,128)(2,1)S(1)} %shard_map.56.refs_0_, bf16[80,2560]{1,0:T(8,128)(2,1)S(1)} %collective-permute-done.1.refs_1_, bf16[80,2560]{1,0:T(8,128)(2,1)} %collective-permute-done.2.refs_2_, ...), custom_call_target="tpu_custom_call" | custom-call | flops 838860800 | bytes 5570560 | tf_op jit(solution)/shard_map/pallas_call | solution.py:145
  24.1 1.5 %collective-permute-start.9 = (f32[4,40,512]{2,1,0:T(8,128)S(1)}, f32[4,40,512]{2,1,0:T(8,128)S(1)}, u32[]{:S(2)}, u32[]{:S(2)}) collective-permute-start(f32[4,40,512]{2,1,0:T(8,128)S(1)} %get-tuple-element.50), channel_id=1, source_target_pairs={{0,1},{1,0},{2,3},{3,2},{4,5},{5,4},{6,7},{7,6},{8,9},{9,8},{10,11... | collective-permute-start | bytes 983048 | tf_op jit(solution)/shard_map/ppermute | solution.py:42
  25.9 1.1 %collective-permute-start.12 = (bf16[40,2560]{1,0:T(8,128)(2,1)S(1)}, bf16[40,2560]{1,0:T(8,128)(2,1)S(1)}, u32[]{:S(2)}, u32[]{:S(2)}) collective-permute-start(bf16[40,2560]{1,0:T(8,128)(2,1)S(1)} %get-tuple-element.82), channel_id=1, source_target_pairs={{0,192},{32,224},{64,0},{96,32},{128,64},{160,96},{192,128},{224,1... | collective-permute-start | bytes 614408 | tf_op jit(solution)/shard_map/ppermute | solution.py:30
  27.4 1.7 %collective-permute-done.8.refs_3_ = bf16[40,2560]{1,0:T(8,128)(2,1)S(1)} collective-permute-done((bf16[40,2560]{1,0:T(8,128)(2,1)S(1)}, bf16[40,2560]{1,0:T(8,128)(2,1)S(1)}, u32[]{:S(2)}, u32[]{:S(2)}) %collective-permute-start.8) | collective-permute-done | bytes 204832 | tf_op jit(solution)/shard_map/ppermute | solution.py:30
  29.6 1.4 %shard_map.59 = f32[176,512]{1,0:T(8,128)S(1)} custom-call(s32[4]{0:T(128)S(1)} %pad_add_fusion.place_ref, bf16[40,2560]{1,0:T(8,128)(2,1)S(1)} %collective-permute-done.5.refs_0_, bf16[40,2560]{1,0:T(8,128)(2,1)S(1)} %collective-permute-done.6.refs_1_, bf16[40,2560]{1,0:T(8,128)(2,1)S(1)} %collective-permute-done.7.refs_2_, ...), custom_call_target="tpu_custom_call" | custom-call | flops 503316480 | bytes 4096000 | tf_op jit(solution)/shard_map/pallas_call | solution.py:145
  31.0 4.0 %collective-permute-done.10.refs_0_ = bf16[40,2560]{1,0:T(8,128)(2,1)S(1)} collective-permute-done((bf16[40,2560]{1,0:T(8,128)(2,1)S(1)}, bf16[40,2560]{1,0:T(8,128)(2,1)S(1)}, u32[]{:S(2)}, u32[]{:S(2)}) %collective-permute-start.10) | collective-permute-done | bytes 204832 | tf_op jit(solution)/shard_map/ppermute | solution.py:30
  35.0 2.7 %collective-permute-start.14 = (f16[176,512]{1,0:T(8,128)(2,1)S(1)}, f16[176,512]{1,0:T(8,128)(2,1)S(1)}, u32[]{:S(2)}, u32[]{:S(2)}) collective-permute-start(f16[176,512]{1,0:T(8,128)(2,1)S(1)} %convert_element_type.16), channel_id=1, source_target_pairs={{0,1},{1,0},{2,3},{3,2},{4,5},{5,4},{6,7},{7,6},{8,9},{9,8},{10,11... | collective-permute-start | bytes 540680 | tf_op jit(solution)/shard_map/ppermute | solution.py:42
  37.8 1.2 %shard_map.58 = f32[4,40,512]{2,1,0:T(8,128)S(1)} custom-call(s32[4]{0:T(128)S(1)} %pad_add_fusion.place_ref, bf16[40,2560]{1,0:T(8,128)(2,1)S(1)} %collective-permute-done.10.refs_0_, bf16[40,2560]{1,0:T(8,128)(2,1)S(1)} %collective-permute-done.11.refs_1_, bf16[40,2560]{1,0:T(8,128)(2,1)S(1)} %collective-permute-done.12.refs_2_, ...), custom_call_target="tpu_custom_call" | custom-call | flops 503316480 | bytes 4096000 | tf_op jit(solution)/shard_map/pallas_call | solution.py:145
  39.1 2.6 %collective-permute-done.14 = f16[176,512]{1,0:T(8,128)(2,1)S(1)} collective-permute-done((f16[176,512]{1,0:T(8,128)(2,1)S(1)}, f16[176,512]{1,0:T(8,128)(2,1)S(1)}, u32[]{:S(2)}, u32[]{:S(2)}) %collective-permute-start.14) | collective-permute-done | bytes 180256 | tf_op jit(solution)/shard_map/ppermute | solution.py:42
  41.9 1.0 %collective-permute-start.15 = (bf16[120,512]{1,0:T(8,128)(2,1)S(1)}, bf16[120,512]{1,0:T(8,128)(2,1)S(1)}, u32[]{:S(2)}, u32[]{:S(2)}) collective-permute-start(bf16[120,512]{1,0:T(8,128)(2,1)S(1)} %pad_maximum_fusion.refs_0_), channel_id=1, source_target_pairs={{0,4},{2,6},{4,8},{6,10},{8,12},{10,14},{12,16},{14,18},{16,20},{1... | collective-permute-start | bytes 368648 | tf_op jit(solution)/shard_map/ppermute | solution.py:34
  43.0 4.0 %collective-permute-start.16 = (bf16[120,512]{1,0:T(8,128)(2,1)S(1)}, bf16[120,512]{1,0:T(8,128)(2,1)S(1)}, u32[]{:S(2)}, u32[]{:S(2)}) collective-permute-start(bf16[120,512]{1,0:T(8,128)(2,1)S(1)} %pad_maximum_fusion.refs_0_), channel_id=1, source_target_pairs={{0,28},{2,30},{4,0},{6,2},{8,4},{10,6},{12,8},{14,10},{16,12},{18,... | collective-permute-start | bytes 368648 | tf_op jit(solution)/shard_map/ppermute | solution.py:34
  47.0 1.2 %collective-permute-start.17 = (bf16[3,40,512]{2,1,0:T(8,128)(2,1)S(1)}, bf16[3,40,512]{2,1,0:T(8,128)(2,1)S(1)}, u32[]{:S(2)}, u32[]{:S(2)}) collective-permute-start(bf16[3,40,512]{2,1,0:T(8,128)(2,1)S(1)} %pad_maximum_fusion.1), channel_id=1, source_target_pairs={{0,32},{32,0},{64,96},{96,64},{128,160},{160,128},{192,224},{224,1... | collective-permute-start | bytes 368648 | tf_op jit(solution)/shard_map/ppermute | solution.py:30
  48.2 1.5 %collective-permute-start.24 = (bf16[120,512]{1,0:T(8,128)(2,1)S(1)}, bf16[120,512]{1,0:T(8,128)(2,1)S(1)}, u32[]{:S(2)}, u32[]{:S(2)}) collective-permute-start(bf16[120,512]{1,0:T(8,128)(2,1)S(1)} %pad_maximum_fusion.2.refs_0_), channel_id=1, source_target_pairs={{0,28},{2,30},{4,0},{6,2},{8,4},{10,6},{12,8},{14,10},{16,12},{18,... | collective-permute-start | bytes 368648 | tf_op jit(solution)/shard_map/ppermute | solution.py:34
  50.9 2.7 %collective-permute-start.19 = (bf16[120,512]{1,0:T(8,128)(2,1)S(1)}, bf16[120,512]{1,0:T(8,128)(2,1)S(1)}, u32[]{:S(2)}, u32[]{:S(2)}) collective-permute-start(bf16[120,512]{1,0:T(8,128)(2,1)S(1)} %collective-permute-done.16.refs_2_), channel_id=1, source_target_pairs={{0,28},{2,30},{4,0},{6,2},{8,4},{10,6},{12,8},{14,10},{16,12},{18,... | collective-permute-start | bytes 368648 | tf_op jit(solution)/shard_map/ppermute | solution.py:34
  55.5 2.5 %collective-permute-done.20.refs_11_ = bf16[2,40,512]{2,1,0:T(8,128)(2,1)S(1)} collective-permute-done((bf16[2,40,512]{2,1,0:T(8,128)(2,1)S(1)}, bf16[2,40,512]{2,1,0:T(8,128)(2,1)S(1)}, u32[]{:S(2)}, u32[]{:S(2)}) %collective-permute-start.20) | collective-permute-done | bytes 81952 | tf_op jit(solution)/shard_map/ppermute | solution.py:30
  58.1 1.1 %collective-permute-done.25.refs_4_ = bf16[120,512]{1,0:T(8,128)(2,1)S(1)} collective-permute-done((bf16[120,512]{1,0:T(8,128)(2,1)S(1)}, bf16[120,512]{1,0:T(8,128)(2,1)S(1)}, u32[]{:S(2)}, u32[]{:S(2)}) %collective-permute-start.25) | collective-permute-done | bytes 122912 | tf_op jit(solution)/shard_map/ppermute | solution.py:34
  59.2 3.4 %collective-permute-start.26 = (bf16[120,512]{1,0:T(8,128)(2,1)S(1)}, bf16[120,512]{1,0:T(8,128)(2,1)S(1)}, u32[]{:S(2)}, u32[]{:S(2)}) collective-permute-start(bf16[120,512]{1,0:T(8,128)(2,1)S(1)} %collective-permute-done.25.refs_4_), channel_id=1, source_target_pairs={{0,28},{2,30},{4,0},{6,2},{8,4},{10,6},{12,8},{14,10},{16,12},{18,... | collective-permute-start | bytes 368648 | tf_op jit(solution)/shard_map/ppermute | solution.py:34
  62.6 2.7 %collective-permute-start.22 = (bf16[120,512]{1,0:T(8,128)(2,1)S(1)}, bf16[120,512]{1,0:T(8,128)(2,1)S(1)}, u32[]{:S(2)}, u32[]{:S(2)}) collective-permute-start(bf16[120,512]{1,0:T(8,128)(2,1)S(1)} %collective-permute-done.19.refs_4_), channel_id=1, source_target_pairs={{0,28},{2,30},{4,0},{6,2},{8,4},{10,6},{12,8},{14,10},{16,12},{18,... | collective-permute-start | bytes 368648 | tf_op jit(solution)/shard_map/ppermute | solution.py:34
  65.3 3.4 %collective-permute-start.27 = (bf16[120,512]{1,0:T(8,128)(2,1)S(1)}, bf16[120,512]{1,0:T(8,128)(2,1)S(1)}, u32[]{:S(2)}, u32[]{:S(2)}) collective-permute-start(bf16[120,512]{1,0:T(8,128)(2,1)S(1)} %collective-permute-done.26.refs_6_), channel_id=1, source_target_pairs={{0,28},{2,30},{4,0},{6,2},{8,4},{10,6},{12,8},{14,10},{16,12},{18,... | collective-permute-start | bytes 368648 | tf_op jit(solution)/shard_map/ppermute | solution.py:34
  68.7 1.7 %collective-permute-start.31 = (bf16[2,40,512]{2,1,0:T(8,128)(2,1)S(1)}, bf16[2,40,512]{2,1,0:T(8,128)(2,1)S(1)}, u32[]{:S(2)}, u32[]{:S(2)}) collective-permute-start(bf16[2,40,512]{2,1,0:T(8,128)(2,1)S(1)} %pad_maximum_fusion.4), channel_id=1, source_target_pairs={{0,128},{32,160},{64,192},{96,224},{128,0},{160,32},{192,64},{224,... | collective-permute-start | bytes 245768 | tf_op jit(solution)/shard_map/ppermute | solution.py:30
  70.4 1.2 %shard_map.61.refs_3_ = f32[120,512]{1,0:T(8,128)S(1)} custom-call(s32[4]{0:T(128)S(1)} %pad_add_fusion.place_ref, bf16[120,512]{1,0:T(8,128)(2,1)S(1)} %pad_maximum_fusion.2.refs_0_, bf16[120,512]{1,0:T(8,128)(2,1)S(1)} %collective-permute-done.28.refs_1_, bf16[120,512]{1,0:T(8,128)(2,1)S(1)} %collective-permute-done.24.refs_2_, ...), custom_call_target="tpu_custom_call" | custom-call | flops 440401920 | bytes 4530176 | tf_op jit(solution)/shard_map/pallas_call | solution.py:193
  71.6 1.4 %shard_map.60 = (f32[1,8]{1,0:T(1,128)S(1)}, f32[1,8]{1,0:T(1,128)S(1)}, f32[1,8]{1,0:T(1,128)S(1)}) custom-call(s32[4]{0:T(128)S(1)} %pad_add_fusion.place_ref, bf16[120,512]{1,0:T(8,128)(2,1)S(1)} %pad_maximum_fusion.refs_0_, bf16[120,512]{1,0:T(8,128)(2,1)S(1)} %collective-permute-done.15.refs_1_, bf16[120,512]{1,0:T(8,128)(2,1)S(1)} %collective-permute-done.16.refs_2_, ...), custom_call_target="tpu_custom_call" | custom-call | flops 503316480 | bytes 5545984 | tf_op jit(solution)/shard_map/pallas_call | solution.py:246
  76.5 26.0 %all_to_all.6 = f32[32,1,8]{2,1,0:T(1,128)S(1)} all-to-all(f32[32,1,8]{2,1,0:T(1,128)S(1)} %broadcast_in_dim.25), channel_id=1, replica_groups=mesh['occ'=8,'cabs'=16,'aux'=2] {'cabs','aux'}, dimensions={0} | all-to-all | bytes 2048 | tf_op jit(solution)/shard_map/all_to_all | solution.py:347
  (73 shorter events, 13.3 us)
Async XLA Ops:
  0.0 17.3 %collective-permute-start.4 = (bf16[4096,256]{1,0:T(8,128)(2,1)}, bf16[4096,256]{1,0:T(8,128)(2,1)S(1)}, u32[]{:S(2)}, u32[]{:S(2)}) collective-permute-start(bf16[4096,256]{1,0:T(8,128)(2,1)} %refs_1_.1), channel_id=1, source_target_pairs={{0,2},{2,0},{4,6},{6,4},{8,10},{10,8},{12,14},{14,12},{16,18},{18,... | collective-permute-start | bytes 6291464 | tf_op jit(solution)/shard_map/ppermute | solution.py:38
  3.2 5.9 %collective-permute-start = (bf16[256,2560]{1,0:T(8,128)(2,1)}, bf16[256,2560]{1,0:T(8,128)(2,1)}, u32[]{:S(2)}, u32[]{:S(2)}) collective-permute-start(bf16[256,2560]{1,0:T(8,128)(2,1)} %bitcast.22), channel_id=1, source_target_pairs={{0,2},{2,0},{4,6},{6,4},{8,10},{10,8},{12,14},{14,12},{16,18},{18,... | collective-permute-start | bytes 3932168 | tf_op jit(solution)/shard_map/ppermute | solution.py:38
  5.2 10.7 %collective-permute-start.1 = (bf16[80,2560]{1,0:T(8,128)(2,1)S(1)}, bf16[80,2560]{1,0:T(8,128)(2,1)S(1)}, u32[]{:S(2)}, u32[]{:S(2)}) collective-permute-start(bf16[80,2560]{1,0:T(8,128)(2,1)S(1)} %shard_map.56.refs_0_), channel_id=1, source_target_pairs={{0,32},{32,0},{64,96},{96,64},{128,160},{160,128},{192,224},{224,1... | collective-permute-start | bytes 1228808 | tf_op jit(solution)/shard_map/ppermute | solution.py:30
  5.3 11.9 %collective-permute-start.2 = (bf16[80,2560]{1,0:T(8,128)(2,1)S(1)}, bf16[80,2560]{1,0:T(8,128)(2,1)}, u32[]{:S(2)}, u32[]{:S(2)}) collective-permute-start(bf16[80,2560]{1,0:T(8,128)(2,1)S(1)} %shard_map.56.refs_0_), channel_id=1, source_target_pairs={{0,64},{32,96},{64,128},{96,160},{128,192},{160,224},{192,0},{224,... | collective-permute-start | bytes 1228808 | tf_op jit(solution)/shard_map/ppermute | solution.py:30
  6.1 11.2 %collective-permute-start.3 = (bf16[80,2560]{1,0:T(8,128)(2,1)S(1)}, bf16[80,2560]{1,0:T(8,128)(2,1)S(1)}, u32[]{:S(2)}, u32[]{:S(2)}) collective-permute-start(bf16[80,2560]{1,0:T(8,128)(2,1)S(1)} %shard_map.56.refs_0_), channel_id=1, source_target_pairs={{0,192},{32,224},{64,0},{96,32},{128,64},{160,96},{192,128},{224,1... | collective-permute-start | bytes 1228808 | tf_op jit(solution)/shard_map/ppermute | solution.py:30
  17.3 8.3 %collective-permute-start.5 = (bf16[40,2560]{1,0:T(8,128)(2,1)S(1)}, bf16[40,2560]{1,0:T(8,128)(2,1)S(1)}, u32[]{:S(2)}, u32[]{:S(2)}) collective-permute-start(bf16[40,2560]{1,0:T(8,128)(2,1)S(1)} %get-tuple-element.81), channel_id=1, source_target_pairs={{0,32},{32,0},{64,96},{96,64},{128,160},{160,128},{192,224},{224,1... | collective-permute-start | bytes 614408 | tf_op jit(solution)/shard_map/ppermute | solution.py:30
  18.5 7.4 %collective-permute-start.6 = (bf16[40,2560]{1,0:T(8,128)(2,1)S(1)}, bf16[40,2560]{1,0:T(8,128)(2,1)S(1)}, u32[]{:S(2)}, u32[]{:S(2)}) collective-permute-start(bf16[40,2560]{1,0:T(8,128)(2,1)S(1)} %get-tuple-element.79), channel_id=1, source_target_pairs={{0,64},{32,96},{64,128},{96,160},{128,192},{160,224},{192,0},{224,... | collective-permute-start | bytes 614408 | tf_op jit(solution)/shard_map/ppermute | solution.py:30
  18.6 8.4 %collective-permute-start.7 = (bf16[40,2560]{1,0:T(8,128)(2,1)S(1)}, bf16[40,2560]{1,0:T(8,128)(2,1)S(1)}, u32[]{:S(2)}, u32[]{:S(2)}) collective-permute-start(bf16[40,2560]{1,0:T(8,128)(2,1)S(1)} %get-tuple-element.81), channel_id=1, source_target_pairs={{0,192},{32,224},{64,0},{96,32},{128,64},{160,96},{192,128},{224,1... | collective-permute-start | bytes 614408 | tf_op jit(solution)/shard_map/ppermute | solution.py:30
  21.2 7.9 %collective-permute-start.8 = (bf16[40,2560]{1,0:T(8,128)(2,1)S(1)}, bf16[40,2560]{1,0:T(8,128)(2,1)S(1)}, u32[]{:S(2)}, u32[]{:S(2)}) collective-permute-start(bf16[40,2560]{1,0:T(8,128)(2,1)S(1)} %get-tuple-element.79), channel_id=1, source_target_pairs={{0,128},{32,160},{64,192},{96,224},{128,0},{160,32},{192,64},{224,... | collective-permute-start | bytes 614408 | tf_op jit(solution)/shard_map/ppermute | solution.py:30
  24.1 13.7 %collective-permute-start.9 = (f32[4,40,512]{2,1,0:T(8,128)S(1)}, f32[4,40,512]{2,1,0:T(8,128)S(1)}, u32[]{:S(2)}, u32[]{:S(2)}) collective-permute-start(f32[4,40,512]{2,1,0:T(8,128)S(1)} %get-tuple-element.50), channel_id=1, source_target_pairs={{0,1},{1,0},{2,3},{3,2},{4,5},{5,4},{6,7},{7,6},{8,9},{9,8},{10,11... | collective-permute-start | bytes 983048 | tf_op jit(solution)/shard_map/ppermute | solution.py:42
  25.6 9.4 %collective-permute-start.10 = (bf16[40,2560]{1,0:T(8,128)(2,1)S(1)}, bf16[40,2560]{1,0:T(8,128)(2,1)S(1)}, u32[]{:S(2)}, u32[]{:S(2)}) collective-permute-start(bf16[40,2560]{1,0:T(8,128)(2,1)S(1)} %get-tuple-element.82), channel_id=1, source_target_pairs={{0,32},{32,0},{64,96},{96,64},{128,160},{160,128},{192,224},{224,1... | collective-permute-start | bytes 614408 | tf_op jit(solution)/shard_map/ppermute | solution.py:30
  25.9 11.9 %collective-permute-start.12 = (bf16[40,2560]{1,0:T(8,128)(2,1)S(1)}, bf16[40,2560]{1,0:T(8,128)(2,1)S(1)}, u32[]{:S(2)}, u32[]{:S(2)}) collective-permute-start(bf16[40,2560]{1,0:T(8,128)(2,1)S(1)} %get-tuple-element.82), channel_id=1, source_target_pairs={{0,192},{32,224},{64,0},{96,32},{128,64},{160,96},{192,128},{224,1... | collective-permute-start | bytes 614408 | tf_op jit(solution)/shard_map/ppermute | solution.py:30
  27.0 10.8 %collective-permute-start.11 = (bf16[40,2560]{1,0:T(8,128)(2,1)S(1)}, bf16[40,2560]{1,0:T(8,128)(2,1)S(1)}, u32[]{:S(2)}, u32[]{:S(2)}) collective-permute-start(bf16[40,2560]{1,0:T(8,128)(2,1)S(1)} %get-tuple-element.80), channel_id=1, source_target_pairs={{0,64},{32,96},{64,128},{96,160},{128,192},{160,224},{192,0},{224,... | collective-permute-start | bytes 614408 | tf_op jit(solution)/shard_map/ppermute | solution.py:30
  29.1 8.7 %collective-permute-start.13 = (bf16[40,2560]{1,0:T(8,128)(2,1)S(1)}, bf16[40,2560]{1,0:T(8,128)(2,1)S(1)}, u32[]{:S(2)}, u32[]{:S(2)}) collective-permute-start(bf16[40,2560]{1,0:T(8,128)(2,1)S(1)} %get-tuple-element.80), channel_id=1, source_target_pairs={{0,128},{32,160},{64,192},{96,224},{128,0},{160,32},{192,64},{224,... | collective-permute-start | bytes 614408 | tf_op jit(solution)/shard_map/ppermute | solution.py:30
  35.0 6.7 %collective-permute-start.14 = (f16[176,512]{1,0:T(8,128)(2,1)S(1)}, f16[176,512]{1,0:T(8,128)(2,1)S(1)}, u32[]{:S(2)}, u32[]{:S(2)}) collective-permute-start(f16[176,512]{1,0:T(8,128)(2,1)S(1)} %convert_element_type.16), channel_id=1, source_target_pairs={{0,1},{1,0},{2,3},{3,2},{4,5},{5,4},{6,7},{7,6},{8,9},{9,8},{10,11... | collective-permute-start | bytes 540680 | tf_op jit(solution)/shard_map/ppermute | solution.py:42
  41.9 7.8 %collective-permute-start.15 = (bf16[120,512]{1,0:T(8,128)(2,1)S(1)}, bf16[120,512]{1,0:T(8,128)(2,1)S(1)}, u32[]{:S(2)}, u32[]{:S(2)}) collective-permute-start(bf16[120,512]{1,0:T(8,128)(2,1)S(1)} %pad_maximum_fusion.refs_0_), channel_id=1, source_target_pairs={{0,4},{2,6},{4,8},{6,10},{8,12},{10,14},{12,16},{14,18},{16,20},{1... | collective-permute-start | bytes 368648 | tf_op jit(solution)/shard_map/ppermute | solution.py:34
  43.0 6.7 %collective-permute-start.16 = (bf16[120,512]{1,0:T(8,128)(2,1)S(1)}, bf16[120,512]{1,0:T(8,128)(2,1)S(1)}, u32[]{:S(2)}, u32[]{:S(2)}) collective-permute-start(bf16[120,512]{1,0:T(8,128)(2,1)S(1)} %pad_maximum_fusion.refs_0_), channel_id=1, source_target_pairs={{0,28},{2,30},{4,0},{6,2},{8,4},{10,6},{12,8},{14,10},{16,12},{18,... | collective-permute-start | bytes 368648 | tf_op jit(solution)/shard_map/ppermute | solution.py:34
  47.0 3.7 %collective-permute-start.17 = (bf16[3,40,512]{2,1,0:T(8,128)(2,1)S(1)}, bf16[3,40,512]{2,1,0:T(8,128)(2,1)S(1)}, u32[]{:S(2)}, u32[]{:S(2)}) collective-permute-start(bf16[3,40,512]{2,1,0:T(8,128)(2,1)S(1)} %pad_maximum_fusion.1), channel_id=1, source_target_pairs={{0,32},{32,0},{64,96},{96,64},{128,160},{160,128},{192,224},{224,1... | collective-permute-start | bytes 368648 | tf_op jit(solution)/shard_map/ppermute | solution.py:30
  48.2 5.9 %collective-permute-start.24 = (bf16[120,512]{1,0:T(8,128)(2,1)S(1)}, bf16[120,512]{1,0:T(8,128)(2,1)S(1)}, u32[]{:S(2)}, u32[]{:S(2)}) collective-permute-start(bf16[120,512]{1,0:T(8,128)(2,1)S(1)} %pad_maximum_fusion.2.refs_0_), channel_id=1, source_target_pairs={{0,28},{2,30},{4,0},{6,2},{8,4},{10,6},{12,8},{14,10},{16,12},{18,... | collective-permute-start | bytes 368648 | tf_op jit(solution)/shard_map/ppermute | solution.py:34
  49.6 5.6 %collective-permute-start.28 = (bf16[120,512]{1,0:T(8,128)(2,1)S(1)}, bf16[120,512]{1,0:T(8,128)(2,1)S(1)}, u32[]{:S(2)}, u32[]{:S(2)}) collective-permute-start(bf16[120,512]{1,0:T(8,128)(2,1)S(1)} %pad_maximum_fusion.2.refs_0_), channel_id=1, source_target_pairs={{0,4},{2,6},{4,8},{6,10},{8,12},{10,14},{12,16},{14,18},{16,20},{1... | collective-permute-start | bytes 368648 | tf_op jit(solution)/shard_map/ppermute | solution.py:34
  50.8 7.3 %collective-permute-start.18 = (bf16[120,512]{1,0:T(8,128)(2,1)S(1)}, bf16[120,512]{1,0:T(8,128)(2,1)S(1)}, u32[]{:S(2)}, u32[]{:S(2)}) collective-permute-start(bf16[120,512]{1,0:T(8,128)(2,1)S(1)} %collective-permute-done.15.refs_1_), channel_id=1, source_target_pairs={{0,4},{2,6},{4,8},{6,10},{8,12},{10,14},{12,16},{14,18},{16,20},{1... | collective-permute-start | bytes 368648 | tf_op jit(solution)/shard_map/ppermute | solution.py:34
  50.9 7.2 %collective-permute-start.19 = (bf16[120,512]{1,0:T(8,128)(2,1)S(1)}, bf16[120,512]{1,0:T(8,128)(2,1)S(1)}, u32[]{:S(2)}, u32[]{:S(2)}) collective-permute-start(bf16[120,512]{1,0:T(8,128)(2,1)S(1)} %collective-permute-done.16.refs_2_), channel_id=1, source_target_pairs={{0,28},{2,30},{4,0},{6,2},{8,4},{10,6},{12,8},{14,10},{16,12},{18,... | collective-permute-start | bytes 368648 | tf_op jit(solution)/shard_map/ppermute | solution.py:34
  53.5 4.5 %collective-permute-start.20 = (bf16[2,40,512]{2,1,0:T(8,128)(2,1)S(1)}, bf16[2,40,512]{2,1,0:T(8,128)(2,1)S(1)}, u32[]{:S(2)}, u32[]{:S(2)}) collective-permute-start(bf16[2,40,512]{2,1,0:T(8,128)(2,1)S(1)} %pad_maximum_fusion.3), channel_id=1, source_target_pairs={{0,64},{32,96},{64,128},{96,160},{128,192},{160,224},{192,0},{224,... | collective-permute-start | bytes 245768 | tf_op jit(solution)/shard_map/ppermute | solution.py:30
  54.1 5.2 %collective-permute-start.25 = (bf16[120,512]{1,0:T(8,128)(2,1)S(1)}, bf16[120,512]{1,0:T(8,128)(2,1)S(1)}, u32[]{:S(2)}, u32[]{:S(2)}) collective-permute-start(bf16[120,512]{1,0:T(8,128)(2,1)S(1)} %collective-permute-done.24.refs_2_), channel_id=1, source_target_pairs={{0,28},{2,30},{4,0},{6,2},{8,4},{10,6},{12,8},{14,10},{16,12},{18,... | collective-permute-start | bytes 368648 | tf_op jit(solution)/shard_map/ppermute | solution.py:34
  55.2 7.4 %collective-permute-start.29 = (bf16[120,512]{1,0:T(8,128)(2,1)S(1)}, bf16[120,512]{1,0:T(8,128)(2,1)S(1)}, u32[]{:S(2)}, u32[]{:S(2)}) collective-permute-start(bf16[120,512]{1,0:T(8,128)(2,1)S(1)} %collective-permute-done.28.refs_1_), channel_id=1, source_target_pairs={{0,4},{2,6},{4,8},{6,10},{8,12},{10,14},{12,16},{14,18},{16,20},{1... | collective-permute-start | bytes 368648 | tf_op jit(solution)/shard_map/ppermute | solution.py:34
  58.0 7.3 %collective-permute-start.21 = (bf16[120,512]{1,0:T(8,128)(2,1)S(1)}, bf16[120,512]{1,0:T(8,128)(2,1)S(1)}, u32[]{:S(2)}, u32[]{:S(2)}) collective-permute-start(bf16[120,512]{1,0:T(8,128)(2,1)S(1)} %collective-permute-done.18.refs_3_), channel_id=1, source_target_pairs={{0,4},{2,6},{4,8},{6,10},{8,12},{10,14},{12,16},{14,18},{16,20},{1... | collective-permute-start | bytes 368648 | tf_op jit(solution)/shard_map/ppermute | solution.py:34
  59.2 6.1 %collective-permute-start.26 = (bf16[120,512]{1,0:T(8,128)(2,1)S(1)}, bf16[120,512]{1,0:T(8,128)(2,1)S(1)}, u32[]{:S(2)}, u32[]{:S(2)}) collective-permute-start(bf16[120,512]{1,0:T(8,128)(2,1)S(1)} %collective-permute-done.25.refs_4_), channel_id=1, source_target_pairs={{0,28},{2,30},{4,0},{6,2},{8,4},{10,6},{12,8},{14,10},{16,12},{18,... | collective-permute-start | bytes 368648 | tf_op jit(solution)/shard_map/ppermute | solution.py:34
  62.6 7.8 %collective-permute-start.30 = (bf16[120,512]{1,0:T(8,128)(2,1)S(1)}, bf16[120,512]{1,0:T(8,128)(2,1)S(1)}, u32[]{:S(2)}, u32[]{:S(2)}) collective-permute-start(bf16[120,512]{1,0:T(8,128)(2,1)S(1)} %collective-permute-done.29.refs_3_), channel_id=1, source_target_pairs={{0,4},{2,6},{4,8},{6,10},{8,12},{10,14},{12,16},{14,18},{16,20},{1... | collective-permute-start | bytes 368648 | tf_op jit(solution)/shard_map/ppermute | solution.py:34
  62.6 9.0 %collective-permute-start.22 = (bf16[120,512]{1,0:T(8,128)(2,1)S(1)}, bf16[120,512]{1,0:T(8,128)(2,1)S(1)}, u32[]{:S(2)}, u32[]{:S(2)}) collective-permute-start(bf16[120,512]{1,0:T(8,128)(2,1)S(1)} %collective-permute-done.19.refs_4_), channel_id=1, source_target_pairs={{0,28},{2,30},{4,0},{6,2},{8,4},{10,6},{12,8},{14,10},{16,12},{18,... | collective-permute-start | bytes 368648 | tf_op jit(solution)/shard_map/ppermute | solution.py:34
  65.3 6.3 %collective-permute-start.23 = (bf16[120,512]{1,0:T(8,128)(2,1)S(1)}, bf16[120,512]{1,0:T(8,128)(2,1)S(1)}, u32[]{:S(2)}, u32[]{:S(2)}) collective-permute-start(bf16[120,512]{1,0:T(8,128)(2,1)S(1)} %collective-permute-done.21.refs_5_), channel_id=1, source_target_pairs={{0,4},{2,6},{4,8},{6,10},{8,12},{10,14},{12,16},{14,18},{16,20},{1... | collective-permute-start | bytes 368648 | tf_op jit(solution)/shard_map/ppermute | solution.py:34
  65.3 9.3 %collective-permute-start.27 = (bf16[120,512]{1,0:T(8,128)(2,1)S(1)}, bf16[120,512]{1,0:T(8,128)(2,1)S(1)}, u32[]{:S(2)}, u32[]{:S(2)}) collective-permute-start(bf16[120,512]{1,0:T(8,128)(2,1)S(1)} %collective-permute-done.26.refs_6_), channel_id=1, source_target_pairs={{0,28},{2,30},{4,0},{6,2},{8,4},{10,6},{12,8},{14,10},{16,12},{18,... | collective-permute-start | bytes 368648 | tf_op jit(solution)/shard_map/ppermute | solution.py:34
  68.7 5.9 %collective-permute-start.31 = (bf16[2,40,512]{2,1,0:T(8,128)(2,1)S(1)}, bf16[2,40,512]{2,1,0:T(8,128)(2,1)S(1)}, u32[]{:S(2)}, u32[]{:S(2)}) collective-permute-start(bf16[2,40,512]{2,1,0:T(8,128)(2,1)S(1)} %pad_maximum_fusion.4), channel_id=1, source_target_pairs={{0,128},{32,160},{64,192},{96,224},{128,0},{160,32},{192,64},{224,... | collective-permute-start | bytes 245768 | tf_op jit(solution)/shard_map/ppermute | solution.py:30
  (6 other events, 40.6 us)

commit v7 on v5

--- a/solution.py
+++ b/solution.py
@@ -325,8 +325,9 @@
         up_a, down_a, value = lax.optimization_barrier((up_a, down_a, rights[-1]))
         up_a, down_a = ring_step(step, up_a, down_a, first_blocks)
         value = occ_hop(value, *moves[step - 1])
-        up_a, down_a, value = lax.optimization_barrier((up_a, down_a, value))
         up_b, down_b = ring_step(step, up_b, down_b, second_blocks)
+        if step < Z // 2 - 1:
+            up_b, down_b, value = lax.optimization_barrier((up_b, down_b, value))
         rights[-1] = value
         if step == 1:
             rights.append(jnp.stack([near[3], value[1]]))

time: 106 us -> 109 us (1.028)
  starting transfers between devices: 41.6 us -> 46 us
  waiting for transfers between devices: 20.2 us -> 17.9 us
    ppermute x14, starting transfers between devices: 17 us -> 23 us  [z_hop(): lax.ppermute(value, 'cabs', [(c, (c // 2 + dz) % Z * 2 + c % 2) for c in...]
    ppermute x16, waiting for transfers between devices: 15.5 us -> 11.8 us  [occ_hop(): lax.ppermute(value, 'occ', [(o, partner(o, dy, flip)) for o in range(OCC)])]
    ppermute x16, starting transfers between devices: 17.1 us -> 15.5 us  [occ_hop(): lax.ppermute(value, 'occ', [(o, partner(o, dy, flip)) for o in range(OCC)])]
    ppermute x14, waiting for transfers between devices: 1.76 us -> 3.22 us  [z_hop(): lax.ppermute(value, 'cabs', [(c, (c // 2 + dz) % Z * 2 + c % 2) for c in...]
  transfers between devices with their start and end apart: 34 -> 34, of which waited for: 12 -> 10; matrix products, arithmetic and copies ran while one was open for 1% -> 1% of each run, Pallas kernels for 10% -> 10%
where the time goes in v7:
time: 109 us; the launch traced here: 108 us
  starting transfers between devices  46 us (42%)
  blocking collectives  28.4 us (26%)
  waiting for transfers between devices  17.9 us (16%)
  Pallas kernels  10.9 us (10%)
  local copies, waits for them, and re-layouts  4 us (4%)
    all_to_all x1, blocking collectives, shards(): lax.all_to_all(jnp.broadcast_to(row, (peers, OCC)), ('cabs', 'aux'), 0, 0...  28.4 us
    ppermute x14, starting transfers between devices, z_hop(): lax.ppermute(value, 'cabs', [(c, (c // 2 + dz) % Z * 2 + c % 2) for c in...  23 us
    ppermute x16, starting transfers between devices, occ_hop(): lax.ppermute(value, 'occ', [(o, partner(o, dy, flip)) for o in range(OCC)])  15.5 us
    ppermute x16, waiting for transfers between devices, occ_hop(): lax.ppermute(value, 'occ', [(o, partner(o, dy, flip)) for o in range(OCC)])  11.8 us
    pallas_call x3, Pallas kernels, fit_sums(): pl.pallas_call(body, out_shape=shapes, in_specs=[SMEM] + [VMEM] * (count...  4.65 us
    ppermute x2, starting transfers between devices, aux_swap(): return lax.ppermute(value, 'aux', [(0, 1), (1, 0)])  4.24 us
    ppermute x2, starting transfers between devices, core_swap(): return lax.ppermute(value, 'cabs', [(c, c ^ 1) for c in range(2 * Z)])  3.24 us
    ppermute x14, waiting for transfers between devices, z_hop(): lax.ppermute(value, 'cabs', [(c, (c // 2 + dz) % Z * 2 + c % 2) for c in...  3.22 us
  transfers between devices with their start and end apart: 34, of which 10 were waited for; matrix products, arithmetic and copies ran while one was open for 1% of the time, Pallas kernels for 10%

profile of v7, /device:TPU:1, one launch (start us, length us, event | category | flops | bytes accessed | tf_op | source)
XLA Modules:
  0.0 108.3 jit_solution(2570133099424235476)
XLA Ops:
  0.0 3.2 %collective-permute-start.4 = (bf16[4096,256]{1,0:T(8,128)(2,1)}, bf16[4096,256]{1,0:T(8,128)(2,1)S(1)}, u32[]{:S(2)}, u32[]{:S(2)}) collective-permute-start(bf16[4096,256]{1,0:T(8,128)(2,1)} %refs_1_.1), channel_id=1, source_target_pairs={{0,2},{2,0},{4,6},{6,4},{8,10},{10,8},{12,14},{14,12},{16,18},{18,... | collective-permute-start | bytes 6291464 | tf_op jit(solution)/shard_map/ppermute | solution.py:38
  3.3 1.1 %copy-done.2 = bf16[1,160,2560]{2,1,0:T(8,128)(2,1)S(1)} copy-done((bf16[1,160,2560]{2,1,0:T(8,128)(2,1)S(1)}, bf16[1,160,2560]{2,1,0:T(8,128)(2,1)}, u32[]{:S(2)}) %copy-start.2) | copy-done | bytes 819224
  6.1 2.0 %collective-permute-start.3 = (bf16[80,2560]{1,0:T(8,128)(2,1)S(1)}, bf16[80,2560]{1,0:T(8,128)(2,1)S(1)}, u32[]{:S(2)}, u32[]{:S(2)}) collective-permute-start(bf16[80,2560]{1,0:T(8,128)(2,1)S(1)} %shard_map.56.refs_0_), channel_id=1, source_target_pairs={{0,192},{32,224},{64,0},{96,32},{128,64},{160,96},{192,128},{224,1... | collective-permute-start | bytes 1228808 | tf_op jit(solution)/shard_map/ppermute | solution.py:30
  9.1 1.3 %copy-done.1 = bf16[1,256,2560]{2,1,0:T(8,128)(2,1)S(1)} copy-done((bf16[1,256,2560]{2,1,0:T(8,128)(2,1)S(1)}, bf16[1,256,2560]{2,1,0:T(8,128)(2,1)}, u32[]{:S(2)}) %copy-start.1) | copy-done | bytes 1310744
  11.1 2.0 %shard_map.55 = (bf16[2560,512]{1,0:T(8,128)(2,1)S(1)}, s32[8,512]{1,0:T(8,128)S(1)}) custom-call(s32[4]{0:T(128)S(1)} %pad_add_fusion.place_ref, s32[8]{0:T(128)S(1)} %copy-done.3, s32[8,512]{1,0:T(8,128)S(1)} %reshape.16.rows_ref, bf16[256,2560]{1,0:T(8,128)(2,1)S(1)} %bitcast.23, bf16[256,2560]{1,0:T(8,128)(2,1)} %collective-permute-done.other_ref), custom_call_target="tpu_custom_call" | custom-call | bytes 5242880 | tf_op jit(solution)/shard_map/pallas_call | solution.py:90
  13.1 2.8 %collective-permute-done.1.refs_1_ = bf16[80,2560]{1,0:T(8,128)(2,1)S(1)} collective-permute-done((bf16[80,2560]{1,0:T(8,128)(2,1)S(1)}, bf16[80,2560]{1,0:T(8,128)(2,1)S(1)}, u32[]{:S(2)}, u32[]{:S(2)}) %collective-permute-start.1) | collective-permute-done | bytes 409632 | tf_op jit(solution)/shard_map/ppermute | solution.py:30
  16.0 1.3 %collective-permute-done.2.refs_2_ = bf16[80,2560]{1,0:T(8,128)(2,1)} collective-permute-done((bf16[80,2560]{1,0:T(8,128)(2,1)S(1)}, bf16[80,2560]{1,0:T(8,128)(2,1)}, u32[]{:S(2)}, u32[]{:S(2)}) %collective-permute-start.2) | collective-permute-done | bytes 409632 | tf_op jit(solution)/shard_map/ppermute | solution.py:30
  17.3 1.1 %collective-permute-start.5 = (bf16[40,2560]{1,0:T(8,128)(2,1)S(1)}, bf16[40,2560]{1,0:T(8,128)(2,1)S(1)}, u32[]{:S(2)}, u32[]{:S(2)}) collective-permute-start(bf16[40,2560]{1,0:T(8,128)(2,1)S(1)} %get-tuple-element.81), channel_id=1, source_target_pairs={{0,32},{32,0},{64,96},{96,64},{128,160},{160,128},{192,224},{224,1... | collective-permute-start | bytes 614408 | tf_op jit(solution)/shard_map/ppermute | solution.py:30
  18.6 2.7 %collective-permute-start.7 = (bf16[40,2560]{1,0:T(8,128)(2,1)S(1)}, bf16[40,2560]{1,0:T(8,128)(2,1)S(1)}, u32[]{:S(2)}, u32[]{:S(2)}) collective-permute-start(bf16[40,2560]{1,0:T(8,128)(2,1)S(1)} %get-tuple-element.81), channel_id=1, source_target_pairs={{0,192},{32,224},{64,0},{96,32},{128,64},{160,96},{192,128},{224,1... | collective-permute-start | bytes 614408 | tf_op jit(solution)/shard_map/ppermute | solution.py:30
  22.0 2.1 %shard_map.57 = (f32[4,40,512]{2,1,0:T(8,128)S(1)}, f32[4,40,512]{2,1,0:T(8,128)S(1)}) custom-call(s32[4]{0:T(128)S(1)} %pad_add_fusion.place_ref, bf16[80,2560]{1,0:T(8,128)(2,1)S(1)} %shard_map.56.refs_0_, bf16[80,2560]{1,0:T(8,128)(2,1)S(1)} %collective-permute-done.1.refs_1_, bf16[80,2560]{1,0:T(8,128)(2,1)} %collective-permute-done.2.refs_2_, ...), custom_call_target="tpu_custom_call" | custom-call | flops 838860800 | bytes 5570560 | tf_op jit(solution)/shard_map/pallas_call | solution.py:145
  24.1 1.5 %collective-permute-start.9 = (f32[4,40,512]{2,1,0:T(8,128)S(1)}, f32[4,40,512]{2,1,0:T(8,128)S(1)}, u32[]{:S(2)}, u32[]{:S(2)}) collective-permute-start(f32[4,40,512]{2,1,0:T(8,128)S(1)} %get-tuple-element.50), channel_id=1, source_target_pairs={{0,1},{1,0},{2,3},{3,2},{4,5},{5,4},{6,7},{7,6},{8,9},{9,8},{10,11... | collective-permute-start | bytes 983048 | tf_op jit(solution)/shard_map/ppermute | solution.py:42
  27.4 1.7 %collective-permute-done.8.refs_3_ = bf16[40,2560]{1,0:T(8,128)(2,1)S(1)} collective-permute-done((bf16[40,2560]{1,0:T(8,128)(2,1)S(1)}, bf16[40,2560]{1,0:T(8,128)(2,1)S(1)}, u32[]{:S(2)}, u32[]{:S(2)}) %collective-permute-start.8) | collective-permute-done | bytes 204832 | tf_op jit(solution)/shard_map/ppermute | solution.py:30
  29.6 1.4 %shard_map.59 = f32[176,512]{1,0:T(8,128)S(1)} custom-call(s32[4]{0:T(128)S(1)} %pad_add_fusion.place_ref, bf16[40,2560]{1,0:T(8,128)(2,1)S(1)} %collective-permute-done.5.refs_0_, bf16[40,2560]{1,0:T(8,128)(2,1)S(1)} %collective-permute-done.6.refs_1_, bf16[40,2560]{1,0:T(8,128)(2,1)S(1)} %collective-permute-done.7.refs_2_, ...), custom_call_target="tpu_custom_call" | custom-call | flops 503316480 | bytes 4096000 | tf_op jit(solution)/shard_map/pallas_call | solution.py:145
  31.0 4.0 %collective-permute-done.10.refs_0_ = bf16[40,2560]{1,0:T(8,128)(2,1)S(1)} collective-permute-done((bf16[40,2560]{1,0:T(8,128)(2,1)S(1)}, bf16[40,2560]{1,0:T(8,128)(2,1)S(1)}, u32[]{:S(2)}, u32[]{:S(2)}) %collective-permute-start.10) | collective-permute-done | bytes 204832 | tf_op jit(solution)/shard_map/ppermute | solution.py:30
  35.0 2.7 %collective-permute-start.14 = (f16[176,512]{1,0:T(8,128)(2,1)S(1)}, f16[176,512]{1,0:T(8,128)(2,1)S(1)}, u32[]{:S(2)}, u32[]{:S(2)}) collective-permute-start(f16[176,512]{1,0:T(8,128)(2,1)S(1)} %convert_element_type.16), channel_id=1, source_target_pairs={{0,1},{1,0},{2,3},{3,2},{4,5},{5,4},{6,7},{7,6},{8,9},{9,8},{10,11... | collective-permute-start | bytes 540680 | tf_op jit(solution)/shard_map/ppermute | solution.py:42
  37.8 1.2 %shard_map.58 = f32[4,40,512]{2,1,0:T(8,128)S(1)} custom-call(s32[4]{0:T(128)S(1)} %pad_add_fusion.place_ref, bf16[40,2560]{1,0:T(8,128)(2,1)S(1)} %collective-permute-done.10.refs_0_, bf16[40,2560]{1,0:T(8,128)(2,1)S(1)} %collective-permute-done.11.refs_1_, bf16[40,2560]{1,0:T(8,128)(2,1)S(1)} %collective-permute-done.12.refs_2_, ...), custom_call_target="tpu_custom_call" | custom-call | flops 503316480 | bytes 4096000 | tf_op jit(solution)/shard_map/pallas_call | solution.py:145
  39.1 2.6 %collective-permute-done.14 = f16[176,512]{1,0:T(8,128)(2,1)S(1)} collective-permute-done((f16[176,512]{1,0:T(8,128)(2,1)S(1)}, f16[176,512]{1,0:T(8,128)(2,1)S(1)}, u32[]{:S(2)}, u32[]{:S(2)}) %collective-permute-start.14) | collective-permute-done | bytes 180256 | tf_op jit(solution)/shard_map/ppermute | solution.py:42
  43.0 4.0 %collective-permute-start.18 = (bf16[120,512]{1,0:T(8,128)(2,1)S(1)}, bf16[120,512]{1,0:T(8,128)(2,1)S(1)}, u32[]{:S(2)}, u32[]{:S(2)}) collective-permute-start(bf16[120,512]{1,0:T(8,128)(2,1)S(1)} %pad_maximum_fusion.2.refs_0_), channel_id=1, source_target_pairs={{0,28},{2,30},{4,0},{6,2},{8,4},{10,6},{12,8},{14,10},{16,12},{18,... | collective-permute-start | bytes 368648 | tf_op jit(solution)/shard_map/ppermute | solution.py:34
  47.0 1.2 %collective-permute-start.19 = (bf16[3,40,512]{2,1,0:T(8,128)(2,1)S(1)}, bf16[3,40,512]{2,1,0:T(8,128)(2,1)S(1)}, u32[]{:S(2)}, u32[]{:S(2)}) collective-permute-start(bf16[3,40,512]{2,1,0:T(8,128)(2,1)S(1)} %pad_maximum_fusion.1), channel_id=1, source_target_pairs={{0,32},{32,0},{64,96},{96,64},{128,160},{160,128},{192,224},{224,1... | collective-permute-start | bytes 368648 | tf_op jit(solution)/shard_map/ppermute | solution.py:30
  48.3 2.7 %collective-permute-start.16 = (bf16[120,512]{1,0:T(8,128)(2,1)S(1)}, bf16[120,512]{1,0:T(8,128)(2,1)S(1)}, u32[]{:S(2)}, u32[]{:S(2)}) collective-permute-start(bf16[120,512]{1,0:T(8,128)(2,1)S(1)} %pad_maximum_fusion.refs_0_), channel_id=1, source_target_pairs={{0,28},{2,30},{4,0},{6,2},{8,4},{10,6},{12,8},{14,10},{16,12},{18,... | collective-permute-start | bytes 368648 | tf_op jit(solution)/shard_map/ppermute | solution.py:34
  51.0 2.2 %collective-permute-done.15.refs_1_ = bf16[120,512]{1,0:T(8,128)(2,1)S(1)} collective-permute-done((bf16[120,512]{1,0:T(8,128)(2,1)S(1)}, bf16[120,512]{1,0:T(8,128)(2,1)S(1)}, u32[]{:S(2)}, u32[]{:S(2)}) %collective-permute-start.15) | collective-permute-done | bytes 122912 | tf_op jit(solution)/shard_map/ppermute | solution.py:34
  53.2 2.7 %collective-permute-start.21 = (bf16[120,512]{1,0:T(8,128)(2,1)S(1)}, bf16[120,512]{1,0:T(8,128)(2,1)S(1)}, u32[]{:S(2)}, u32[]{:S(2)}) collective-permute-start(bf16[120,512]{1,0:T(8,128)(2,1)S(1)} %collective-permute-done.16.refs_2_), channel_id=1, source_target_pairs={{0,28},{2,30},{4,0},{6,2},{8,4},{10,6},{12,8},{14,10},{16,12},{18,... | collective-permute-start | bytes 368648 | tf_op jit(solution)/shard_map/ppermute | solution.py:34
  56.4 2.7 %collective-permute-start.26 = (bf16[120,512]{1,0:T(8,128)(2,1)S(1)}, bf16[120,512]{1,0:T(8,128)(2,1)S(1)}, u32[]{:S(2)}, u32[]{:S(2)}) collective-permute-start(bf16[120,512]{1,0:T(8,128)(2,1)S(1)} %collective-permute-done.18.refs_2_), channel_id=1, source_target_pairs={{0,28},{2,30},{4,0},{6,2},{8,4},{10,6},{12,8},{14,10},{16,12},{18,... | collective-permute-start | bytes 368648 | tf_op jit(solution)/shard_map/ppermute | solution.py:34
  59.1 1.1 %collective-permute-start.22 = (bf16[120,512]{1,0:T(8,128)(2,1)S(1)}, bf16[120,512]{1,0:T(8,128)(2,1)S(1)}, u32[]{:S(2)}, u32[]{:S(2)}) collective-permute-start(bf16[120,512]{1,0:T(8,128)(2,1)S(1)} %collective-permute-done.20.refs_3_), channel_id=1, source_target_pairs={{0,4},{2,6},{4,8},{6,10},{8,12},{10,14},{12,16},{14,18},{16,20},{1... | collective-permute-start | bytes 368648 | tf_op jit(solution)/shard_map/ppermute | solution.py:34
  61.4 2.7 %collective-permute-start.28 = (bf16[120,512]{1,0:T(8,128)(2,1)S(1)}, bf16[120,512]{1,0:T(8,128)(2,1)S(1)}, u32[]{:S(2)}, u32[]{:S(2)}) collective-permute-start(bf16[120,512]{1,0:T(8,128)(2,1)S(1)} %collective-permute-done.26.refs_4_), channel_id=1, source_target_pairs={{0,28},{2,30},{4,0},{6,2},{8,4},{10,6},{12,8},{14,10},{16,12},{18,... | collective-permute-start | bytes 368648 | tf_op jit(solution)/shard_map/ppermute | solution.py:34
  64.0 2.7 %collective-permute-start.23 = (bf16[120,512]{1,0:T(8,128)(2,1)S(1)}, bf16[120,512]{1,0:T(8,128)(2,1)S(1)}, u32[]{:S(2)}, u32[]{:S(2)}) collective-permute-start(bf16[120,512]{1,0:T(8,128)(2,1)S(1)} %collective-permute-done.21.refs_4_), channel_id=1, source_target_pairs={{0,28},{2,30},{4,0},{6,2},{8,4},{10,6},{12,8},{14,10},{16,12},{18,... | collective-permute-start | bytes 368648 | tf_op jit(solution)/shard_map/ppermute | solution.py:34
  66.7 3.4 %collective-permute-start.29 = (bf16[120,512]{1,0:T(8,128)(2,1)S(1)}, bf16[120,512]{1,0:T(8,128)(2,1)S(1)}, u32[]{:S(2)}, u32[]{:S(2)}) collective-permute-start(bf16[120,512]{1,0:T(8,128)(2,1)S(1)} %collective-permute-done.28.refs_6_), channel_id=1, source_target_pairs={{0,28},{2,30},{4,0},{6,2},{8,4},{10,6},{12,8},{14,10},{16,12},{18,... | collective-permute-start | bytes 368648 | tf_op jit(solution)/shard_map/ppermute | solution.py:34
  70.1 2.1 %collective-permute-start.31 = (bf16[2,40,512]{2,1,0:T(8,128)(2,1)S(1)}, bf16[2,40,512]{2,1,0:T(8,128)(2,1)S(1)}, u32[]{:S(2)}, u32[]{:S(2)}) collective-permute-start(bf16[2,40,512]{2,1,0:T(8,128)(2,1)S(1)} %pad_maximum_fusion.4), channel_id=1, source_target_pairs={{0,128},{32,160},{64,192},{96,224},{128,0},{160,32},{192,64},{224,... | collective-permute-start | bytes 245768 | tf_op jit(solution)/shard_map/ppermute | solution.py:30
  72.3 1.2 %shard_map.61.refs_3_ = f32[120,512]{1,0:T(8,128)S(1)} custom-call(s32[4]{0:T(128)S(1)} %pad_add_fusion.place_ref, bf16[120,512]{1,0:T(8,128)(2,1)S(1)} %pad_maximum_fusion.2.refs_0_, bf16[120,512]{1,0:T(8,128)(2,1)S(1)} %collective-permute-done.17.refs_1_, bf16[120,512]{1,0:T(8,128)(2,1)S(1)} %collective-permute-done.18.refs_2_, ...), custom_call_target="tpu_custom_call" | custom-call | flops 440401920 | bytes 4530176 | tf_op jit(solution)/shard_map/pallas_call | solution.py:193
  73.5 1.4 %shard_map.60 = (f32[1,8]{1,0:T(1,128)S(1)}, f32[1,8]{1,0:T(1,128)S(1)}, f32[1,8]{1,0:T(1,128)S(1)}) custom-call(s32[4]{0:T(128)S(1)} %pad_add_fusion.place_ref, bf16[120,512]{1,0:T(8,128)(2,1)S(1)} %pad_maximum_fusion.refs_0_, bf16[120,512]{1,0:T(8,128)(2,1)S(1)} %collective-permute-done.15.refs_1_, bf16[120,512]{1,0:T(8,128)(2,1)S(1)} %collective-permute-done.16.refs_2_, ...), custom_call_target="tpu_custom_call" | custom-call | flops 503316480 | bytes 5545984 | tf_op jit(solution)/shard_map/pallas_call | solution.py:246
  77.6 1.7 %collective-permute-done.33 = f32[1,8]{1,0:T(1,128)S(1)} collective-permute-done((f32[1,8]{1,0:T(1,128)S(1)}, f32[1,8]{1,0:T(1,128)S(1)}, u32[]{:S(2)}, u32[]{:S(2)}) %collective-permute-start.33) | collective-permute-done | bytes 64 | tf_op jit(solution)/shard_map/ppermute | solution.py:30
  79.3 28.4 %all_to_all.6 = f32[32,1,8]{2,1,0:T(1,128)S(1)} all-to-all(f32[32,1,8]{2,1,0:T(1,128)S(1)} %broadcast_in_dim.25), channel_id=1, replica_groups=mesh['occ'=8,'cabs'=16,'aux'=2] {'cabs','aux'}, dimensions={0} | all-to-all | bytes 2048 | tf_op jit(solution)/shard_map/all_to_all | solution.py:347
  (73 shorter events, 12.9 us)
Async XLA Ops:
  0.0 17.3 %collective-permute-start.4 = (bf16[4096,256]{1,0:T(8,128)(2,1)}, bf16[4096,256]{1,0:T(8,128)(2,1)S(1)}, u32[]{:S(2)}, u32[]{:S(2)}) collective-permute-start(bf16[4096,256]{1,0:T(8,128)(2,1)} %refs_1_.1), channel_id=1, source_target_pairs={{0,2},{2,0},{4,6},{6,4},{8,10},{10,8},{12,14},{14,12},{16,18},{18,... | collective-permute-start | bytes 6291464 | tf_op jit(solution)/shard_map/ppermute | solution.py:38
  3.2 5.9 %collective-permute-start = (bf16[256,2560]{1,0:T(8,128)(2,1)}, bf16[256,2560]{1,0:T(8,128)(2,1)}, u32[]{:S(2)}, u32[]{:S(2)}) collective-permute-start(bf16[256,2560]{1,0:T(8,128)(2,1)} %bitcast.22), channel_id=1, source_target_pairs={{0,2},{2,0},{4,6},{6,4},{8,10},{10,8},{12,14},{14,12},{16,18},{18,... | collective-permute-start | bytes 3932168 | tf_op jit(solution)/shard_map/ppermute | solution.py:38
  5.2 10.7 %collective-permute-start.1 = (bf16[80,2560]{1,0:T(8,128)(2,1)S(1)}, bf16[80,2560]{1,0:T(8,128)(2,1)S(1)}, u32[]{:S(2)}, u32[]{:S(2)}) collective-permute-start(bf16[80,2560]{1,0:T(8,128)(2,1)S(1)} %shard_map.56.refs_0_), channel_id=1, source_target_pairs={{0,32},{32,0},{64,96},{96,64},{128,160},{160,128},{192,224},{224,1... | collective-permute-start | bytes 1228808 | tf_op jit(solution)/shard_map/ppermute | solution.py:30
  5.3 11.9 %collective-permute-start.2 = (bf16[80,2560]{1,0:T(8,128)(2,1)S(1)}, bf16[80,2560]{1,0:T(8,128)(2,1)}, u32[]{:S(2)}, u32[]{:S(2)}) collective-permute-start(bf16[80,2560]{1,0:T(8,128)(2,1)S(1)} %shard_map.56.refs_0_), channel_id=1, source_target_pairs={{0,64},{32,96},{64,128},{96,160},{128,192},{160,224},{192,0},{224,... | collective-permute-start | bytes 1228808 | tf_op jit(solution)/shard_map/ppermute | solution.py:30
  6.1 11.2 %collective-permute-start.3 = (bf16[80,2560]{1,0:T(8,128)(2,1)S(1)}, bf16[80,2560]{1,0:T(8,128)(2,1)S(1)}, u32[]{:S(2)}, u32[]{:S(2)}) collective-permute-start(bf16[80,2560]{1,0:T(8,128)(2,1)S(1)} %shard_map.56.refs_0_), channel_id=1, source_target_pairs={{0,192},{32,224},{64,0},{96,32},{128,64},{160,96},{192,128},{224,1... | collective-permute-start | bytes 1228808 | tf_op jit(solution)/shard_map/ppermute | solution.py:30
  17.3 8.3 %collective-permute-start.5 = (bf16[40,2560]{1,0:T(8,128)(2,1)S(1)}, bf16[40,2560]{1,0:T(8,128)(2,1)S(1)}, u32[]{:S(2)}, u32[]{:S(2)}) collective-permute-start(bf16[40,2560]{1,0:T(8,128)(2,1)S(1)} %get-tuple-element.81), channel_id=1, source_target_pairs={{0,32},{32,0},{64,96},{96,64},{128,160},{160,128},{192,224},{224,1... | collective-permute-start | bytes 614408 | tf_op jit(solution)/shard_map/ppermute | solution.py:30
  18.5 7.4 %collective-permute-start.6 = (bf16[40,2560]{1,0:T(8,128)(2,1)S(1)}, bf16[40,2560]{1,0:T(8,128)(2,1)S(1)}, u32[]{:S(2)}, u32[]{:S(2)}) collective-permute-start(bf16[40,2560]{1,0:T(8,128)(2,1)S(1)} %get-tuple-element.79), channel_id=1, source_target_pairs={{0,64},{32,96},{64,128},{96,160},{128,192},{160,224},{192,0},{224,... | collective-permute-start | bytes 614408 | tf_op jit(solution)/shard_map/ppermute | solution.py:30
  18.6 8.4 %collective-permute-start.7 = (bf16[40,2560]{1,0:T(8,128)(2,1)S(1)}, bf16[40,2560]{1,0:T(8,128)(2,1)S(1)}, u32[]{:S(2)}, u32[]{:S(2)}) collective-permute-start(bf16[40,2560]{1,0:T(8,128)(2,1)S(1)} %get-tuple-element.81), channel_id=1, source_target_pairs={{0,192},{32,224},{64,0},{96,32},{128,64},{160,96},{192,128},{224,1... | collective-permute-start | bytes 614408 | tf_op jit(solution)/shard_map/ppermute | solution.py:30
  21.2 7.9 %collective-permute-start.8 = (bf16[40,2560]{1,0:T(8,128)(2,1)S(1)}, bf16[40,2560]{1,0:T(8,128)(2,1)S(1)}, u32[]{:S(2)}, u32[]{:S(2)}) collective-permute-start(bf16[40,2560]{1,0:T(8,128)(2,1)S(1)} %get-tuple-element.79), channel_id=1, source_target_pairs={{0,128},{32,160},{64,192},{96,224},{128,0},{160,32},{192,64},{224,... | collective-permute-start | bytes 614408 | tf_op jit(solution)/shard_map/ppermute | solution.py:30
  24.1 13.7 %collective-permute-start.9 = (f32[4,40,512]{2,1,0:T(8,128)S(1)}, f32[4,40,512]{2,1,0:T(8,128)S(1)}, u32[]{:S(2)}, u32[]{:S(2)}) collective-permute-start(f32[4,40,512]{2,1,0:T(8,128)S(1)} %get-tuple-element.50), channel_id=1, source_target_pairs={{0,1},{1,0},{2,3},{3,2},{4,5},{5,4},{6,7},{7,6},{8,9},{9,8},{10,11... | collective-permute-start | bytes 983048 | tf_op jit(solution)/shard_map/ppermute | solution.py:42
  25.6 9.4 %collective-permute-start.10 = (bf16[40,2560]{1,0:T(8,128)(2,1)S(1)}, bf16[40,2560]{1,0:T(8,128)(2,1)S(1)}, u32[]{:S(2)}, u32[]{:S(2)}) collective-permute-start(bf16[40,2560]{1,0:T(8,128)(2,1)S(1)} %get-tuple-element.82), channel_id=1, source_target_pairs={{0,32},{32,0},{64,96},{96,64},{128,160},{160,128},{192,224},{224,1... | collective-permute-start | bytes 614408 | tf_op jit(solution)/shard_map/ppermute | solution.py:30
  25.9 11.9 %collective-permute-start.12 = (bf16[40,2560]{1,0:T(8,128)(2,1)S(1)}, bf16[40,2560]{1,0:T(8,128)(2,1)S(1)}, u32[]{:S(2)}, u32[]{:S(2)}) collective-permute-start(bf16[40,2560]{1,0:T(8,128)(2,1)S(1)} %get-tuple-element.82), channel_id=1, source_target_pairs={{0,192},{32,224},{64,0},{96,32},{128,64},{160,96},{192,128},{224,1... | collective-permute-start | bytes 614408 | tf_op jit(solution)/shard_map/ppermute | solution.py:30
  27.0 10.8 %collective-permute-start.11 = (bf16[40,2560]{1,0:T(8,128)(2,1)S(1)}, bf16[40,2560]{1,0:T(8,128)(2,1)S(1)}, u32[]{:S(2)}, u32[]{:S(2)}) collective-permute-start(bf16[40,2560]{1,0:T(8,128)(2,1)S(1)} %get-tuple-element.80), channel_id=1, source_target_pairs={{0,64},{32,96},{64,128},{96,160},{128,192},{160,224},{192,0},{224,... | collective-permute-start | bytes 614408 | tf_op jit(solution)/shard_map/ppermute | solution.py:30
  29.1 8.7 %collective-permute-start.13 = (bf16[40,2560]{1,0:T(8,128)(2,1)S(1)}, bf16[40,2560]{1,0:T(8,128)(2,1)S(1)}, u32[]{:S(2)}, u32[]{:S(2)}) collective-permute-start(bf16[40,2560]{1,0:T(8,128)(2,1)S(1)} %get-tuple-element.80), channel_id=1, source_target_pairs={{0,128},{32,160},{64,192},{96,224},{128,0},{160,32},{192,64},{224,... | collective-permute-start | bytes 614408 | tf_op jit(solution)/shard_map/ppermute | solution.py:30
  35.0 6.7 %collective-permute-start.14 = (f16[176,512]{1,0:T(8,128)(2,1)S(1)}, f16[176,512]{1,0:T(8,128)(2,1)S(1)}, u32[]{:S(2)}, u32[]{:S(2)}) collective-permute-start(f16[176,512]{1,0:T(8,128)(2,1)S(1)} %convert_element_type.16), channel_id=1, source_target_pairs={{0,1},{1,0},{2,3},{3,2},{4,5},{5,4},{6,7},{7,6},{8,9},{9,8},{10,11... | collective-permute-start | bytes 540680 | tf_op jit(solution)/shard_map/ppermute | solution.py:42
  41.9 9.0 %collective-permute-start.17 = (bf16[120,512]{1,0:T(8,128)(2,1)S(1)}, bf16[120,512]{1,0:T(8,128)(2,1)S(1)}, u32[]{:S(2)}, u32[]{:S(2)}) collective-permute-start(bf16[120,512]{1,0:T(8,128)(2,1)S(1)} %pad_maximum_fusion.2.refs_0_), channel_id=1, source_target_pairs={{0,4},{2,6},{4,8},{6,10},{8,12},{10,14},{12,16},{14,18},{16,20},{1... | collective-permute-start | bytes 368648 | tf_op jit(solution)/shard_map/ppermute | solution.py:34
  43.0 8.0 %collective-permute-start.18 = (bf16[120,512]{1,0:T(8,128)(2,1)S(1)}, bf16[120,512]{1,0:T(8,128)(2,1)S(1)}, u32[]{:S(2)}, u32[]{:S(2)}) collective-permute-start(bf16[120,512]{1,0:T(8,128)(2,1)S(1)} %pad_maximum_fusion.2.refs_0_), channel_id=1, source_target_pairs={{0,28},{2,30},{4,0},{6,2},{8,4},{10,6},{12,8},{14,10},{16,12},{18,... | collective-permute-start | bytes 368648 | tf_op jit(solution)/shard_map/ppermute | solution.py:34
  47.0 3.9 %collective-permute-start.19 = (bf16[3,40,512]{2,1,0:T(8,128)(2,1)S(1)}, bf16[3,40,512]{2,1,0:T(8,128)(2,1)S(1)}, u32[]{:S(2)}, u32[]{:S(2)}) collective-permute-start(bf16[3,40,512]{2,1,0:T(8,128)(2,1)S(1)} %pad_maximum_fusion.1), channel_id=1, source_target_pairs={{0,32},{32,0},{64,96},{96,64},{128,160},{160,128},{192,224},{224,1... | collective-permute-start | bytes 368648 | tf_op jit(solution)/shard_map/ppermute | solution.py:30
  48.3 4.9 %collective-permute-start.15 = (bf16[120,512]{1,0:T(8,128)(2,1)S(1)}, bf16[120,512]{1,0:T(8,128)(2,1)S(1)}, u32[]{:S(2)}, u32[]{:S(2)}) collective-permute-start(bf16[120,512]{1,0:T(8,128)(2,1)S(1)} %pad_maximum_fusion.refs_0_), channel_id=1, source_target_pairs={{0,4},{2,6},{4,8},{6,10},{8,12},{10,14},{12,16},{14,18},{16,20},{1... | collective-permute-start | bytes 368648 | tf_op jit(solution)/shard_map/ppermute | solution.py:34
  48.3 4.9 %collective-permute-start.16 = (bf16[120,512]{1,0:T(8,128)(2,1)S(1)}, bf16[120,512]{1,0:T(8,128)(2,1)S(1)}, u32[]{:S(2)}, u32[]{:S(2)}) collective-permute-start(bf16[120,512]{1,0:T(8,128)(2,1)S(1)} %pad_maximum_fusion.refs_0_), channel_id=1, source_target_pairs={{0,28},{2,30},{4,0},{6,2},{8,4},{10,6},{12,8},{14,10},{16,12},{18,... | collective-permute-start | bytes 368648 | tf_op jit(solution)/shard_map/ppermute | solution.py:34
  53.2 5.9 %collective-permute-start.20 = (bf16[120,512]{1,0:T(8,128)(2,1)S(1)}, bf16[120,512]{1,0:T(8,128)(2,1)S(1)}, u32[]{:S(2)}, u32[]{:S(2)}) collective-permute-start(bf16[120,512]{1,0:T(8,128)(2,1)S(1)} %collective-permute-done.15.refs_1_), channel_id=1, source_target_pairs={{0,4},{2,6},{4,8},{6,10},{8,12},{10,14},{12,16},{14,18},{16,20},{1... | collective-permute-start | bytes 368648 | tf_op jit(solution)/shard_map/ppermute | solution.py:34
  53.2 5.9 %collective-permute-start.21 = (bf16[120,512]{1,0:T(8,128)(2,1)S(1)}, bf16[120,512]{1,0:T(8,128)(2,1)S(1)}, u32[]{:S(2)}, u32[]{:S(2)}) collective-permute-start(bf16[120,512]{1,0:T(8,128)(2,1)S(1)} %collective-permute-done.16.refs_2_), channel_id=1, source_target_pairs={{0,28},{2,30},{4,0},{6,2},{8,4},{10,6},{12,8},{14,10},{16,12},{18,... | collective-permute-start | bytes 368648 | tf_op jit(solution)/shard_map/ppermute | solution.py:34
  55.9 4.5 %collective-permute-start.27 = (bf16[2,40,512]{2,1,0:T(8,128)(2,1)S(1)}, bf16[2,40,512]{2,1,0:T(8,128)(2,1)S(1)}, u32[]{:S(2)}, u32[]{:S(2)}) collective-permute-start(bf16[2,40,512]{2,1,0:T(8,128)(2,1)S(1)} %pad_maximum_fusion.3), channel_id=1, source_target_pairs={{0,64},{32,96},{64,128},{96,160},{128,192},{160,224},{192,0},{224,... | collective-permute-start | bytes 245768 | tf_op jit(solution)/shard_map/ppermute | solution.py:30
  56.4 4.9 %collective-permute-start.25 = (bf16[120,512]{1,0:T(8,128)(2,1)S(1)}, bf16[120,512]{1,0:T(8,128)(2,1)S(1)}, u32[]{:S(2)}, u32[]{:S(2)}) collective-permute-start(bf16[120,512]{1,0:T(8,128)(2,1)S(1)} %collective-permute-done.17.refs_1_), channel_id=1, source_target_pairs={{0,4},{2,6},{4,8},{6,10},{8,12},{10,14},{12,16},{14,18},{16,20},{1... | collective-permute-start | bytes 368648 | tf_op jit(solution)/shard_map/ppermute | solution.py:34
  56.4 4.9 %collective-permute-start.26 = (bf16[120,512]{1,0:T(8,128)(2,1)S(1)}, bf16[120,512]{1,0:T(8,128)(2,1)S(1)}, u32[]{:S(2)}, u32[]{:S(2)}) collective-permute-start(bf16[120,512]{1,0:T(8,128)(2,1)S(1)} %collective-permute-done.18.refs_2_), channel_id=1, source_target_pairs={{0,28},{2,30},{4,0},{6,2},{8,4},{10,6},{12,8},{14,10},{16,12},{18,... | collective-permute-start | bytes 368648 | tf_op jit(solution)/shard_map/ppermute | solution.py:34
  59.1 7.6 %collective-permute-start.22 = (bf16[120,512]{1,0:T(8,128)(2,1)S(1)}, bf16[120,512]{1,0:T(8,128)(2,1)S(1)}, u32[]{:S(2)}, u32[]{:S(2)}) collective-permute-start(bf16[120,512]{1,0:T(8,128)(2,1)S(1)} %collective-permute-done.20.refs_3_), channel_id=1, source_target_pairs={{0,4},{2,6},{4,8},{6,10},{8,12},{10,14},{12,16},{14,18},{16,20},{1... | collective-permute-start | bytes 368648 | tf_op jit(solution)/shard_map/ppermute | solution.py:34
  61.4 5.4 %collective-permute-start.28 = (bf16[120,512]{1,0:T(8,128)(2,1)S(1)}, bf16[120,512]{1,0:T(8,128)(2,1)S(1)}, u32[]{:S(2)}, u32[]{:S(2)}) collective-permute-start(bf16[120,512]{1,0:T(8,128)(2,1)S(1)} %collective-permute-done.26.refs_4_), channel_id=1, source_target_pairs={{0,28},{2,30},{4,0},{6,2},{8,4},{10,6},{12,8},{14,10},{16,12},{18,... | collective-permute-start | bytes 368648 | tf_op jit(solution)/shard_map/ppermute | solution.py:34
  64.0 8.3 %collective-permute-start.30 = (bf16[120,512]{1,0:T(8,128)(2,1)S(1)}, bf16[120,512]{1,0:T(8,128)(2,1)S(1)}, u32[]{:S(2)}, u32[]{:S(2)}) collective-permute-start(bf16[120,512]{1,0:T(8,128)(2,1)S(1)} %collective-permute-done.25.refs_3_), channel_id=1, source_target_pairs={{0,4},{2,6},{4,8},{6,10},{8,12},{10,14},{12,16},{14,18},{16,20},{1... | collective-permute-start | bytes 368648 | tf_op jit(solution)/shard_map/ppermute | solution.py:34
  64.0 9.5 %collective-permute-start.23 = (bf16[120,512]{1,0:T(8,128)(2,1)S(1)}, bf16[120,512]{1,0:T(8,128)(2,1)S(1)}, u32[]{:S(2)}, u32[]{:S(2)}) collective-permute-start(bf16[120,512]{1,0:T(8,128)(2,1)S(1)} %collective-permute-done.21.refs_4_), channel_id=1, source_target_pairs={{0,28},{2,30},{4,0},{6,2},{8,4},{10,6},{12,8},{14,10},{16,12},{18,... | collective-permute-start | bytes 368648 | tf_op jit(solution)/shard_map/ppermute | solution.py:34
  66.7 6.8 %collective-permute-start.24 = (bf16[120,512]{1,0:T(8,128)(2,1)S(1)}, bf16[120,512]{1,0:T(8,128)(2,1)S(1)}, u32[]{:S(2)}, u32[]{:S(2)}) collective-permute-start(bf16[120,512]{1,0:T(8,128)(2,1)S(1)} %collective-permute-done.22.refs_5_), channel_id=1, source_target_pairs={{0,4},{2,6},{4,8},{6,10},{8,12},{10,14},{12,16},{14,18},{16,20},{1... | collective-permute-start | bytes 368648 | tf_op jit(solution)/shard_map/ppermute | solution.py:34
  66.7 9.9 %collective-permute-start.29 = (bf16[120,512]{1,0:T(8,128)(2,1)S(1)}, bf16[120,512]{1,0:T(8,128)(2,1)S(1)}, u32[]{:S(2)}, u32[]{:S(2)}) collective-permute-start(bf16[120,512]{1,0:T(8,128)(2,1)S(1)} %collective-permute-done.28.refs_6_), channel_id=1, source_target_pairs={{0,28},{2,30},{4,0},{6,2},{8,4},{10,6},{12,8},{14,10},{16,12},{18,... | collective-permute-start | bytes 368648 | tf_op jit(solution)/shard_map/ppermute | solution.py:34
  70.1 6.5 %collective-permute-start.31 = (bf16[2,40,512]{2,1,0:T(8,128)(2,1)S(1)}, bf16[2,40,512]{2,1,0:T(8,128)(2,1)S(1)}, u32[]{:S(2)}, u32[]{:S(2)}) collective-permute-start(bf16[2,40,512]{2,1,0:T(8,128)(2,1)S(1)} %pad_maximum_fusion.4), channel_id=1, source_target_pairs={{0,128},{32,160},{64,192},{96,224},{128,0},{160,32},{192,64},{224,... | collective-permute-start | bytes 245768 | tf_op jit(solution)/shard_map/ppermute | solution.py:30
  (6 other events, 42.7 us)
